TPU v7x, 32 devices: a whole 2x2x4 slice. The times are simulated.
32 devices in a mesh: dp: 8 (over z, x), fsdp: 4 (over y, core).
Axes of the slice: x: 2, y: 2, z: 4, core: 2. Of those that a mesh axis runs over, the one named last changes fastest.
Arguments:
- tokens: float32 [16384, 768], P(('dp', 'fsdp')), may hold values from -6 to 6
- doc_ids: int32 [16384], P(('dp', 'fsdp')), may hold values from -1 to 68, as said below
- teacher: float32 [16384, 768], P(('dp', 'fsdp')), may hold values from -6 to 6
- seg_qkv: float32 [768, 2304], P(('dp', 'fsdp')), may hold values from -0.21875 to 0.21875
- seg_out: float32 [768, 768], P(('dp', 'fsdp')), may hold values from -1.75 to 1.75
- seg_in: float32 [768, 3072], P(('dp', 'fsdp')), may hold values from -0.21875 to 0.21875
- seg_fc2: float32 [3072, 768], P(('dp', 'fsdp')), may hold values from -0.109375 to 0.109375
- seg_gains: float32 [2, 768], P(None, ('dp', 'fsdp')), may hold values from 0.1 to 1.9
- seg_biases: float32 [6, 768], P(None, ('dp', 'fsdp')), may hold values from -0.3 to 0.3
- seg_in_bias: float32 [3072], P(('dp', 'fsdp')), may hold values from -0.3 to 0.3
- cls_qkv: float32 [768, 2304], P(('dp', 'fsdp')), may hold values from -0.21875 to 0.21875
- cls_out: float32 [768, 768], P(('dp', 'fsdp')), may hold values from -0.4375 to 0.4375
- cls_in: float32 [768, 3072], P(('dp', 'fsdp')), may hold values from -0.21875 to 0.21875
- cls_fc2: float32 [3072, 768], P(('dp', 'fsdp')), may hold values from -0.109375 to 0.109375
- cls_gains: float32 [2, 768], P(None, ('dp', 'fsdp')), may hold values from 0.1 to 1.9
- cls_biases: float32 [6, 768], P(None, ('dp', 'fsdp')), may hold values from -0.3 to 0.3
- cls_in_bias: float32 [3072], P(('dp', 'fsdp')), may hold values from -0.3 to 0.3
- seg_pos: float32 [16, 768], P(None, ('dp', 'fsdp')), may hold values from -3 to 3
Outputs:
- output: float32 [16384, 768], P(('dp', 'fsdp'))
- loss: float32 [], replicated
- grad_tokens: float32 [16384, 768], P(('dp', 'fsdp'))
- grad_seg_qkv: float32 [768, 2304], P(('dp', 'fsdp'))
- grad_seg_out: float32 [768, 768], P(('dp', 'fsdp'))
- grad_seg_in: float32 [768, 3072], P(('dp', 'fsdp'))
- grad_seg_fc2: float32 [3072, 768], P(('dp', 'fsdp'))
- grad_seg_gains: float32 [2, 768], P(None, ('dp', 'fsdp'))
- grad_seg_biases: float32 [6, 768], P(None, ('dp', 'fsdp'))
- grad_seg_in_bias: float32 [3072], P(('dp', 'fsdp'))
- grad_cls_qkv: float32 [768, 2304], P(('dp', 'fsdp'))
- grad_cls_out: float32 [768, 768], P(('dp', 'fsdp'))
- grad_cls_in: float32 [768, 3072], P(('dp', 'fsdp'))
- grad_cls_fc2: float32 [3072, 768], P(('dp', 'fsdp'))
- grad_cls_gains: float32 [2, 768], P(None, ('dp', 'fsdp'))
- grad_cls_biases: float32 [6, 768], P(None, ('dp', 'fsdp'))
- grad_cls_in_bias: float32 [3072], P(('dp', 'fsdp'))
- grad_seg_pos: float32 [16, 768], P(None, ('dp', 'fsdp'))
Inputs may be any that keep to these rules, and one draw needn't show every extreme that they name: `doc_ids`: within each sequence of 2048 tokens the document numbers start at 0 on its first token and rise by one at each new document; every sequence ends with pads, -1.
All inputs are finite; a program needn't handle non-finite values.
Results may differ from a plain program's by a relative error of at most 0.02.
The roundings to bfloat16 on the way count: a program that leaves them out, or rounds other values in their place, can miss the bound.
Values may be sent and summed in bfloat16 or wider, within the bound.
No kernel may reach another device: no remote copies, remote signals or barrier semaphores. Data moves between devices by JAX's collectives and lax.ppermute only.
A program may use at most 256 MiB of HBM per device.

v0:
```python
import jax
import jax.numpy as jnp
from jax import lax
from jax.sharding import PartitionSpec as P

NHEADS = 12
HEAD = 64
SEG = 128


def layer_norm(row_data, gain_row, shift_row):
    centered = row_data - jnp.mean(row_data, axis=-1, keepdims=True)
    normed = centered * lax.rsqrt(jnp.mean(centered * centered, axis=-1, keepdims=True) + 1e-05)
    return normed * gain_row + shift_row


def exact_gelu(hidden_pre):
    return jax.nn.gelu(hidden_pre, approximate=False)


def to_heads(flat, groups):
    return flat.reshape(groups, flat.shape[0] // groups, NHEADS, HEAD)


def project_forward(row_data, weights):
    features = weights[1].shape[0]
    bias_rows = weights[5].astype(jnp.float32)
    rows_low = row_data.astype(jnp.bfloat16)
    joined = jnp.dot(rows_low, weights[0], preferred_element_type=jnp.float32)
    queries = (joined[:, :features] + bias_rows[0]).astype(jnp.bfloat16)
    key_rows = joined[:, features : 2 * features].astype(jnp.bfloat16)
    value_rows = (joined[:, 2 * features :] + bias_rows[1]).astype(jnp.bfloat16)
    return (rows_low, queries, key_rows, value_rows)


def masked_scores(queries, key_rows, allowed):
    scaling = queries.shape[-1] ** (-0.5)
    scores = (
        jnp.einsum("wqhd,wkhd->whqk", queries, key_rows, preferred_element_type=jnp.float32)
        * scaling
    )
    return jnp.where(allowed[:, None], scores, -1e30)


def attend(queries, key_rows, value_rows, allowed):
    scores = masked_scores(queries, key_rows, allowed)
    top_score = jnp.max(scores, axis=-1, keepdims=True)
    log_total = top_score + jnp.log(jnp.sum(jnp.exp(scores - top_score), axis=-1, keepdims=True))
    attn_probs = jnp.exp(scores - log_total).astype(jnp.bfloat16)
    mixed = jnp.einsum(
        "whqk,wkhd->wqhd", attn_probs, value_rows, preferred_element_type=jnp.float32
    )
    return (mixed, log_total)


def attend_back(queries, key_rows, value_rows, allowed, log_total, grad_mixed):
    scaling = queries.shape[-1] ** (-0.5)
    attn_probs = jnp.exp(masked_scores(queries, key_rows, allowed) - log_total)
    grad_values = jnp.einsum(
        "whqk,wqhd->wkhd",
        attn_probs.astype(jnp.bfloat16),
        grad_mixed,
        preferred_element_type=jnp.float32,
    )
    grad_probs = jnp.einsum(
        "wqhd,wkhd->whqk", grad_mixed, value_rows, preferred_element_type=jnp.float32
    )
    grad_scores = attn_probs * (
        grad_probs - jnp.sum(attn_probs * grad_probs, axis=-1, keepdims=True)
    )
    grad_scores = grad_scores.astype(jnp.bfloat16)
    grad_query = (
        jnp.einsum("whqk,wkhd->wqhd", grad_scores, key_rows, preferred_element_type=jnp.float32)
        * scaling
    )
    grad_keys = (
        jnp.einsum("whqk,wqhd->wkhd", grad_scores, queries, preferred_element_type=jnp.float32)
        * scaling
    )
    return (grad_query, grad_keys, grad_values)


def finish_forward(row_data, mixed_low, weights):
    gain_rows = weights[4].astype(jnp.float32)
    bias_rows = weights[5].astype(jnp.float32)
    branch = jnp.dot(mixed_low, weights[1], preferred_element_type=jnp.float32) + bias_rows[2]
    first_norm, first_back = jax.vjp(layer_norm, row_data + branch, gain_rows[0], bias_rows[3])
    first_low = first_norm.astype(jnp.bfloat16)
    hidden_pre = jnp.dot(first_low, weights[2], preferred_element_type=jnp.float32) + weights[
        6
    ].astype(jnp.float32)
    activated, gelu_back = jax.vjp(exact_gelu, hidden_pre)
    activ_low = activated.astype(jnp.bfloat16)
    second = jnp.dot(activ_low, weights[3], preferred_element_type=jnp.float32) + bias_rows[4]
    result, result_back = jax.vjp(layer_norm, first_norm + second, gain_rows[1], bias_rows[5])
    return (result, (first_back, first_low, gelu_back, activ_low, result_back))


def finish_backward(grad_result, kept, mixed_low, weights):
    first_back, first_low, gelu_back, activ_low, result_back = kept
    grad_sum2, grad_gain2, grad_shift2 = result_back(grad_result)
    grad_second = grad_sum2.astype(jnp.bfloat16)
    grad_activ = jnp.dot(grad_second, weights[3].T, preferred_element_type=jnp.float32)
    grad_pre = gelu_back(grad_activ)[0].astype(jnp.bfloat16)
    grad_first = jnp.dot(grad_pre, weights[2].T, preferred_element_type=jnp.float32) + grad_sum2
    grad_sum1, grad_gain1, grad_shift1 = first_back(grad_first)
    grad_branch = grad_sum1.astype(jnp.bfloat16)
    grad_mixed = jnp.dot(grad_branch, weights[1].T, preferred_element_type=jnp.float32).astype(
        jnp.bfloat16
    )
    tail_bias = jnp.stack(
        [
            jnp.sum(grad_branch.astype(jnp.float32), axis=0),
            grad_shift1,
            jnp.sum(grad_second.astype(jnp.float32), axis=0),
            grad_shift2,
        ]
    )
    grad_gains = jnp.stack([grad_gain1, grad_gain2])
    grad_in_bias = jnp.sum(grad_pre.astype(jnp.float32), axis=0)
    factors = (grad_branch, first_low, grad_pre, activ_low, grad_second)
    matrices = ()
    grad_out = jnp.dot(mixed_low.T, grad_branch, preferred_element_type=jnp.float32)
    grad_in = jnp.dot(first_low.T, grad_pre, preferred_element_type=jnp.float32)
    grad_fc2 = jnp.dot(activ_low.T, grad_second, preferred_element_type=jnp.float32)
    matrices = (grad_out, grad_in, grad_fc2)
    return (grad_sum1, grad_mixed, matrices, (grad_gains, tail_bias, grad_in_bias), factors)


def start_backward(grad_query, grad_keys, grad_values, rows_low, weights, grad_resid):
    grad_joined = jnp.concatenate([grad_query, grad_keys, grad_values], axis=1)
    grad_rows = jnp.dot(grad_joined, weights[0].T, preferred_element_type=jnp.float32) + grad_resid
    head_bias = jnp.stack(
        [
            jnp.sum(grad_query.astype(jnp.float32), axis=0),
            jnp.sum(grad_values.astype(jnp.float32), axis=0),
        ]
    )
    grad_qkv = None
    grad_qkv = jnp.dot(rows_low.T, grad_joined, preferred_element_type=jnp.float32)
    return (grad_qkv, grad_rows, head_bias, grad_joined)


def per_device(
    tokens,
    doc_ids,
    teacher,
    seg_qkv,
    seg_out,
    seg_in,
    seg_fc2,
    seg_gains,
    seg_biases,
    seg_in_bias,
    cls_qkv,
    cls_out,
    cls_in,
    cls_fc2,
    cls_gains,
    cls_biases,
    cls_in_bias,
    seg_pos,
):
    rows_count, features = tokens.shape
    windows = rows_count // SEG
    seq_tokens = rows_count * lax.axis_size("fsdp")
    highest = lax.Precision.HIGHEST
    seg_full = (
        lax.all_gather(seg_qkv.astype(jnp.bfloat16), ("dp", "fsdp"), axis=0, tiled=True),
        lax.all_gather(seg_out.astype(jnp.bfloat16), ("dp", "fsdp"), axis=0, tiled=True),
        lax.all_gather(seg_in.astype(jnp.bfloat16), ("dp", "fsdp"), axis=0, tiled=True),
        lax.all_gather(seg_fc2.astype(jnp.bfloat16), ("dp", "fsdp"), axis=0, tiled=True),
        lax.all_gather(seg_gains.astype(jnp.bfloat16), ("dp", "fsdp"), axis=1, tiled=True),
        lax.all_gather(seg_biases.astype(jnp.bfloat16), ("dp", "fsdp"), axis=1, tiled=True),
        lax.all_gather(seg_in_bias.astype(jnp.bfloat16), ("dp", "fsdp"), axis=0, tiled=True),
    )
    doc_block = doc_ids.reshape(windows, SEG)
    allowed = doc_block[:, :, None] == doc_block[:, None, :]
    seg_rows_low, seg_queries, seg_keys, seg_values = project_forward(tokens, seg_full)
    seg_mixed, seg_log_total = attend(
        to_heads(seg_queries, windows),
        to_heads(seg_keys, windows),
        to_heads(seg_values, windows),
        allowed,
    )
    seg_mixed_low = seg_mixed.reshape(rows_count, features).astype(jnp.bfloat16)
    first_out, seg_kept = finish_forward(tokens, seg_mixed_low, seg_full)
    cls_full = (
        lax.all_gather(cls_qkv.astype(jnp.bfloat16), ("dp", "fsdp"), axis=0, tiled=True),
        lax.all_gather(cls_out.astype(jnp.bfloat16), ("dp", "fsdp"), axis=0, tiled=True),
        lax.all_gather(cls_in.astype(jnp.bfloat16), ("dp", "fsdp"), axis=0, tiled=True),
        lax.all_gather(cls_fc2.astype(jnp.bfloat16), ("dp", "fsdp"), axis=0, tiled=True),
        lax.all_gather(cls_gains.astype(jnp.bfloat16), ("dp", "fsdp"), axis=1, tiled=True),
        lax.all_gather(cls_biases.astype(jnp.bfloat16), ("dp", "fsdp"), axis=1, tiled=True),
        lax.all_gather(cls_in_bias.astype(jnp.bfloat16), ("dp", "fsdp"), axis=0, tiled=True),
        lax.all_gather(seg_pos.astype(jnp.bfloat16), ("dp", "fsdp"), axis=1, tiled=True),
    )
    cls_weights = cls_full[:7]
    pos_table = cls_full[7].astype(jnp.float32)
    slot_count = pos_table.shape[0]
    places = lax.axis_index("fsdp") * rows_count + jnp.arange(windows, dtype=jnp.int32) * SEG
    slot_index = places % seq_tokens // SEG
    picker = (slot_index[:, None] == jnp.arange(slot_count, dtype=jnp.int32)[None, :]).astype(
        jnp.float32
    )
    shaped_out = first_out.reshape(windows, SEG, features)
    cls_rows = shaped_out[:, 0] + jnp.dot(picker, pos_table, precision=highest)
    cls_rows_low, cls_queries, cls_keys, cls_values = project_forward(cls_rows, cls_weights)
    all_keys, all_values = (
        lax.all_gather(cls_keys, "fsdp", axis=0, tiled=True),
        lax.all_gather(cls_values, "fsdp", axis=0, tiled=True),
    )
    gathered_count = all_keys.shape[0]
    key_seq = jnp.arange(gathered_count, dtype=jnp.int32) * SEG // seq_tokens
    cls_allowed = ((places // seq_tokens)[:, None] == key_seq[None, :])[None]
    cls_mixed, cls_log_total = attend(
        to_heads(cls_queries, 1), to_heads(all_keys, 1), to_heads(all_values, 1), cls_allowed
    )
    cls_mixed_low = cls_mixed.reshape(windows, features).astype(jnp.bfloat16)
    cls_result, cls_kept = finish_forward(cls_rows, cls_mixed_low, cls_weights)
    output = shaped_out.at[:, 0].set(cls_result).reshape(rows_count, features)
    validity = (doc_ids >= 0).astype(jnp.float32)
    misfit = output - teacher
    err_part = jnp.sum(validity * jnp.sum(misfit * misfit, axis=1))
    err_total, token_count = lax.psum((err_part, jnp.sum(validity)), ("dp", "fsdp"))
    loss = err_total / (features * token_count)
    scaling = 2.0 * rows_count * lax.axis_size(("dp", "fsdp")) / token_count
    grad_output = (scaling * validity)[:, None] * misfit
    cls_again = (
        lax.all_gather(cls_qkv.astype(jnp.bfloat16), ("dp", "fsdp"), axis=0, tiled=True),
        lax.all_gather(cls_out.astype(jnp.bfloat16), ("dp", "fsdp"), axis=0, tiled=True),
        lax.all_gather(cls_in.astype(jnp.bfloat16), ("dp", "fsdp"), axis=0, tiled=True),
        lax.all_gather(cls_fc2.astype(jnp.bfloat16), ("dp", "fsdp"), axis=0, tiled=True),
        lax.all_gather(cls_gains.astype(jnp.bfloat16), ("dp", "fsdp"), axis=1, tiled=True),
        lax.all_gather(cls_biases.astype(jnp.bfloat16), ("dp", "fsdp"), axis=1, tiled=True),
        lax.all_gather(cls_in_bias.astype(jnp.bfloat16), ("dp", "fsdp"), axis=0, tiled=True),
    )
    grad_shaped = grad_output.reshape(windows, SEG, features)
    cls_resid, cls_grad_mixed, cls_mats, cls_small, cls_factors = finish_backward(
        grad_shaped[:, 0], cls_kept, cls_mixed_low, cls_again
    )
    cls_grad_query, key_part, value_part = attend_back(
        to_heads(cls_queries, 1),
        to_heads(all_keys, 1),
        to_heads(all_values, 1),
        cls_allowed,
        cls_log_total,
        to_heads(cls_grad_mixed, 1),
    )
    own_keys, own_values = (
        lax.psum_scatter(
            key_part.reshape(gathered_count, features).astype(jnp.bfloat16),
            "fsdp",
            scatter_dimension=0,
            tiled=True,
        ).astype(jnp.float32),
        lax.psum_scatter(
            value_part.reshape(gathered_count, features).astype(jnp.bfloat16),
            "fsdp",
            scatter_dimension=0,
            tiled=True,
        ).astype(jnp.float32),
    )
    cls_grad_qkv, grad_cls_rows, cls_head_bias, cls_joined = start_backward(
        cls_grad_query.reshape(windows, features).astype(jnp.bfloat16),
        own_keys.astype(jnp.bfloat16),
        own_values.astype(jnp.bfloat16),
        cls_rows_low,
        cls_again,
        cls_resid,
    )
    grad_pos = jnp.dot(picker.T, grad_cls_rows, precision=highest)
    cls_grads = (
        lax.psum_scatter(cls_grad_qkv, ("dp", "fsdp"), scatter_dimension=0, tiled=True),
        lax.psum_scatter(cls_mats[0], ("dp", "fsdp"), scatter_dimension=0, tiled=True),
        lax.psum_scatter(cls_mats[1], ("dp", "fsdp"), scatter_dimension=0, tiled=True),
        lax.psum_scatter(cls_mats[2], ("dp", "fsdp"), scatter_dimension=0, tiled=True),
        lax.psum_scatter(cls_small[0], ("dp", "fsdp"), scatter_dimension=1, tiled=True),
        lax.psum_scatter(
            jnp.concatenate([cls_head_bias, cls_small[1]], axis=0),
            ("dp", "fsdp"),
            scatter_dimension=1,
            tiled=True,
        ),
        lax.psum_scatter(cls_small[2], ("dp", "fsdp"), scatter_dimension=0, tiled=True),
        lax.psum_scatter(grad_pos, ("dp", "fsdp"), scatter_dimension=1, tiled=True),
    )
    seg_again = (
        lax.all_gather(seg_qkv.astype(jnp.bfloat16), ("dp", "fsdp"), axis=0, tiled=True),
        lax.all_gather(seg_out.astype(jnp.bfloat16), ("dp", "fsdp"), axis=0, tiled=True),
        lax.all_gather(seg_in.astype(jnp.bfloat16), ("dp", "fsdp"), axis=0, tiled=True),
        lax.all_gather(seg_fc2.astype(jnp.bfloat16), ("dp", "fsdp"), axis=0, tiled=True),
        lax.all_gather(seg_gains.astype(jnp.bfloat16), ("dp", "fsdp"), axis=1, tiled=True),
        lax.all_gather(seg_biases.astype(jnp.bfloat16), ("dp", "fsdp"), axis=1, tiled=True),
        lax.all_gather(seg_in_bias.astype(jnp.bfloat16), ("dp", "fsdp"), axis=0, tiled=True),
    )
    grad_first = grad_shaped.at[:, 0].set(grad_cls_rows).reshape(rows_count, features)
    seg_resid, seg_grad_mixed, seg_mats, seg_small, seg_factors = finish_backward(
        grad_first, seg_kept, seg_mixed_low, seg_again
    )
    seg_grad_query, seg_grad_keys, seg_grad_values = attend_back(
        to_heads(seg_queries, windows),
        to_heads(seg_keys, windows),
        to_heads(seg_values, windows),
        allowed,
        seg_log_total,
        to_heads(seg_grad_mixed, windows),
    )
    seg_grad_qkv, grad_tokens, seg_head_bias, seg_joined = start_backward(
        seg_grad_query.reshape(rows_count, features).astype(jnp.bfloat16),
        seg_grad_keys.reshape(rows_count, features).astype(jnp.bfloat16),
        seg_grad_values.reshape(rows_count, features).astype(jnp.bfloat16),
        seg_rows_low,
        seg_again,
        seg_resid,
    )
    seg_grads = (
        lax.psum_scatter(seg_grad_qkv, ("dp", "fsdp"), scatter_dimension=0, tiled=True),
        lax.psum_scatter(seg_mats[0], ("dp", "fsdp"), scatter_dimension=0, tiled=True),
        lax.psum_scatter(seg_mats[1], ("dp", "fsdp"), scatter_dimension=0, tiled=True),
        lax.psum_scatter(seg_mats[2], ("dp", "fsdp"), scatter_dimension=0, tiled=True),
        lax.psum_scatter(seg_small[0], ("dp", "fsdp"), scatter_dimension=1, tiled=True),
        lax.psum_scatter(
            jnp.concatenate([seg_head_bias, seg_small[1]], axis=0),
            ("dp", "fsdp"),
            scatter_dimension=1,
            tiled=True,
        ),
        lax.psum_scatter(seg_small[2], ("dp", "fsdp"), scatter_dimension=0, tiled=True),
    )
    return (
        output,
        loss,
        grad_tokens,
        seg_grads[0],
        seg_grads[1],
        seg_grads[2],
        seg_grads[3],
        seg_grads[4],
        seg_grads[5],
        seg_grads[6],
        cls_grads[0],
        cls_grads[1],
        cls_grads[2],
        cls_grads[3],
        cls_grads[4],
        cls_grads[5],
        cls_grads[6],
        cls_grads[7],
    )


def solution(mesh):
    return jax.shard_map(
        per_device,
        mesh=mesh,
        in_specs=(
            P(("dp", "fsdp"), None),
            P(("dp", "fsdp")),
            P(("dp", "fsdp"), None),
            P(("dp", "fsdp"), None),
            P(("dp", "fsdp"), None),
            P(("dp", "fsdp"), None),
            P(("dp", "fsdp"), None),
            P(None, ("dp", "fsdp")),
            P(None, ("dp", "fsdp")),
            P(("dp", "fsdp")),
            P(("dp", "fsdp"), None),
            P(("dp", "fsdp"), None),
            P(("dp", "fsdp"), None),
            P(("dp", "fsdp"), None),
            P(None, ("dp", "fsdp")),
            P(None, ("dp", "fsdp")),
            P(("dp", "fsdp")),
            P(None, ("dp", "fsdp")),
        ),
        out_specs=(
            P(("dp", "fsdp"), None),
            P(),
            P(("dp", "fsdp"), None),
            P(("dp", "fsdp"), None),
            P(("dp", "fsdp"), None),
            P(("dp", "fsdp"), None),
            P(("dp", "fsdp"), None),
            P(None, ("dp", "fsdp")),
            P(None, ("dp", "fsdp")),
            P(("dp", "fsdp")),
            P(("dp", "fsdp"), None),
            P(("dp", "fsdp"), None),
            P(("dp", "fsdp"), None),
            P(("dp", "fsdp"), None),
            P(None, ("dp", "fsdp")),
            P(None, ("dp", "fsdp")),
            P(("dp", "fsdp")),
            P(None, ("dp", "fsdp")),
        ),
        check_vma=False,
    )
```

profile of v0, /device:TPU:0, one launch (start us, length us, event | category | flops | bytes accessed | tf_op | source)
XLA Modules:
  0.0 1647.6 jit_solution(9354592035308909439)
XLA Ops:
  20.6 42.3 %all-reduce.12 = (bf16[3072]{0:T(1024)(128)(2,1)S(1)}, bf16[3072]{0:T(1024)(128)(2,1)S(1)}) all-reduce(bf16[3072]{0:T(1024)(128)(2,1)S(1)} %dynamic-update-slice.6, bf16[3072]{0:T(1024)(128)(2,1)S(1)} %dynamic-update-slice.7), channel_id=1, replica_groups=mesh['dp'=8,'fsdp'=4] {'dp','fsdp'}, use_global_device_ids=true, to_apply=%add | all-reduce | flops 6144 | bytes 24576
  63.0 40.1 %all-gather.6 = bf16[32,24,2]{1,2,0:T(2,128)(2,1)S(1)} all-gather(bf16[1,24,2]{1,2,0:T(2,128)(2,1)S(1)} %convert_bitcast_fusion.3), channel_id=1, replica_groups=mesh['dp'=8,'fsdp'=4] {'dp','fsdp'}, dimensions={0}, use_global_device_ids=true | all-gather | bytes 3168 | tf_op jit(solution)/shard_map/all_gather | solution.py:193
  103.2 36.4 %all-gather.1 = bf16[32,24,2]{1,2,0:T(2,128)(2,1)S(1)} all-gather(bf16[1,24,2]{1,2,0:T(2,128)(2,1)S(1)} %convert_bitcast_fusion.4), channel_id=1, replica_groups=mesh['dp'=8,'fsdp'=4] {'dp','fsdp'}, dimensions={0}, use_global_device_ids=true | all-gather | bytes 3168 | tf_op jit(solution)/shard_map/all_gather | solution.py:173
  140.1 38.6 %all-gather.3 = bf16[32,24,6]{1,2,0:T(8,128)(2,1)S(1)} all-gather(bf16[1,24,6]{1,2,0:T(8,128)(2,1)S(1)} %convert_bitcast_fusion.1), channel_id=1, replica_groups=mesh['dp'=8,'fsdp'=4] {'dp','fsdp'}, dimensions={0}, use_global_device_ids=true | all-gather | bytes 9504 | tf_op jit(solution)/shard_map/all_gather | solution.py:194
  179.6 36.8 %all-gather = bf16[32,24,6]{1,2,0:T(8,128)(2,1)S(1)} all-gather(bf16[1,24,6]{1,2,0:T(8,128)(2,1)S(1)} %convert_bitcast_fusion.2), channel_id=1, replica_groups=mesh['dp'=8,'fsdp'=4] {'dp','fsdp'}, dimensions={0}, use_global_device_ids=true | all-gather | bytes 9504 | tf_op jit(solution)/shard_map/all_gather | solution.py:174
  217.0 39.3 %all-gather.2 = bf16[32,24,16]{1,2,0:T(8,128)(2,1)S(1)} all-gather(bf16[1,24,16]{1,2,0:T(8,128)(2,1)S(1)} %convert_bitcast_fusion), channel_id=1, replica_groups=mesh['dp'=8,'fsdp'=4] {'dp','fsdp'}, dimensions={0}, use_global_device_ids=true | all-gather | bytes 25344 | tf_op jit(solution)/shard_map/all_gather | solution.py:196
  276.2 21.3 %multiply_convert_fusion = (bf16[512,3072]{1,0:T(8,128)(2,1)}, f32[512,3072]{1,0:T(8,128)}, f32[512,3072]{1,0:T(8,128)}) fusion(f32[3072]{0:T(1024)S(1)} %convert_element_type.298, bf16[768,3072]{1,0:T(8,128)(2,1)} %all-gather.20.cloned.1.call-done, f32[512,768]{1,0:T(8,128)} %copy-done.7, f32[768]{0:T(1024)S(1)} %get-tuple-element.131, ...), kind=kOutput, calls=%fused_computation.4 | convolution fusion | flops 2521694208 | bytes 22042624 | tf_op jit(solution)/shard_map/dot_general | solution.py:89
  297.6 6.5 fusion.90
  306.9 19.1 %all-gather.24.cloned.1.call-done = bf16[768,2304]{1,0:T(8,128)(2,1)} async-done(((bf16[24,2304]{1,0:T(8,128)(2,1)}), bf16[768,2304]{1,0:T(8,128)(2,1)}) %all-gather.24.cloned.1.call-update) | async-done | bytes 3538960 | tf_op jit(solution)/shard_map/all_gather | solution.py:189
  328.7 5.2 all-gather.4
  334.0 5.2 all-gather.5
  340.1 42.2 %all-gather.26.cloned.1.call-done = bf16[768,768]{1,0:T(8,128)(2,1)} async-done(((bf16[24,768]{1,0:T(8,128)(2,1)}), bf16[768,768]{1,0:T(8,128)(2,1)}) %all-gather.26.cloned.1.call-update) | async-done | bytes 1179664 | tf_op jit(solution)/shard_map/all_gather | solution.py:190
  384.2 64.1 %all-gather.28.cloned.1.call-done = bf16[768,3072]{1,0:T(8,128)(2,1)} async-done(((bf16[24,3072]{1,0:T(8,128)(2,1)}), bf16[768,3072]{1,0:T(8,128)(2,1)}) %all-gather.28.cloned.1.call-update) | async-done | bytes 4718608 | tf_op jit(solution)/shard_map/all_gather | solution.py:191
  451.5 62.7 %all-gather.30.cloned.1.call-done = bf16[3072,768]{1,0:T(8,128)(2,1)} async-done(((bf16[96,768]{1,0:T(8,128)(2,1)}), bf16[3072,768]{1,0:T(8,128)(2,1)}) %all-gather.30.cloned.1.call-update) | async-done | bytes 4718608 | tf_op jit(solution)/shard_map/all_gather | solution.py:192
  522.0 40.0 %psum.15 = f32[]{:T(128)} all-reduce(f32[]{:T(128)} %get-tuple-element.140), channel_id=1, replica_groups=mesh['dp'=8,'fsdp'=4] {'dp','fsdp'}, use_global_device_ids=true, to_apply=%region_16.17 | all-reduce | flops 1 | bytes 8 | tf_op jit(solution)/shard_map/psum | solution.py:225
  582.4 11.7 all-reduce.13
  602.6 9.4 convert_reduce_fusion
  641.2 4.9 convolution_bitcast_fusion
  646.1 8.1 copy.194
  659.7 7.2 fusion.79
  668.1 8.2 fusion.94
  677.0 5.2 fusion.76
  682.3 5.1 fusion.96
  689.7 42.1 %all-reduce.15 = (f32[]{:T(128)}, f32[2,768]{1,0:T(2,128)S(1)}, f32[6,768]{1,0:T(8,128)S(1)}, f32[3072]{0:T(1024)S(1)}, f32[2,768]{1,0:T(2,128)S(1)}, /*index=5*...) all-reduce(f32[]{:T(128)} %get-tuple-element.141, ...), channel_id=1, replica_groups=mesh['dp'=8,'fsdp'=4] {'dp','fsdp'}, use_global_device_ids=true, to_apply=%region_14.15 | all-reduce | flops 30721 | bytes 245768 | tf_op jit(solution)/shard_map/psum | solution.py:225
  736.3 6.0 add_add_fusion.4
  742.3 81.3 %reduce-scatter.24.cloned.1.call-done = f32[24,768]{1,0:T(8,128)} async-done(((f32[768,768]{1,0:T(8,128)}), f32[24,768]{1,0:T(8,128)}) %reduce-scatter.24.cloned.1.call-update) | async-done | bytes 73744 | tf_op jit(solution)/shard_map/reduce_scatter | solution.py:275
  823.6 124.4 %reduce-scatter.30.cloned.1.call-done = f32[24,2304]{1,0:T(8,128)} async-done(((f32[768,2304]{1,0:T(8,128)}), f32[24,2304]{1,0:T(8,128)}) %reduce-scatter.30.cloned.1.call-update) | async-done | bytes 221200
  948.1 125.5 %reduce-scatter.22.cloned.1.call-done = f32[24,2304]{1,0:T(8,128)} async-done(((f32[768,2304]{1,0:T(8,128)}), f32[24,2304]{1,0:T(8,128)}) %reduce-scatter.22.cloned.1.call-update) | async-done | bytes 221200 | tf_op jit(solution)/shard_map/reduce_scatter | solution.py:274
  1073.5 141.0 %reduce-scatter.18.cloned.1.call-done = f32[24,3072]{1,0:T(8,128)} async-done(((f32[768,3072]{1,0:T(8,128)}), f32[24,3072]{1,0:T(8,128)}) %reduce-scatter.18.cloned.1.call-update) | async-done | bytes 294928 | tf_op jit(solution)/shard_map/reduce_scatter | solution.py:320
  1214.6 142.1 %reduce-scatter.20.cloned.1.call-done = f32[96,768]{1,0:T(8,128)} async-done(((f32[3072,768]{1,0:T(8,128)}), f32[96,768]{1,0:T(8,128)}) %reduce-scatter.20.cloned.1.call-update) | async-done | bytes 294928 | tf_op jit(solution)/shard_map/reduce_scatter | solution.py:321
  1356.6 141.0 %reduce-scatter.26.cloned.1.call-done = f32[24,3072]{1,0:T(8,128)} async-done(((f32[768,3072]{1,0:T(8,128)}), f32[24,3072]{1,0:T(8,128)}) %reduce-scatter.26.cloned.1.call-update) | async-done | bytes 294928 | tf_op jit(solution)/shard_map/reduce_scatter | solution.py:276
  1497.7 141.8 %reduce-scatter.28.cloned.1.call-done = f32[96,768]{1,0:T(8,128)} async-done(((f32[3072,768]{1,0:T(8,128)}), f32[96,768]{1,0:T(8,128)}) %reduce-scatter.28.cloned.1.call-update) | async-done | bytes 294928 | tf_op jit(solution)/shard_map/reduce_scatter | solution.py:277
  (393 shorter events, 123.0 us)
Async XLA Ops:
  7.2 249.3 %copy-start.83 = (u32[32]{0:T(128)S(1)}, u32[32]{0:T(128)}, u32[]{:S(2)}) copy-start(u32[32]{0:T(128)} %constant.260) | copy-start | bytes 388
  7.3 209.5 %copy-start.48 = (s32[512]{0:T(512)S(1)}, s32[512]{0:T(512)}, u32[]{:S(2)}) copy-start(s32[512]{0:T(512)} %param.23) | copy-start | bytes 6148
  7.3 250.5 %copy-start.21 = (f32[512,768]{1,0:T(8,128)S(1)}, f32[512,768]{1,0:T(8,128)}, u32[]{:S(2)}) copy-start(f32[512,768]{1,0:T(8,128)} %param.22) | copy-start | bytes 4718596
  7.3 250.5 %all-gather.16.cloned.1.call-start = ((), (), s32[]{:S(2)}) async-start(), calls=%async_computation.8 | async-start | bytes 3649536 | tf_op jit(solution)/shard_map/all_gather | solution.py:169
  9.1 262.7 %all-gather.18.cloned.1.call-start = ((), (), s32[]{:S(2)}) async-start(), calls=%async_computation.9 | async-start | bytes 1216512 | tf_op jit(solution)/shard_map/all_gather | solution.py:170
  10.7 265.5 %all-gather.20.cloned.1.call-start = ((), (), s32[]{:S(2)}) async-start(), calls=%async_computation.10 | async-start | bytes 4866048 | tf_op jit(solution)/shard_map/all_gather | solution.py:171
  12.4 285.2 %all-gather.22.cloned.1.call-start = ((), (), s32[]{:S(2)}) async-start(), calls=%async_computation.11 | async-start | bytes 4866048 | tf_op jit(solution)/shard_map/all_gather | solution.py:172
  14.1 311.9 %all-gather.24.cloned.1.call-start = ((), (), s32[]{:S(2)}) async-start(), calls=%async_computation.12 | async-start | bytes 3649536 | tf_op jit(solution)/shard_map/all_gather | solution.py:189
  15.8 366.5 %all-gather.26.cloned.1.call-start = ((), (), s32[]{:S(2)}) async-start(), calls=%async_computation.13 | async-start | bytes 1216512 | tf_op jit(solution)/shard_map/all_gather | solution.py:190
  17.4 430.9 %all-gather.28.cloned.1.call-start = ((), (), s32[]{:S(2)}) async-start(), calls=%async_computation.14 | async-start | bytes 4866048 | tf_op jit(solution)/shard_map/all_gather | solution.py:191
  19.1 495.1 %all-gather.30.cloned.1.call-start = ((), (), s32[]{:S(2)}) async-start(), calls=%async_computation.15 | async-start | bytes 4866048 | tf_op jit(solution)/shard_map/all_gather | solution.py:192
  19.8 722.5 %reduce-scatter.16.cloned.1.call-start = ((), (), s32[]{:S(2)}) async-start(), calls=%async_computation.16 | async-start | bytes 2433024 | tf_op jit(solution)/shard_map/reduce_scatter | solution.py:319
  19.9 286.8 %copy-start.81 = (s32[4]{0:T(128)}, s32[4]{0:T(128)S(1)}, u32[]{:S(2)}) copy-start(s32[4]{0:T(128)S(1)} %and_select_fusion.2) | copy-start | bytes 52
  63.0 213.3 %copy-start.62 = (f32[3072]{0:T(1024)}, f32[3072]{0:T(1024)S(1)}, u32[]{:S(2)}) copy-start(f32[3072]{0:T(1024)S(1)} %convert_element_type.298) | copy-start | bytes 36868
  139.9 157.7 %copy-start.58 = (f32[768]{0:T(1024)}, f32[768]{0:T(1024)S(1)}, u32[]{:S(2)}) copy-start(f32[768]{0:T(1024)S(1)} %get-tuple-element.139) | copy-start | bytes 9220
  216.8 80.8 %copy-start.70 = (f32[768]{0:T(1024)}, f32[768]{0:T(1024)S(1)}, u32[]{:S(2)}) copy-start(f32[768]{0:T(1024)S(1)} %get-tuple-element.131) | copy-start | bytes 9220
  328.7 119.6 %copy-start.54 = (bf16[4,12,64]{2,1,0:T(8,128)(2,1)}, bf16[4,12,64]{2,1,0:T(8,128)(2,1)S(1)}, u32[]{:S(2)}) copy-start(bf16[4,12,64]{2,1,0:T(8,128)(2,1)S(1)} %reshape.491) | copy-start | bytes 18436
  334.0 114.3 %copy-start.26 = (bf16[16,12,64]{2,1,0:T(8,128)(2,1)}, bf16[16,12,64]{2,1,0:T(8,128)(2,1)S(1)}, u32[]{:S(2)}) copy-start(bf16[16,12,64]{2,1,0:T(8,128)(2,1)S(1)} %reshape.490) | copy-start | bytes 73732
  339.8 111.8 %copy-start.35 = (f32[12,4]{1,0:T(8,128)}, f32[12,4]{1,0:T(8,128)S(1)}, u32[]{:S(2)}) copy-start(f32[12,4]{1,0:T(8,128)S(1)} %log_add_fusion.1) | copy-start | bytes 580
  340.1 108.2 %copy-start.28 = (bf16[4,768]{1,0:T(4,128)(2,1)}, bf16[4,768]{1,0:T(4,128)(2,1)S(1)}, u32[]{:S(2)}) copy-start(bf16[4,768]{1,0:T(4,128)(2,1)S(1)} %convert_element_type.312) | copy-start | bytes 18436
  383.9 133.5 %copy-start.39 = (f32[4]{0:T(128)}, f32[4]{0:T(128)S(1)}, u32[]{:S(2)}) copy-start(f32[4]{0:T(128)S(1)} %broadcast_multiply_fusion.4) | copy-start | bytes 52
  384.1 130.1 %copy-start.73 = (f32[4]{0:T(128)}, f32[4]{0:T(128)S(1)}, u32[]{:S(2)}) copy-start(f32[4]{0:T(128)S(1)} %multiply_reduce_fusion.13) | copy-start | bytes 52
  384.2 130.0 %copy-start.49 = (f32[4]{0:T(128)}, f32[4]{0:T(128)S(1)}, u32[]{:S(2)}) copy-start(f32[4]{0:T(128)S(1)} %fusion.70) | copy-start | bytes 52
  451.5 66.1 %copy-start.57 = (f32[768]{0:T(1024)S(1)}, f32[768]{0:T(1024)}, u32[]{:S(2)}) copy-start(f32[768]{0:T(1024)} %get-tuple-element.123) | copy-start | bytes 9220
  620.4 203.2 %reduce-scatter.24.cloned.1.call-start = ((), (), s32[]{:S(2)}) async-start(), calls=%async_computation.20 | async-start | bytes 2433024 | tf_op jit(solution)/shard_map/reduce_scatter | solution.py:275
  622.7 325.4 %reduce-scatter.30.cloned.1.call-start = ((), (), s32[]{:S(2)}) async-start(), calls=%async_computation.23 | async-start | bytes 7299072
  654.2 419.3 %reduce-scatter.22.cloned.1.call-start = ((), (), s32[]{:S(2)}) async-start(), calls=%async_computation.19 | async-start | bytes 7299072 | tf_op jit(solution)/shard_map/reduce_scatter | solution.py:274
  658.4 556.2 %reduce-scatter.18.cloned.1.call-start = ((), (), s32[]{:S(2)}) async-start(), calls=%async_computation.17 | async-start | bytes 9732096 | tf_op jit(solution)/shard_map/reduce_scatter | solution.py:320
  667.0 689.7 %reduce-scatter.20.cloned.1.call-start = ((), (), s32[]{:S(2)}) async-start(), calls=%async_computation.18 | async-start | bytes 9732096 | tf_op jit(solution)/shard_map/reduce_scatter | solution.py:321
  676.3 821.4 %reduce-scatter.26.cloned.1.call-start = ((), (), s32[]{:S(2)}) async-start(), calls=%async_computation.21 | async-start | bytes 9732096 | tf_op jit(solution)/shard_map/reduce_scatter | solution.py:276
  682.2 957.2 %reduce-scatter.28.cloned.1.call-start = ((), (), s32[]{:S(2)}) async-start(), calls=%async_computation.22 | async-start | bytes 9732096 | tf_op jit(solution)/shard_map/reduce_scatter | solution.py:277
  687.4 48.8 %copy-start.11 = (f32[512,768]{1,0:T(8,128)S(1)}, f32[512,768]{1,0:T(8,128)}, u32[]{:S(2)}) copy-start(f32[512,768]{1,0:T(8,128)} %copy-done.10) | copy-start | bytes 4718596
  (71 other events, 486.9 us)
Sparse Core Ops, SparseCore 0:
  11.6 63.3 all-gather.15
  78.5 52.7 all-gather.17
  134.8 62.7 all-gather.19
  201.0 62.5 all-gather.21
  266.9 59.0 all-gather.23
  329.4 52.8 all-gather.25
  385.8 62.5 all-gather.27
  451.8 62.3 all-gather.29
  620.6 98.3 reduce-scatter.15
  725.5 98.0 reduce-scatter.23
  829.9 118.1 reduce-scatter.29
  955.1 118.3 reduce-scatter.21
  1080.0 134.5 reduce-scatter.17
  1221.9 134.6 reduce-scatter.19
  1363.0 134.6 reduce-scatter.25
  1505.0 134.4 reduce-scatter.27
where the time goes:
time: 1650 us
  waiting for transfers between devices  1090 us (66%)
  blocking collectives  338 us (20%)
  matrix products  130 us (8%)
  local copies, waits for them, and re-layouts  45.2 us (3%)
  other arithmetic  28.8 us (2%)
  between operations  19.8 us (1%)
    reduce_scatter x1, waiting for transfers between devices, per_device(): lax.psum_scatter(seg_mats[2], ('dp', 'fsdp'), scatter_dimension=0, tiled=...  142 us
    reduce_scatter x1, waiting for transfers between devices, per_device(): lax.psum_scatter(cls_mats[2], ('dp', 'fsdp'), scatter_dimension=0, tiled=...  142 us
    reduce_scatter x1, waiting for transfers between devices, per_device(): lax.psum_scatter(cls_mats[1], ('dp', 'fsdp'), scatter_dimension=0, tiled=...  141 us
    reduce_scatter x1, waiting for transfers between devices, per_device(): lax.psum_scatter(seg_mats[1], ('dp', 'fsdp'), scatter_dimension=0, tiled=...  141 us
    reduce_scatter x1, waiting for transfers between devices, per_device(): lax.psum_scatter(cls_grad_qkv, ('dp', 'fsdp'), scatter_dimension=0, tiled...  125 us
    unnamed x17, waiting for transfers between devices  125 us
    psum x2, blocking collectives, per_device(): lax.psum((err_part, jnp.sum(validity)), ('dp', 'fsdp'))  82 us
    reduce_scatter x1, waiting for transfers between devices, per_device(): lax.psum_scatter(cls_mats[0], ('dp', 'fsdp'), scatter_dimension=0, tiled=...  81.3 us
  transfers between devices with their start and end apart: 16, of which 11 were waited for; matrix products, arithmetic and copies ran while one was open for 8% of the time, Pallas kernels for 0%

commit v1 on v0

v1 whole, which is shorter than its diff:
```python
import jax
import jax.numpy as jnp
from jax import lax
from jax.sharding import PartitionSpec as P

NHEADS = 12
HEAD = 64
SEG = 128


def layer_norm(row_data, gain_row, shift_row):
    centered = row_data - jnp.mean(row_data, axis=-1, keepdims=True)
    normed = centered * lax.rsqrt(jnp.mean(centered * centered, axis=-1, keepdims=True) + 1e-05)
    return normed * gain_row + shift_row


def exact_gelu(hidden_pre):
    return jax.nn.gelu(hidden_pre, approximate=False)


def to_heads(flat, groups):
    return flat.reshape(groups, flat.shape[0] // groups, NHEADS, HEAD)


def project_forward(row_data, weights):
    features = weights[1].shape[0]
    bias_rows = weights[5].astype(jnp.float32)
    rows_low = row_data.astype(jnp.bfloat16)
    joined = jnp.dot(rows_low, weights[0], preferred_element_type=jnp.float32)
    queries = (joined[:, :features] + bias_rows[0]).astype(jnp.bfloat16)
    key_rows = joined[:, features : 2 * features].astype(jnp.bfloat16)
    value_rows = (joined[:, 2 * features :] + bias_rows[1]).astype(jnp.bfloat16)
    return (rows_low, queries, key_rows, value_rows)


def masked_scores(queries, key_rows, allowed):
    scaling = queries.shape[-1] ** (-0.5)
    scores = (
        jnp.einsum("wqhd,wkhd->whqk", queries, key_rows, preferred_element_type=jnp.float32)
        * scaling
    )
    return jnp.where(allowed[:, None], scores, -1e30)


def attend(queries, key_rows, value_rows, allowed):
    scores = masked_scores(queries, key_rows, allowed)
    top_score = jnp.max(scores, axis=-1, keepdims=True)
    log_total = top_score + jnp.log(jnp.sum(jnp.exp(scores - top_score), axis=-1, keepdims=True))
    attn_probs = jnp.exp(scores - log_total).astype(jnp.bfloat16)
    mixed = jnp.einsum(
        "whqk,wkhd->wqhd", attn_probs, value_rows, preferred_element_type=jnp.float32
    )
    return (mixed, log_total)


def attend_back(queries, key_rows, value_rows, allowed, log_total, grad_mixed):
    scaling = queries.shape[-1] ** (-0.5)
    attn_probs = jnp.exp(masked_scores(queries, key_rows, allowed) - log_total)
    grad_values = jnp.einsum(
        "whqk,wqhd->wkhd",
        attn_probs.astype(jnp.bfloat16),
        grad_mixed,
        preferred_element_type=jnp.float32,
    )
    grad_probs = jnp.einsum(
        "wqhd,wkhd->whqk", grad_mixed, value_rows, preferred_element_type=jnp.float32
    )
    grad_scores = attn_probs * (
        grad_probs - jnp.sum(attn_probs * grad_probs, axis=-1, keepdims=True)
    )
    grad_scores = grad_scores.astype(jnp.bfloat16)
    grad_query = (
        jnp.einsum("whqk,wkhd->wqhd", grad_scores, key_rows, preferred_element_type=jnp.float32)
        * scaling
    )
    grad_keys = (
        jnp.einsum("whqk,wqhd->wkhd", grad_scores, queries, preferred_element_type=jnp.float32)
        * scaling
    )
    return (grad_query, grad_keys, grad_values)


def finish_forward(row_data, mixed_low, weights):
    gain_rows = weights[4].astype(jnp.float32)
    bias_rows = weights[5].astype(jnp.float32)
    branch = jnp.dot(mixed_low, weights[1], preferred_element_type=jnp.float32) + bias_rows[2]
    first_norm, first_back = jax.vjp(layer_norm, row_data + branch, gain_rows[0], bias_rows[3])
    first_low = first_norm.astype(jnp.bfloat16)
    hidden_pre = jnp.dot(first_low, weights[2], preferred_element_type=jnp.float32) + weights[
        6
    ].astype(jnp.float32)
    activated, gelu_back = jax.vjp(exact_gelu, hidden_pre)
    activ_low = activated.astype(jnp.bfloat16)
    second = jnp.dot(activ_low, weights[3], preferred_element_type=jnp.float32) + bias_rows[4]
    result, result_back = jax.vjp(layer_norm, first_norm + second, gain_rows[1], bias_rows[5])
    return (result, (first_back, first_low, gelu_back, activ_low, result_back))


def finish_backward(grad_result, kept, mixed_low, weights):
    first_back, first_low, gelu_back, activ_low, result_back = kept
    grad_sum2, grad_gain2, grad_shift2 = result_back(grad_result)
    grad_second = grad_sum2.astype(jnp.bfloat16)
    grad_activ = jnp.dot(grad_second, weights[3].T, preferred_element_type=jnp.float32)
    grad_pre = gelu_back(grad_activ)[0].astype(jnp.bfloat16)
    grad_first = jnp.dot(grad_pre, weights[2].T, preferred_element_type=jnp.float32) + grad_sum2
    grad_sum1, grad_gain1, grad_shift1 = first_back(grad_first)
    grad_branch = grad_sum1.astype(jnp.bfloat16)
    grad_mixed = jnp.dot(grad_branch, weights[1].T, preferred_element_type=jnp.float32).astype(
        jnp.bfloat16
    )
    tail_bias = jnp.stack(
        [
            jnp.sum(grad_branch.astype(jnp.float32), axis=0),
            grad_shift1,
            jnp.sum(grad_second.astype(jnp.float32), axis=0),
            grad_shift2,
        ]
    )
    grad_gains = jnp.stack([grad_gain1, grad_gain2])
    grad_in_bias = jnp.sum(grad_pre.astype(jnp.float32), axis=0)
    factors = (grad_branch, first_low, grad_pre, activ_low, grad_second)
    return (grad_sum1, grad_mixed, (grad_gains, tail_bias, grad_in_bias), factors)


def start_backward(grad_query, grad_keys, grad_values, weights, grad_resid):
    grad_joined = jnp.concatenate([grad_query, grad_keys, grad_values], axis=1)
    grad_rows = jnp.dot(grad_joined, weights[0].T, preferred_element_type=jnp.float32) + grad_resid
    head_bias = jnp.stack(
        [
            jnp.sum(grad_query.astype(jnp.float32), axis=0),
            jnp.sum(grad_values.astype(jnp.float32), axis=0),
        ]
    )
    return (grad_rows, head_bias, grad_joined)


AXES = ("dp", "fsdp")


class Grid:
    def __init__(self):
        fsdp, dp = lax.axis_size("fsdp"), lax.axis_size("dp")
        self.ny = fsdp // 2
        self.nx = self.ny
        self.nz = dp // self.nx
        self.count = fsdp * dp
        me = lax.axis_index("dp")
        chip = lax.axis_index("fsdp")
        self.z, self.x = me // self.nx, me % self.nx
        self.y, self.core = chip // 2, chip % 2
        self.even = self.core == 0
        self.index = me * fsdp + chip
        self.first = jnp.where(self.even, self.x, self.y)
        self.second = jnp.where(self.even, self.y, self.x)

    def pairs(self, axis, step):
        out = []
        for i in range(self.count):
            c, y = i % 2, i // 2 % self.ny
            x, z = i // (2 * self.ny) % self.nx, i // (2 * self.ny * self.nx)
            along = axis
            if axis == "first":
                along = "x" if c == 0 else "y"
            if axis == "second":
                along = "y" if c == 0 else "x"
            if along == "core":
                c = (c + step) % 2
            if along == "y":
                y = (y + step) % self.ny
            if along == "x":
                x = (x + step) % self.nx
            if along == "z":
                z = (z + step) % self.nz
            out.append((i, ((z * self.nx + x) * self.ny + y) * 2 + c))
        return out

    def size(self, axis):
        return {"core": 2, "z": self.nz}.get(axis, self.nx)

    def place(self, axis):
        return {"core": self.core, "z": self.z, "first": self.first, "second": self.second}[axis]

    def send(self, value, axis, step=1):
        return lax.ppermute(value, AXES, self.pairs(axis, step))

    def gather_axis(self, rows, axis):
        n, place = self.size(axis), self.place(axis)
        parts = [rows] + [self.send(rows, axis, n - k) for k in range(1, n)]
        if n == 1:
            return rows
        if n == 2:
            return jnp.where(
                place == 0, jnp.concatenate(parts), jnp.concatenate([parts[1], parts[0]])
            )
        ring = jnp.concatenate(parts + parts[:-1])
        step = rows.shape[0]
        return lax.dynamic_slice_in_dim(ring, (n - place) % n * step, n * step, 0)

    def scatter_axis(self, blocks, axis):
        n, place = self.size(axis), self.place(axis)
        total = lax.dynamic_index_in_dim(blocks, place, 0, keepdims=False).astype(jnp.float32)
        for k in range(1, n):
            block = lax.dynamic_index_in_dim(blocks, (place + k) % n, 0, keepdims=False)
            total = total + self.send(block, axis, k).astype(jnp.float32)
        return total.astype(jnp.bfloat16)

    def gather(self, shard):
        rows, half = shard.shape[0], shard.shape[1] // 2
        left, right = shard[:, :half], shard[:, half:]
        keep = jnp.where(self.even, left, right)
        came = self.send(jnp.where(self.even, right, left), "core")
        pair = jnp.where(self.even, jnp.concatenate([keep, came]), jnp.concatenate([came, keep]))
        mine = self.gather_axis(pair, "z")
        mine = self.gather_axis(mine, "first")
        mine = self.gather_axis(mine, "second")
        other = self.send(mine, "core")
        left = jnp.where(self.even, mine, other)
        right = jnp.where(self.even, other, mine)
        left = left.reshape(self.ny, self.nx, self.nz, 2 * rows, half).transpose(2, 1, 0, 3, 4)
        right = right.reshape(self.nx, self.ny, self.nz, 2 * rows, half).transpose(2, 0, 1, 3, 4)
        return (left.reshape(-1, half), right.reshape(-1, half))

    def scatter(self, left, right):
        half = left.shape[1]
        rows = left.shape[0] // self.count
        places = (self.nz, self.nx, self.ny, 2 * rows, half)
        left = left.reshape(places).transpose(2, 1, 0, 3, 4)
        right = right.reshape(places).transpose(1, 2, 0, 3, 4)
        keep = jnp.where(self.even, left, right).astype(jnp.float32)
        away = jnp.where(self.even, right, left).astype(jnp.bfloat16)
        mine = (keep + self.send(away, "core").astype(jnp.float32)).astype(jnp.bfloat16)
        mine = self.scatter_axis(mine, "second")
        mine = self.scatter_axis(mine, "first")
        mine = self.scatter_axis(mine, "z")
        parts = mine.reshape(2, rows, half)
        keep = jnp.where(self.even, parts[0], parts[1])
        came = self.send(jnp.where(self.even, parts[1], parts[0]), "core")
        return jnp.where(
            self.even,
            jnp.concatenate([keep, came], axis=1),
            jnp.concatenate([came, keep], axis=1),
        ).astype(jnp.float32)

    def total(self, value):
        value = value.reshape(1, 1)
        for axis in ("core", "y", "x", "z"):
            n = {"core": 2, "y": self.ny, "x": self.nx, "z": self.nz}[axis]
            if n & (n - 1):
                value = sum([value] + [self.send(value, axis, k) for k in range(1, n)])
                continue
            bit = 1
            while bit < n:
                swap = []
                for i in range(self.count):
                    c, y = i % 2, i // 2 % self.ny
                    x, z = i // (2 * self.ny) % self.nx, i // (2 * self.ny * self.nx)
                    to = {"core": c, "y": y, "x": x, "z": z}
                    to[axis] ^= bit
                    swap.append(
                        (i, ((to["z"] * self.nx + to["x"]) * self.ny + to["y"]) * 2 + to["core"])
                    )
                value = value + lax.ppermute(value, AXES, swap)
                bit *= 2
        return value[0, 0]


def halves(*arrays):
    return jnp.concatenate(
        [a[:, : a.shape[1] // 2] for a in arrays] + [a[:, a.shape[1] // 2 :] for a in arrays],
        axis=1,
    )


def cut(pair, *widths):
    out, at = [], 0
    for width in widths:
        out.append(jnp.concatenate([p[:, at : at + width // 2] for p in pair], axis=1))
        at += width // 2
    return out


def pad_to(array, columns):
    return jnp.pad(array, ((0, 0), (0, columns - array.shape[1])))


def small_rows(gains, biases, in_bias):
    features = gains.shape[1]
    return jnp.concatenate([gains.T, biases.T, in_bias.reshape(features, -1)], axis=1)


def small_back(rows):
    return (rows[:, :2].T, rows[:, 2:8].T, rows[:, 8:].reshape(-1))


SMALL = 128


def per_device(
    tokens,
    doc_ids,
    teacher,
    seg_qkv,
    seg_out,
    seg_in,
    seg_fc2,
    seg_gains,
    seg_biases,
    seg_in_bias,
    cls_qkv,
    cls_out,
    cls_in,
    cls_fc2,
    cls_gains,
    cls_biases,
    cls_in_bias,
    seg_pos,
):
    rows_count, features = tokens.shape
    windows = rows_count // SEG
    seq_tokens = rows_count * lax.axis_size("fsdp")
    highest = lax.Precision.HIGHEST
    low = jnp.bfloat16
    grid = Grid()
    hidden = seg_in.shape[1]
    slot_count = seg_pos.shape[0]
    per_feature = 8 + hidden // features
    validity = (doc_ids >= 0).astype(jnp.float32)
    counts = jnp.sum(validity.reshape(windows, SEG), axis=1)
    own = jnp.arange(seg_qkv.shape[0], dtype=jnp.int32)[:, None] == 0
    small = jnp.concatenate(
        [
            pad_to(small_rows(seg_gains, seg_biases, seg_in_bias), SMALL),
            pad_to(
                jnp.concatenate(
                    [
                        small_rows(cls_gains, cls_biases, cls_in_bias),
                        seg_pos.T,
                        jnp.where(own, counts[None, :], 0.0),
                    ],
                    axis=1,
                ),
                SMALL,
            ),
        ],
        axis=1,
    ).astype(low)
    group = grid.gather(halves(seg_qkv.astype(low), small))
    full_qkv = cut(group, 3 * features)[0]
    small_seg, small_cls = (half[:, -SMALL:] for half in group)
    group = grid.gather(halves(seg_out.astype(low), seg_in.astype(low)))
    full_out, full_in = cut(group, features, hidden)
    full_fc2 = cut(grid.gather(seg_fc2.astype(low)), features)[0]
    seg_full = (full_qkv, full_out, full_in, full_fc2) + small_back(small_seg[:, :per_feature])
    pos_table = small_cls[:, per_feature : per_feature + slot_count].T.astype(jnp.float32)
    token_count = jnp.sum(
        small_cls[:, per_feature + slot_count : per_feature + slot_count + windows].astype(
            jnp.float32
        )
    )
    group = grid.gather(halves(cls_qkv.astype(low), cls_out.astype(low)))
    cls_full_qkv, cls_full_out = cut(group, 3 * features, features)
    cls_full_in = cut(grid.gather(cls_in.astype(low)), hidden)[0]
    cls_full_fc2 = cut(grid.gather(cls_fc2.astype(low)), features)[0]
    cls_weights = (cls_full_qkv, cls_full_out, cls_full_in, cls_full_fc2) + small_back(
        small_cls[:, :per_feature]
    )
    doc_block = doc_ids.reshape(windows, SEG)
    allowed = doc_block[:, :, None] == doc_block[:, None, :]
    seg_rows_low, seg_queries, seg_keys, seg_values = project_forward(tokens, seg_full)
    seg_mixed, seg_log_total = attend(
        to_heads(seg_queries, windows),
        to_heads(seg_keys, windows),
        to_heads(seg_values, windows),
        allowed,
    )
    seg_mixed_low = seg_mixed.reshape(rows_count, features).astype(low)
    first_out, seg_kept = finish_forward(tokens, seg_mixed_low, seg_full)
    places = lax.axis_index("fsdp") * rows_count + jnp.arange(windows, dtype=jnp.int32) * SEG
    slot_index = places % seq_tokens // SEG
    picker = (slot_index[:, None] == jnp.arange(slot_count, dtype=jnp.int32)[None, :]).astype(
        jnp.float32
    )
    shaped_out = first_out.reshape(windows, SEG, features)
    cls_rows = shaped_out[:, 0] + jnp.dot(picker, pos_table, precision=highest)
    cls_rows_low, cls_queries, cls_keys, cls_values = project_forward(cls_rows, cls_weights)
    both = lax.all_gather(
        jnp.concatenate([cls_keys, cls_values], axis=1), "fsdp", axis=0, tiled=True
    )
    all_keys, all_values = both[:, :features], both[:, features:]
    gathered_count = all_keys.shape[0]
    key_seq = jnp.arange(gathered_count, dtype=jnp.int32) * SEG // seq_tokens
    cls_allowed = ((places // seq_tokens)[:, None] == key_seq[None, :])[None]
    cls_mixed, cls_log_total = attend(
        to_heads(cls_queries, 1), to_heads(all_keys, 1), to_heads(all_values, 1), cls_allowed
    )
    cls_mixed_low = cls_mixed.reshape(windows, features).astype(low)
    cls_result, cls_kept = finish_forward(cls_rows, cls_mixed_low, cls_weights)
    output = shaped_out.at[:, 0].set(cls_result).reshape(rows_count, features)
    misfit = output - teacher
    err_part = jnp.sum(validity * jnp.sum(misfit * misfit, axis=1))
    loss = grid.total(err_part) / (features * token_count)
    scaling = 2.0 * rows_count * grid.count / token_count
    grad_output = (scaling * validity)[:, None] * misfit
    grad_shaped = grad_output.reshape(windows, SEG, features)
    cls_resid, cls_grad_mixed, cls_small, cls_factors = finish_backward(
        grad_shaped[:, 0], cls_kept, cls_mixed_low, cls_weights
    )
    cls_grad_query, key_part, value_part = attend_back(
        to_heads(cls_queries, 1),
        to_heads(all_keys, 1),
        to_heads(all_values, 1),
        cls_allowed,
        cls_log_total,
        to_heads(cls_grad_mixed, 1),
    )
    parts = jnp.concatenate(
        [
            key_part.reshape(gathered_count, features).astype(low),
            value_part.reshape(gathered_count, features).astype(low),
        ],
        axis=1,
    )
    parts = lax.all_to_all(parts, "fsdp", 0, 0, tiled=True)
    own_both = jnp.sum(
        parts.reshape(-1, windows, 2 * features).astype(jnp.float32), axis=0
    ).astype(low)
    grad_cls_rows, cls_head_bias, cls_joined = start_backward(
        cls_grad_query.reshape(windows, features).astype(low),
        own_both[:, :features],
        own_both[:, features:],
        cls_weights,
        cls_resid,
    )
    grad_pos = jnp.dot(picker.T, grad_cls_rows, precision=highest)
    grad_branch, first_low, grad_pre, activ_low, grad_second = cls_factors
    factors = lax.all_gather(
        jnp.concatenate(
            [
                cls_rows_low,
                cls_mixed_low,
                first_low,
                activ_low,
                cls_joined,
                grad_branch,
                grad_pre,
                grad_second,
            ],
            axis=1,
        ),
        AXES,
        axis=0,
        tiled=True,
    )
    cls_grads = []
    left, right = 0, 3 * features + hidden
    for width, columns in (
        (features, 3 * features),
        (features, features),
        (features, hidden),
        (hidden, features),
    ):
        share = width // grid.count
        mine = lax.dynamic_slice_in_dim(factors, left + grid.index * share, share, 1)
        cls_grads.append(
            jnp.dot(mine.T, factors[:, right : right + columns], preferred_element_type=jnp.float32)
        )
        left += width
        right += columns
    grad_first = grad_shaped.at[:, 0].set(grad_cls_rows).reshape(rows_count, features)
    seg_resid, seg_grad_mixed, seg_small, seg_factors = finish_backward(
        grad_first, seg_kept, seg_mixed_low, seg_full
    )
    grad_branch, first_low, grad_pre, activ_low, grad_second = seg_factors
    grad_fc2 = weight_grad(activ_low, grad_second)
    seg_grad_fc2 = grid.scatter(grad_fc2[:, : features // 2], grad_fc2[:, features // 2 :])
    grad_in = weight_grad(first_low, grad_pre)
    grad_out = weight_grad(seg_mixed_low, grad_branch)
    merged = halves(grad_out, grad_in)
    merged = grid.scatter(merged[:, : merged.shape[1] // 2], merged[:, merged.shape[1] // 2 :])
    seg_grad_out, seg_grad_in = cut(
        (merged[:, : merged.shape[1] // 2], merged[:, merged.shape[1] // 2 :]), features, hidden
    )
    seg_grad_query, seg_grad_keys, seg_grad_values = attend_back(
        to_heads(seg_queries, windows),
        to_heads(seg_keys, windows),
        to_heads(seg_values, windows),
        allowed,
        seg_log_total,
        to_heads(seg_grad_mixed, windows),
    )
    grad_tokens, seg_head_bias, seg_joined = start_backward(
        seg_grad_query.reshape(rows_count, features).astype(low),
        seg_grad_keys.reshape(rows_count, features).astype(low),
        seg_grad_values.reshape(rows_count, features).astype(low),
        seg_full,
        seg_resid,
    )
    grad_qkv = weight_grad(seg_rows_low, seg_joined)
    small = jnp.concatenate(
        [
            pad_to(
                small_rows(seg_small[0], jnp.concatenate([seg_head_bias, seg_small[1]]), seg_small[2]),
                SMALL,
            ),
            pad_to(
                jnp.concatenate(
                    [
                        small_rows(
                            cls_small[0], jnp.concatenate([cls_head_bias, cls_small[1]]), cls_small[2]
                        ),
                        grad_pos.T,
                    ],
                    axis=1,
                ),
                SMALL,
            ),
        ],
        axis=1,
    ).astype(low)
    merged = halves(grad_qkv, small)
    merged = grid.scatter(merged[:, : merged.shape[1] // 2], merged[:, merged.shape[1] // 2 :])
    pair = (merged[:, : merged.shape[1] // 2], merged[:, merged.shape[1] // 2 :])
    seg_grad_qkv = cut(pair, 3 * features)[0]
    small_seg, small_cls = (half[:, -SMALL:] for half in pair)
    seg_tail = small_back(small_seg[:, :per_feature])
    cls_tail = small_back(small_cls[:, :per_feature])
    grad_seg_pos = small_cls[:, per_feature : per_feature + slot_count].T
    return (
        (output, loss, grad_tokens, seg_grad_qkv, seg_grad_out, seg_grad_in, seg_grad_fc2)
        + seg_tail
        + tuple(cls_grads)
        + cls_tail
        + (grad_seg_pos,)
    )


def weight_grad(rows, grad):
    return jnp.dot(rows.T, grad, preferred_element_type=jnp.float32).astype(jnp.bfloat16)


def solution(mesh):
    return jax.shard_map(
        per_device,
        mesh=mesh,
        in_specs=(
            P(("dp", "fsdp"), None),
            P(("dp", "fsdp")),
            P(("dp", "fsdp"), None),
            P(("dp", "fsdp"), None),
            P(("dp", "fsdp"), None),
            P(("dp", "fsdp"), None),
            P(("dp", "fsdp"), None),
            P(None, ("dp", "fsdp")),
            P(None, ("dp", "fsdp")),
            P(("dp", "fsdp")),
            P(("dp", "fsdp"), None),
            P(("dp", "fsdp"), None),
            P(("dp", "fsdp"), None),
            P(("dp", "fsdp"), None),
            P(None, ("dp", "fsdp")),
            P(None, ("dp", "fsdp")),
            P(("dp", "fsdp")),
            P(None, ("dp", "fsdp")),
        ),
        out_specs=(
            P(("dp", "fsdp"), None),
            P(),
            P(("dp", "fsdp"), None),
            P(("dp", "fsdp"), None),
            P(("dp", "fsdp"), None),
            P(("dp", "fsdp"), None),
            P(("dp", "fsdp"), None),
            P(None, ("dp", "fsdp")),
            P(None, ("dp", "fsdp")),
            P(("dp", "fsdp")),
            P(("dp", "fsdp"), None),
            P(("dp", "fsdp"), None),
            P(("dp", "fsdp"), None),
            P(("dp", "fsdp"), None),
            P(None, ("dp", "fsdp")),
            P(None, ("dp", "fsdp")),
            P(("dp", "fsdp")),
            P(None, ("dp", "fsdp")),
        ),
        check_vma=False,
    )
```

time: 1650 us -> 601 us (0.36)
  waiting for transfers between devices: 1090 us -> 163 us
  blocking collectives: 338 us -> 5.63 us
  starting transfers between devices: 1.13 us -> 107 us
  other arithmetic: 28.8 us -> 103 us
  local copies, waits for them, and re-layouts: 45.2 us -> 99.8 us
  matrix products: 130 us -> 90.7 us
    reduce_scatter x7 -> x0, waiting for transfers between devices: 773 us -> none  [the longest x1 142 us: per_device(): lax.psum_scatter(seg_mats[2], ('dp', 'fsdp'), scatter_dimension=0, tiled=...]
    all_gather x7 -> x1, blocking collectives: 202 us -> 5.63 us  [per_device(): lax.all_gather(jnp.concatenate([cls_keys, cls_values], axis=1), 'fsdp', a...]
    all_gather x8 -> x1, waiting for transfers between devices: 188 us -> 0.01 us  [per_device(): lax.all_gather(jnp.concatenate([cls_rows_low, cls_mixed_low, first_low, a...]
    ppermute x0 -> x68, waiting for transfers between devices: none -> 163 us  [the longest x63 161 us: send(): return lax.ppermute(value, AXES, self.pairs(axis, step))]
    unnamed x17 -> x1, waiting for transfers between devices: 125 us -> 0.02 us
    ppermute x0 -> x68, starting transfers between devices: none -> 104 us  [the longest x63 87.3 us: send(): return lax.ppermute(value, AXES, self.pairs(axis, step))]
    psum x2 -> x0, blocking collectives: 82 us -> none  [per_device(): lax.psum((err_part, jnp.sum(validity)), ('dp', 'fsdp'))]
    unnamed x2 -> x0, blocking collectives: 54 us -> none
  transfers between devices with their start and end apart: 16 -> 70, of which waited for: 11 -> 28; matrix products, arithmetic and copies ran while one was open for 8% -> 26% of each run, Pallas kernels for 0% -> 0%
where the time goes in v1:
time: 601 us; the launch traced here: 592 us
  waiting for transfers between devices  163 us (27%)
  starting transfers between devices  107 us (18%)
  other arithmetic  103 us (17%)
  local copies, waits for them, and re-layouts  99.8 us (17%)
  matrix products  90.7 us (15%)
  between operations  23.6 us (4%)
    ppermute x63, waiting for transfers between devices, send(): return lax.ppermute(value, AXES, self.pairs(axis, step))  161 us
    ppermute x63, starting transfers between devices, send(): return lax.ppermute(value, AXES, self.pairs(axis, step))  87.3 us
    unnamed x261, local copies, waits for them, and re-layouts  31.7 us
    select_n x12, other arithmetic, gather_axis(): jnp.where(place == 0, jnp.concatenate(parts), jnp.concatenate([parts[1],...  27.3 us
    dot_general x2, matrix products, finish_forward(): jnp.dot(first_low, weights[2], preferred_element_type=jnp.float32)  22.9 us
    ppermute x5, starting transfers between devices, total(): value = value + lax.ppermute(value, AXES, swap)  16.6 us
    select_n x5, other arithmetic, gather(): left = jnp.where(self.even, mine, other)  16.3 us
    dot_general x4, matrix products, weight_grad(): jnp.dot(rows.T, grad, preferred_element_type=jnp.float32)  13.1 us
  transfers between devices with their start and end apart: 70, of which 28 were waited for; matrix products, arithmetic and copies ran while one was open for 26% of the time, Pallas kernels for 0%

profile of v1, /device:TPU:0, one launch (start us, length us, event | category | flops | bytes accessed | tf_op | source)
XLA Modules:
  0.0 592.3 jit_solution(9761429585347771008)
XLA Ops:
  33.3 4.3 collective-permute-start.36
  37.6 7.1 %collective-permute-start.31 = (bf16[48,1536]{1,0:T(8,128)(2,1)S(1)}, bf16[48,1536]{1,0:T(8,128)(2,1)S(1)}, u32[]{:S(2)}, u32[]{:S(2)}) collective-permute-start(bf16[48,1536]{1,0:T(8,128)(2,1)S(1)} %get-tuple-element.193), channel_id=1, source_target_pairs={{0,8},{1,9},{2,10},{3,11},{4,12},{5,13},{6,14},{7,15},{8,16},{9,17... | collective-permute-start | bytes 442376 | tf_op jit(solution)/shard_map/ppermute | solution.py:184
  46.7 10.0 %collective-permute-done.29 = bf16[48,1536]{1,0:T(8,128)(2,1)S(1)} collective-permute-done((bf16[48,1536]{1,0:T(8,128)(2,1)S(1)}, bf16[48,1536]{1,0:T(8,128)(2,1)S(1)}, u32[]{:S(2)}, u32[]{:S(2)}) %collective-permute-start.29) | collective-permute-done | bytes 147488 | tf_op jit(solution)/shard_map/ppermute | solution.py:184
  56.6 9.4 %collective-permute-done.30 = bf16[48,1536]{1,0:T(8,128)(2,1)S(1)} collective-permute-done((bf16[48,1536]{1,0:T(8,128)(2,1)S(1)}, bf16[48,1536]{1,0:T(8,128)(2,1)S(1)}, u32[]{:S(2)}, u32[]{:S(2)}) %collective-permute-start.30) | collective-permute-done | bytes 147488 | tf_op jit(solution)/shard_map/ppermute | solution.py:184
  72.4 5.3 collective-permute-done.15
  81.0 9.2 %collective-permute-start.10 = (bf16[48,1920]{1,0:T(8,128)(2,1)S(1)}, bf16[48,1920]{1,0:T(8,128)(2,1)S(1)}, u32[]{:S(2)}, u32[]{:S(2)}) collective-permute-start(bf16[48,1920]{1,0:T(8,128)(2,1)S(1)} %get-tuple-element.207), channel_id=1, source_target_pairs={{0,8},{1,9},{2,10},{3,11},{4,12},{5,13},{6,14},{7,15},{8,16},{9,17... | collective-permute-start | bytes 552968 | tf_op jit(solution)/shard_map/ppermute | solution.py:184
  91.8 6.9 %collective-permute-done.22 = bf16[48,1536]{1,0:T(8,128)(2,1)S(1)} collective-permute-done((bf16[48,1536]{1,0:T(8,128)(2,1)S(1)}, bf16[48,1536]{1,0:T(8,128)(2,1)S(1)}, u32[]{:S(2)}, u32[]{:S(2)}) %collective-permute-start.22) | collective-permute-done | bytes 147488 | tf_op jit(solution)/shard_map/ppermute | solution.py:184
  103.1 7.5 %collective-permute-done.8 = bf16[48,1920]{1,0:T(8,128)(2,1)S(1)} collective-permute-done((bf16[48,1920]{1,0:T(8,128)(2,1)S(1)}, bf16[48,1920]{1,0:T(8,128)(2,1)S(1)}, u32[]{:S(2)}, u32[]{:S(2)}) %collective-permute-start.8) | collective-permute-done | bytes 184352 | tf_op jit(solution)/shard_map/ppermute | solution.py:184
  117.7 27.5 %collective-permute-done.25 = bf16[192,1536]{1,0:T(8,128)(2,1)S(1)} collective-permute-done((bf16[192,1536]{1,0:T(8,128)(2,1)S(1)}, bf16[192,1536]{1,0:T(8,128)(2,1)S(1)}, u32[]{:S(2)}, u32[]{:S(2)}) %collective-permute-start.25) | collective-permute-done | bytes 589856 | tf_op jit(solution)/shard_map/ppermute | solution.py:184
  153.1 7.8 %collective-permute-done.11 = bf16[192,1920]{1,0:T(8,128)(2,1)S(1)} collective-permute-done((bf16[192,1920]{1,0:T(8,128)(2,1)S(1)}, bf16[192,1920]{1,0:T(8,128)(2,1)S(1)}, u32[]{:S(2)}, u32[]{:S(2)}) %collective-permute-start.11) | collective-permute-done | bytes 737312 | tf_op jit(solution)/shard_map/ppermute | solution.py:184
  167.6 4.4 maximum_select_fusion.4
  172.0 29.2 %collective-permute-done.33 = bf16[384,1536]{1,0:T(8,128)(2,1)} collective-permute-done((bf16[384,1536]{1,0:T(8,128)(2,1)}, bf16[384,1536]{1,0:T(8,128)(2,1)}, u32[]{:S(2)}, u32[]{:S(2)}) %collective-permute-start.33) | collective-permute-done | bytes 1179680 | tf_op jit(solution)/shard_map/ppermute | solution.py:184
  208.1 4.5 maximum_select_fusion.1
  219.4 4.4 maximum_select_fusion
  288.4 4.7 broadcast_select_fusion.1
  297.9 19.5 %multiply_convert_fusion = (bf16[512,3072]{1,0:T(8,128)(2,1)S(1)}, f32[512,3072]{1,0:T(8,128)}, f32[512,3072]{1,0:T(8,128)}) fusion(f32[3072]{0:T(1024)S(1)} %copy-done.81, bf16[768,1536]{1,0:T(8,128)(2,1)S(1)} %slice.509, bf16[768,1536]{1,0:T(8,128)(2,1)S(1)} %slice.508, f32[512,768]{1,0:T(8,128)S(1)} %get-tuple-element.292, f32[768]{0:T(1024)S(1)} %copy-done.88, ...), kind=kOutput, calls=%fused_computation.3 | convolution fusion | flops 2531131392 | bytes 22042624 | tf_op jit(solution)/shard_map/dot_general | solution.py:89
  324.6 5.6 all-gather
  368.8 5.2 collective-permute-start.45
  374.9 4.8 collective-permute-start.46
  391.1 7.9 %fusion.184 = (bf16[3072]{0:T(1024)(128)(2,1)S(1)}, bf16[512,3072]{1,0:T(8,128)(2,1)S(1)}) fusion(f32[512,3072]{1,0:T(8,128)} %get-tuple-element.201, bf16[512,768]{1,0:T(8,128)(2,1)S(1)} %get-tuple-element.177, bf16[3072,384]{1,0:T(8,128)(2,1)S(1)} %bitcast.344, bf16[3072,384]{1,0:T(8,128)(2,1)S(1)} %bitcast.342, f32[512,3072]{1,0:T(8,128)} %get-tuple-element.293, ...), kind=kOutput, calls=%fused_computation.513 | convolution fusion | flops 2450519040 | bytes 21252096 | tf_op jit(solution)/shard_map/dot_general | solution.py:103
  402.3 4.9 convolution_convert_fusion.1
  413.4 4.4 convolution_convert_fusion
  437.2 4.3 fusion.164
  460.5 4.2 copy.381
  478.7 5.4 add_add_fusion.4
  485.5 9.2 %collective-permute-done.48 = bf16[2,4,48,1280]{3,2,1,0:T(8,128)(2,1)S(1)} collective-permute-done((bf16[2,4,48,1280]{3,2,1,0:T(8,128)(2,1)S(1)}, bf16[2,4,48,1280]{3,2,1,0:T(8,128)(2,1)S(1)}, u32[]{:S(2)}, u32[]{:S(2)}) %collective-permute-start.48) | collective-permute-done | bytes 983072 | tf_op jit(solution)/shard_map/ppermute | solution.py:184
  499.3 9.8 %collective-permute-done.49 = bf16[4,48,1280]{2,1,0:T(8,128)(2,1)S(1)} collective-permute-done((bf16[4,48,1280]{2,1,0:T(8,128)(2,1)S(1)}, bf16[4,48,1280]{2,1,0:T(8,128)(2,1)S(1)}, u32[]{:S(2)}, u32[]{:S(2)}) %collective-permute-start.49) | collective-permute-done | bytes 491552 | tf_op jit(solution)/shard_map/ppermute | solution.py:184
  517.7 5.9 collective-permute-done.51
  548.3 6.0 %collective-permute-done.65 = bf16[192,384]{1,0:T(8,128)(2,1)S(1)} collective-permute-done((bf16[192,384]{1,0:T(8,128)(2,1)}, bf16[192,384]{1,0:T(8,128)(2,1)S(1)}, u32[]{:S(2)}, u32[]{:S(2)}) %collective-permute-start.65) | collective-permute-done | bytes 147488 | tf_op jit(solution)/shard_map/ppermute | solution.py:184
  558.6 5.4 collective-permute-done.57
  564.1 8.3 %collective-permute-done.58 = bf16[48,1920]{1,0:T(8,128)(2,1)S(1)} collective-permute-done((bf16[48,1920]{1,0:T(8,128)(2,1)S(1)}, bf16[48,1920]{1,0:T(8,128)(2,1)S(1)}, u32[]{:S(2)}, u32[]{:S(2)}) %collective-permute-start.58) | collective-permute-done | bytes 184352 | tf_op jit(solution)/shard_map/ppermute | solution.py:184
  575.4 4.5 reshape.745
  (679 shorter events, 311.2 us)
Async XLA Ops:
  21.1 23.6 %collective-permute-start.3 = (bf16[48,1280]{1,0:T(8,128)(2,1)S(1)}, bf16[48,1280]{1,0:T(8,128)(2,1)S(1)}, u32[]{:S(2)}, u32[]{:S(2)}) collective-permute-start(bf16[48,1280]{1,0:T(8,128)(2,1)S(1)} %get-tuple-element.203), channel_id=1, source_target_pairs={{0,8},{1,9},{2,10},{3,11},{4,12},{5,13},{6,14},{7,15},{8,16},{9,17... | collective-permute-start | bytes 368648 | tf_op jit(solution)/shard_map/ppermute | solution.py:184
  28.3 42.5 %collective-permute-start.38 = (bf16[192,384]{1,0:T(8,128)(2,1)S(1)}, bf16[192,384]{1,0:T(8,128)(2,1)S(1)}, u32[]{:S(2)}, u32[]{:S(2)}) collective-permute-start(bf16[192,384]{1,0:T(8,128)(2,1)S(1)} %get-tuple-element.197), channel_id=1, source_target_pairs={{0,8},{1,9},{2,10},{3,11},{4,12},{5,13},{6,14},{7,15},{8,16},{9,17... | collective-permute-start | bytes 442376 | tf_op jit(solution)/shard_map/ppermute | solution.py:184
  29.1 41.0 %collective-permute-start.37 = (bf16[192,384]{1,0:T(8,128)(2,1)S(1)}, bf16[192,384]{1,0:T(8,128)(2,1)S(1)}, u32[]{:S(2)}, u32[]{:S(2)}) collective-permute-start(bf16[192,384]{1,0:T(8,128)(2,1)S(1)} %get-tuple-element.197), channel_id=1, source_target_pairs={{0,16},{1,17},{2,18},{3,19},{4,20},{5,21},{6,22},{7,23},{8,24},{9,... | collective-permute-start | bytes 442376 | tf_op jit(solution)/shard_map/ppermute | solution.py:184
  33.3 33.8 %collective-permute-start.36 = (bf16[192,384]{1,0:T(8,128)(2,1)S(1)}, bf16[192,384]{1,0:T(8,128)(2,1)S(1)}, u32[]{:S(2)}, u32[]{:S(2)}) collective-permute-start(bf16[192,384]{1,0:T(8,128)(2,1)S(1)} %get-tuple-element.197), channel_id=1, source_target_pairs={{0,24},{1,25},{2,26},{3,27},{4,28},{5,29},{6,30},{7,31},{8,0},{9,1... | collective-permute-start | bytes 442376 | tf_op jit(solution)/shard_map/ppermute | solution.py:184
  37.6 28.4 %collective-permute-start.31 = (bf16[48,1536]{1,0:T(8,128)(2,1)S(1)}, bf16[48,1536]{1,0:T(8,128)(2,1)S(1)}, u32[]{:S(2)}, u32[]{:S(2)}) collective-permute-start(bf16[48,1536]{1,0:T(8,128)(2,1)S(1)} %get-tuple-element.193), channel_id=1, source_target_pairs={{0,8},{1,9},{2,10},{3,11},{4,12},{5,13},{6,14},{7,15},{8,16},{9,17... | collective-permute-start | bytes 442376 | tf_op jit(solution)/shard_map/ppermute | solution.py:184
  66.0 24.2 %collective-permute-start.17 = (bf16[192,384]{1,0:T(8,128)(2,1)S(1)}, bf16[192,384]{1,0:T(8,128)(2,1)S(1)}, u32[]{:S(2)}, u32[]{:S(2)}) collective-permute-start(bf16[192,384]{1,0:T(8,128)(2,1)S(1)} %get-tuple-element.199), channel_id=1, source_target_pairs={{0,8},{1,9},{2,10},{3,11},{4,12},{5,13},{6,14},{7,15},{8,16},{9,17... | collective-permute-start | bytes 442376 | tf_op jit(solution)/shard_map/ppermute | solution.py:184
  70.2 32.1 %collective-permute-start.24 = (bf16[48,1536]{1,0:T(8,128)(2,1)S(1)}, bf16[48,1536]{1,0:T(8,128)(2,1)S(1)}, u32[]{:S(2)}, u32[]{:S(2)}) collective-permute-start(bf16[48,1536]{1,0:T(8,128)(2,1)S(1)} %get-tuple-element.195), channel_id=1, source_target_pairs={{0,8},{1,9},{2,10},{3,11},{4,12},{5,13},{6,14},{7,15},{8,16},{9,17... | collective-permute-start | bytes 442376 | tf_op jit(solution)/shard_map/ppermute | solution.py:184
  70.8 29.8 %collective-permute-start.23 = (bf16[48,1536]{1,0:T(8,128)(2,1)S(1)}, bf16[48,1536]{1,0:T(8,128)(2,1)S(1)}, u32[]{:S(2)}, u32[]{:S(2)}) collective-permute-start(bf16[48,1536]{1,0:T(8,128)(2,1)S(1)} %get-tuple-element.195), channel_id=1, source_target_pairs={{0,16},{1,17},{2,18},{3,19},{4,20},{5,21},{6,22},{7,23},{8,24},{9,... | collective-permute-start | bytes 442376 | tf_op jit(solution)/shard_map/ppermute | solution.py:184
  77.7 21.0 %collective-permute-start.22 = (bf16[48,1536]{1,0:T(8,128)(2,1)S(1)}, bf16[48,1536]{1,0:T(8,128)(2,1)S(1)}, u32[]{:S(2)}, u32[]{:S(2)}) collective-permute-start(bf16[48,1536]{1,0:T(8,128)(2,1)S(1)} %get-tuple-element.195), channel_id=1, source_target_pairs={{0,24},{1,25},{2,26},{3,27},{4,28},{5,29},{6,30},{7,31},{8,0},{9,1... | collective-permute-start | bytes 442376 | tf_op jit(solution)/shard_map/ppermute | solution.py:184
  81.0 31.8 %collective-permute-start.10 = (bf16[48,1920]{1,0:T(8,128)(2,1)S(1)}, bf16[48,1920]{1,0:T(8,128)(2,1)S(1)}, u32[]{:S(2)}, u32[]{:S(2)}) collective-permute-start(bf16[48,1920]{1,0:T(8,128)(2,1)S(1)} %get-tuple-element.207), channel_id=1, source_target_pairs={{0,8},{1,9},{2,10},{3,11},{4,12},{5,13},{6,14},{7,15},{8,16},{9,17... | collective-permute-start | bytes 552968 | tf_op jit(solution)/shard_map/ppermute | solution.py:184
  90.2 22.0 %collective-permute-start.9 = (bf16[48,1920]{1,0:T(8,128)(2,1)S(1)}, bf16[48,1920]{1,0:T(8,128)(2,1)S(1)}, u32[]{:S(2)}, u32[]{:S(2)}) collective-permute-start(bf16[48,1920]{1,0:T(8,128)(2,1)S(1)} %get-tuple-element.207), channel_id=1, source_target_pairs={{0,16},{1,17},{2,18},{3,19},{4,20},{5,21},{6,22},{7,23},{8,24},{9,... | collective-permute-start | bytes 552968 | tf_op jit(solution)/shard_map/ppermute | solution.py:184
  110.7 39.5 %collective-permute-start.32 = (bf16[192,1536]{1,0:T(8,128)(2,1)S(1)}, bf16[192,1536]{1,0:T(8,128)(2,1)S(1)}, u32[]{:S(2)}, u32[]{:S(2)}) collective-permute-start(bf16[192,1536]{1,0:T(8,128)(2,1)S(1)} %constant_dynamic-slice_fusion.1), channel_id=1, source_target_pairs={{0,4},{1,3},{2,6},{3,1},{4,0},{5,7},{6,2},{7,5},{8,12},{9,11},{10,... | collective-permute-start | bytes 1769480 | tf_op jit(solution)/shard_map/ppermute | solution.py:184
  112.2 36.0 %collective-permute-start.18 = (bf16[768,384]{1,0:T(8,128)(2,1)S(1)}, bf16[768,384]{1,0:T(8,128)(2,1)S(1)}, u32[]{:S(2)}, u32[]{:S(2)}) collective-permute-start(bf16[768,384]{1,0:T(8,128)(2,1)S(1)} %constant_dynamic-slice_fusion.3), channel_id=1, source_target_pairs={{0,4},{1,3},{2,6},{3,1},{4,0},{5,7},{6,2},{7,5},{8,12},{9,11},{10,... | collective-permute-start | bytes 1769480 | tf_op jit(solution)/shard_map/ppermute | solution.py:184
  112.8 32.4 %collective-permute-start.25 = (bf16[192,1536]{1,0:T(8,128)(2,1)S(1)}, bf16[192,1536]{1,0:T(8,128)(2,1)S(1)}, u32[]{:S(2)}, u32[]{:S(2)}) collective-permute-start(bf16[192,1536]{1,0:T(8,128)(2,1)S(1)} %constant_dynamic-slice_fusion.2), channel_id=1, source_target_pairs={{0,4},{1,3},{2,6},{3,1},{4,0},{5,7},{6,2},{7,5},{8,12},{9,11},{10,... | collective-permute-start | bytes 1769480 | tf_op jit(solution)/shard_map/ppermute | solution.py:184
  114.5 46.4 %collective-permute-start.11 = (bf16[192,1920]{1,0:T(8,128)(2,1)S(1)}, bf16[192,1920]{1,0:T(8,128)(2,1)S(1)}, u32[]{:S(2)}, u32[]{:S(2)}) collective-permute-start(bf16[192,1920]{1,0:T(8,128)(2,1)S(1)} %constant_dynamic-slice_fusion.4), channel_id=1, source_target_pairs={{0,4},{1,3},{2,6},{3,1},{4,0},{5,7},{6,2},{7,5},{8,12},{9,11},{10,... | collective-permute-start | bytes 2211848 | tf_op jit(solution)/shard_map/ppermute | solution.py:184
  115.8 47.1 %collective-permute-start.5 = (bf16[384,1280]{1,0:T(8,128)(2,1)S(1)}, bf16[384,1280]{1,0:T(8,128)(2,1)S(1)}, u32[]{:S(2)}, u32[]{:S(2)}) collective-permute-start(bf16[384,1280]{1,0:T(8,128)(2,1)S(1)} %maximum_select_fusion.11), channel_id=1, source_target_pairs={{0,2},{1,5},{2,0},{3,7},{4,6},{5,1},{6,4},{7,3},{8,10},{9,13},{10,... | collective-permute-start | bytes 2949128 | tf_op jit(solution)/shard_map/ppermute | solution.py:184
  148.2 64.4 %collective-permute-start.26 = (bf16[384,1536]{1,0:T(8,128)(2,1)}, bf16[384,1536]{1,0:T(8,128)(2,1)}, u32[]{:S(2)}, u32[]{:S(2)}) collective-permute-start(bf16[384,1536]{1,0:T(8,128)(2,1)} %maximum_select_fusion.8), channel_id=1, source_target_pairs={{0,2},{1,5},{2,0},{3,7},{4,6},{5,1},{6,4},{7,3},{8,10},{9,13},{10,... | collective-permute-start | bytes 3538952 | tf_op jit(solution)/shard_map/ppermute | solution.py:184
  150.2 57.9 %collective-permute-start.19 = (bf16[1536,384]{1,0:T(8,128)(2,1)}, bf16[1536,384]{1,0:T(8,128)(2,1)}, u32[]{:S(2)}, u32[]{:S(2)}) collective-permute-start(bf16[1536,384]{1,0:T(8,128)(2,1)} %maximum_select_fusion.7), channel_id=1, source_target_pairs={{0,2},{1,5},{2,0},{3,7},{4,6},{5,1},{6,4},{7,3},{8,10},{9,13},{10,... | collective-permute-start | bytes 3538952 | tf_op jit(solution)/shard_map/ppermute | solution.py:184
  160.9 40.3 %collective-permute-start.33 = (bf16[384,1536]{1,0:T(8,128)(2,1)}, bf16[384,1536]{1,0:T(8,128)(2,1)}, u32[]{:S(2)}, u32[]{:S(2)}) collective-permute-start(bf16[384,1536]{1,0:T(8,128)(2,1)} %maximum_select_fusion.9), channel_id=1, source_target_pairs={{0,2},{1,5},{2,0},{3,7},{4,6},{5,1},{6,4},{7,3},{8,10},{9,13},{10,... | collective-permute-start | bytes 3538952 | tf_op jit(solution)/shard_map/ppermute | solution.py:184
  162.9 54.1 %collective-permute-start.12 = (bf16[384,1920]{1,0:T(8,128)(2,1)S(1)}, bf16[384,1920]{1,0:T(8,128)(2,1)}, u32[]{:S(2)}, u32[]{:S(2)}) collective-permute-start(bf16[384,1920]{1,0:T(8,128)(2,1)S(1)} %maximum_select_fusion.6), channel_id=1, source_target_pairs={{0,2},{1,5},{2,0},{3,7},{4,6},{5,1},{6,4},{7,3},{8,10},{9,13},{10,... | collective-permute-start | bytes 4423688 | tf_op jit(solution)/shard_map/ppermute | solution.py:184
  165.2 58.6 %collective-permute-start.6 = (bf16[768,1280]{1,0:T(8,128)(2,1)S(1)}, bf16[768,1280]{1,0:T(8,128)(2,1)}, u32[]{:S(2)}, u32[]{:S(2)}) collective-permute-start(bf16[768,1280]{1,0:T(8,128)(2,1)S(1)} %maximum_select_fusion.5), channel_id=1, source_target_pairs={{0,1},{1,0},{2,3},{3,2},{4,5},{5,4},{6,7},{7,6},{8,9},{9,8},{10,11... | collective-permute-start | bytes 5898248 | tf_op jit(solution)/shard_map/ppermute | solution.py:184
  201.2 71.2 %collective-permute-start.41 = (bf16[3072,384]{1,0:T(8,128)(2,1)}, bf16[3072,384]{1,0:T(8,128)(2,1)}, u32[]{:S(2)}, u32[]{:S(2)}) collective-permute-start(bf16[3072,384]{1,0:T(8,128)(2,1)} %maximum_select_fusion.4), channel_id=1, source_target_pairs={{0,1},{1,0},{2,3},{3,2},{4,5},{5,4},{6,7},{7,6},{8,9},{9,8},{10,11... | collective-permute-start | bytes 7077896 | tf_op jit(solution)/shard_map/ppermute | solution.py:184
  208.1 71.1 %collective-permute-start.34 = (bf16[768,1536]{1,0:T(8,128)(2,1)}, bf16[768,1536]{1,0:T(8,128)(2,1)}, u32[]{:S(2)}, u32[]{:S(2)}) collective-permute-start(bf16[768,1536]{1,0:T(8,128)(2,1)} %maximum_select_fusion.3), channel_id=1, source_target_pairs={{0,1},{1,0},{2,3},{3,2},{4,5},{5,4},{6,7},{7,6},{8,9},{9,8},{10,11... | collective-permute-start | bytes 7077896 | tf_op jit(solution)/shard_map/ppermute | solution.py:184
  212.6 72.5 %collective-permute-start.20 = (bf16[3072,384]{1,0:T(8,128)(2,1)}, bf16[3072,384]{1,0:T(8,128)(2,1)}, u32[]{:S(2)}, u32[]{:S(2)}) collective-permute-start(bf16[3072,384]{1,0:T(8,128)(2,1)} %maximum_select_fusion.1), channel_id=1, source_target_pairs={{0,1},{1,0},{2,3},{3,2},{4,5},{5,4},{6,7},{7,6},{8,9},{9,8},{10,11... | collective-permute-start | bytes 7077896 | tf_op jit(solution)/shard_map/ppermute | solution.py:184
  217.0 50.0 %collective-permute-start.27 = (bf16[768,1536]{1,0:T(8,128)(2,1)}, bf16[768,1536]{1,0:T(8,128)(2,1)}, u32[]{:S(2)}, u32[]{:S(2)}) collective-permute-start(bf16[768,1536]{1,0:T(8,128)(2,1)} %maximum_select_fusion.2), channel_id=1, source_target_pairs={{0,1},{1,0},{2,3},{3,2},{4,5},{5,4},{6,7},{7,6},{8,9},{9,8},{10,11... | collective-permute-start | bytes 7077896 | tf_op jit(solution)/shard_map/ppermute | solution.py:184
  223.8 64.6 %collective-permute-start.13 = (bf16[768,1920]{1,0:T(8,128)(2,1)}, bf16[768,1920]{1,0:T(8,128)(2,1)}, u32[]{:S(2)}, u32[]{:S(2)}) collective-permute-start(bf16[768,1920]{1,0:T(8,128)(2,1)} %maximum_select_fusion), channel_id=1, source_target_pairs={{0,1},{1,0},{2,3},{3,2},{4,5},{5,4},{6,7},{7,6},{8,9},{9,8},{10,11... | collective-permute-start | bytes 8847368 | tf_op jit(solution)/shard_map/ppermute | solution.py:184
  354.1 26.6 %all-to-all-start = ((bf16[4,4,1536]{2,1,0:T(4,128)(2,1)}), bf16[4,4,1536]{2,1,0:T(4,128)(2,1)S(1)}, u32[]{:S(2)}, u32[]{:S(2)}) async-start(bf16[4,4,1536]{2,1,0:T(4,128)(2,1)} %pad_maximum_fusion.51), calls=%async_computation | async-start | bytes 98304 | tf_op jit(solution)/shard_map/all_to_all | solution.py:423
  357.3 218.1 %all-gather.4.cloned.1.call-start = ((), (), s32[]{:S(2)}) async-start(), calls=%async_computation.1 | async-start | bytes 3244032 | tf_op jit(solution)/shard_map/all_gather | solution.py:436
  472.5 23.9 %collective-permute-start.54 = (bf16[2,2,4,48,1920]{4,3,2,1,0:T(8,128)(2,1)S(1)}, bf16[2,2,4,48,1920]{4,3,2,1,0:T(8,128)(2,1)S(1)}, u32[]{:S(2)}, u32[]{:S(2)}) collective-permute-start(bf16[2,2,4,48,1920]{4,3,2,1,0:T(8,128)(2,1)S(1)} %bitcast_select_fusion), channel_id=1, source_target_pairs={{0,1},{1,0},{2,3},{3,2},{4,5},{5,4},{6,7},{7,6},{8,9},{9,8},{10,11... | collective-permute-start | bytes 8847368 | tf_op jit(solution)/shard_map/ppermute | solution.py:184
  485.3 28.5 %collective-permute-start.62 = (bf16[2,4,192,384]{3,2,1,0:T(8,128)(2,1)S(1)}, bf16[2,4,192,384]{3,2,1,0:T(8,128)(2,1)S(1)}, u32[]{:S(2)}, u32[]{:S(2)}) collective-permute-start(bf16[2,4,192,384]{3,2,1,0:T(8,128)(2,1)S(1)} %dynamic-slice_bitcast_fusion.1), channel_id=1, source_target_pairs={{0,2},{1,5},{2,0},{3,7},{4,6},{5,1},{6,4},{7,3},{8,10},{9,13},{10,... | collective-permute-start | bytes 3538952 | tf_op jit(solution)/shard_map/ppermute | solution.py:184
  498.8 30.4 %collective-permute-start.55 = (bf16[2,4,48,1920]{3,2,1,0:T(8,128)(2,1)}, bf16[2,4,48,1920]{3,2,1,0:T(8,128)(2,1)}, u32[]{:S(2)}, u32[]{:S(2)}) collective-permute-start(bf16[2,4,48,1920]{3,2,1,0:T(8,128)(2,1)} %dynamic-slice_bitcast_fusion), channel_id=1, source_target_pairs={{0,2},{1,5},{2,0},{3,7},{4,6},{5,1},{6,4},{7,3},{8,10},{9,13},{10,... | collective-permute-start | bytes 4423688 | tf_op jit(solution)/shard_map/ppermute | solution.py:184
  533.0 21.3 %collective-permute-start.56 = (bf16[4,48,1920]{2,1,0:T(8,128)(2,1)}, bf16[4,48,1920]{2,1,0:T(8,128)(2,1)S(1)}, u32[]{:S(2)}, u32[]{:S(2)}) collective-permute-start(bf16[4,48,1920]{2,1,0:T(8,128)(2,1)} %dynamic-slice_bitcast_fusion.3), channel_id=1, source_target_pairs={{0,4},{1,3},{2,6},{3,1},{4,0},{5,7},{6,2},{7,5},{8,12},{9,11},{10,... | collective-permute-start | bytes 2211848 | tf_op jit(solution)/shard_map/ppermute | solution.py:184
  (146 other events, 1269.6 us)
Sparse Core Ops, SparseCore 0:
  433.0 61.9 all-gather.3

commit v2 on v1

v2 whole, which is shorter than its diff:
```python
import jax
import jax.numpy as jnp
from jax import lax
from jax.experimental import pallas as pl
from jax.experimental.pallas import tpu as pltpu
from jax.sharding import PartitionSpec as P

HEAD = 64
SEG = 128
SMALL = 128

AXES = ("dp", "fsdp")


class Grid:
    def __init__(self, features):
        fsdp, dp = lax.axis_size("fsdp"), lax.axis_size("dp")
        self.ny = fsdp // 2
        self.nx = self.ny
        self.nz = dp // self.nx
        self.count = fsdp * dp
        me = lax.axis_index("dp")
        chip = lax.axis_index("fsdp")
        self.z, self.x = me // self.nx, me % self.nx
        self.y, self.core = chip // 2, chip % 2
        self.even = self.core == 0
        self.index = me * fsdp + chip
        self.pieces = self.nx == 2 and 2 * features // self.count % 16 == 0
        self.first = jnp.where(self.even, self.x, self.y)
        self.second = jnp.where(self.even, self.y, self.x)

    def pairs(self, axis, step):
        out = []
        for i in range(self.count):
            c, y = i % 2, i // 2 % self.ny
            x, z = i // (2 * self.ny) % self.nx, i // (2 * self.ny * self.nx)
            along = axis
            if axis == "first":
                along = "x" if c == 0 else "y"
            if axis == "second":
                along = "y" if c == 0 else "x"
            if along == "core":
                c = (c + step) % 2
            if along == "y":
                y = (y + step) % self.ny
            if along == "x":
                x = (x + step) % self.nx
            if along == "z":
                z = (z + step) % self.nz
            out.append((i, ((z * self.nx + x) * self.ny + y) * 2 + c))
        return out

    def size(self, axis):
        return {"core": 2, "z": self.nz}.get(axis, self.nx)

    def place(self, axis):
        return {"core": self.core, "z": self.z, "first": self.first, "second": self.second}[axis]

    def send(self, value, axis, step=1):
        return lax.ppermute(value, AXES, self.pairs(axis, step))

    def gather_axis(self, rows, axis):
        n, place = self.size(axis), self.place(axis)
        parts = [rows] + [self.send(rows, axis, n - k) for k in range(1, n)]
        if n == 1:
            return rows
        if n == 2:
            return jnp.where(
                place == 0, jnp.concatenate(parts), jnp.concatenate([parts[1], parts[0]])
            )
        ring = jnp.concatenate(parts + parts[:-1])
        step = rows.shape[0]
        return lax.dynamic_slice_in_dim(ring, (n - place) % n * step, n * step, 0)

    def scatter_axis(self, blocks, axis):
        n, place = self.size(axis), self.place(axis)
        total = lax.dynamic_index_in_dim(blocks, place, 0, keepdims=False).astype(jnp.float32)
        for k in range(1, n):
            block = lax.dynamic_index_in_dim(blocks, (place + k) % n, 0, keepdims=False)
            total = total + self.send(block, axis, k).astype(jnp.float32)
        return total.astype(jnp.bfloat16)

    def gather(self, shard):
        rows, half = shard.shape[0], shard.shape[1] // 2
        left, right = shard[:, :half], shard[:, half:]
        keep = jnp.where(self.even, left, right)
        came = self.send(jnp.where(self.even, right, left), "core")
        pair = jnp.where(self.even, jnp.concatenate([keep, came]), jnp.concatenate([came, keep]))
        mine = self.gather_axis(pair, "z")
        mine = self.gather_axis(mine, "first")
        mine = self.gather_axis(mine, "second")
        other = self.send(mine, "core")
        left = jnp.where(self.even, mine, other)
        right = jnp.where(self.even, other, mine)
        left = left.reshape(self.ny, self.nx, self.nz, 2 * rows, half).transpose(2, 1, 0, 3, 4)
        right = right.reshape(self.nx, self.ny, self.nz, 2 * rows, half).transpose(2, 0, 1, 3, 4)
        return (left.reshape(-1, half), right.reshape(-1, half))

    def pair(self, shard):
        half = shard.shape[1] // 2
        left, right = shard[:, :half], shard[:, half:]
        keep = jnp.where(self.even, left, right)
        came = self.send(jnp.where(self.even, right, left), "core")
        return jnp.where(self.even, jnp.concatenate([keep, came]), jnp.concatenate([came, keep]))

    def group(self, shard, *widths):
        return self.share(self.spread(shard), *widths)

    def spread(self, shard):
        if not self.pieces:
            return self.gather(shard)
        rows = self.pair(shard)
        here = self.line(rows, self.along(rows))
        first, second = self.plane(here)
        return (here, first, second, self.send(first, "second"))

    def along(self, rows):
        return [self.send(rows, "z", self.nz - k) for k in range(1, self.nz)]

    def line(self, rows, came):
        return jnp.concatenate([rows] + list(came))

    def plane(self, here):
        return (self.send(here, "first"), self.send(here, "second"))

    def swap(self, parts):
        return tuple(self.send(part, "core") for part in parts)

    def spread_all(self, shards):
        if not self.pieces:
            return [self.gather(shard) for shard in shards], None
        one, two, three = (self.pair(shard) for shard in shards)
        came, two = sync((self.along(one), two))
        one = self.line(one, came)
        ones, came, three = sync((self.plane(one), self.along(two), three))
        two = self.line(two, came)
        last, twos, came = sync((self.send(ones[0], "second"), self.plane(two), self.along(three)))
        one = (one,) + tuple(ones) + (last,)
        three = self.line(three, came)
        other, last, threes = sync((self.swap(one), self.send(twos[0], "second"), self.plane(three)))
        two = (two,) + tuple(twos) + (last,)
        return [(one, other), two, (three,) + tuple(threes)], ones

    def share(self, mine, *widths, other=None):
        if not self.pieces:
            left, right = mine
            out, at = [], 0
            for width in widths:
                parts = [p[:, at : at + width] for p in (left, right)]
                out += parts if width == SMALL else [jnp.concatenate(parts, axis=1)]
                at += width
            return Group(self, out, 2 * left.shape[0] // self.count, widths)
        other = self.swap(mine) if other is None else other
        return Group(self, tuple(mine) + tuple(other), mine[0].shape[0] // self.nz, widths)

    def everything(self, near, widths, wide, after):
        if not self.pieces:
            return self.group(near, *widths), self.group(wide, wide.shape[1] // 2)
        near, wide = self.pair(near), self.pair(wide)
        rows = near.shape[0]
        stacks = [wide[at : at + rows] for at in range(0, wide.shape[0], rows)]
        unit = jnp.concatenate([near] + stacks, axis=1)
        unit, _ = sync((unit, after))
        unit = lax.all_gather(unit, AXES, axis=0, tiled=True)
        return (Whole(self, unit, rows, widths, near.shape[1], wide.shape),)

    def deliver(self, keep, away):
        terms = [keep, (yield self.send(away, "core"))]

        def total(start, stop):
            made = terms[0][start:stop].astype(jnp.float32)
            for term in terms[1:]:
                made = made + term[start:stop].astype(jnp.float32)
            return made.astype(jnp.bfloat16)

        half = keep.shape[0] // 2
        for axis in ("second", "first"):
            terms.append((yield self.send(total(half, 2 * half), axis)))
            half = half // 2
        rows = 2 * half // self.nz
        steps = [total(k * rows, (k + 1) * rows) for k in range(1, self.nz)]
        terms += list((yield [self.send(step, "z", k + 1) for k, step in enumerate(steps)]))
        mine = total(0, rows)
        rows = mine.shape[0] // 2
        keep = jnp.where(self.even, mine[:rows], mine[rows:])
        came = yield self.send(jnp.where(self.even, mine[rows:], mine[:rows]), "core")
        yield jnp.where(
            self.even,
            jnp.concatenate([keep, came], axis=1),
            jnp.concatenate([came, keep], axis=1),
        ).astype(jnp.float32)

    def settle(self, mine):
        rows = mine.shape[0] // 2
        keep = jnp.where(self.even, mine[:rows], mine[rows:])
        came = self.send(jnp.where(self.even, mine[rows:], mine[:rows]), "core")
        return jnp.where(
            self.even,
            jnp.concatenate([keep, came], axis=1),
            jnp.concatenate([came, keep], axis=1),
        ).astype(jnp.float32)

    def scatter(self, left, right):
        half = left.shape[1]
        rows = left.shape[0] // self.count
        places = (self.nz, self.nx, self.ny, 2 * rows, half)
        left = left.reshape(places).transpose(2, 1, 0, 3, 4)
        right = right.reshape(places).transpose(1, 2, 0, 3, 4)
        keep = jnp.where(self.even, left, right).astype(jnp.float32)
        away = jnp.where(self.even, right, left).astype(jnp.bfloat16)
        mine = (keep + self.send(away, "core").astype(jnp.float32)).astype(jnp.bfloat16)
        mine = self.scatter_axis(mine, "second")
        mine = self.scatter_axis(mine, "first")
        mine = self.scatter_axis(mine, "z")
        return self.settle(mine)

    def total(self, value):
        value = value.reshape(1, 1)
        for axis in ("core", "y", "x", "z"):
            n = {"core": 2, "y": self.ny, "x": self.nx, "z": self.nz}[axis]
            if n & (n - 1):
                value = sum([value] + [self.send(value, axis, k) for k in range(1, n)])
                continue
            bit = 1
            while bit < n:
                swap = []
                for i in range(self.count):
                    c, y = i % 2, i // 2 % self.ny
                    x, z = i // (2 * self.ny) % self.nx, i // (2 * self.ny * self.nx)
                    to = {"core": c, "y": y, "x": x, "z": z}
                    to[axis] ^= bit
                    swap.append(
                        (i, ((to["z"] * self.nx + to["x"]) * self.ny + to["y"]) * 2 + to["core"])
                    )
                value = value + lax.ppermute(value, AXES, swap)
                bit *= 2
        return value[0, 0]


def sync(values):
    return lax.optimization_barrier(values)


class Delivery:
    def __init__(self, grid, pair):
        if grid.pieces:
            self.steps = grid.deliver(*pair)
            self.under_way = next(self.steps)
        else:
            self.steps, self.under_way = None, grid.scatter(*pair)

    def beside(self, values):
        values, came = sync((values, self.under_way))
        self.under_way = self.steps.send(came) if self.steps else came
        return values


def halves(*arrays):
    return jnp.concatenate(
        [a[:, : a.shape[1] // 2] for a in arrays] + [a[:, a.shape[1] // 2 :] for a in arrays],
        axis=1,
    )


def cut(pair, *widths):
    out, at = [], 0
    for width in widths:
        out.append(jnp.concatenate([p[:, at : at + width // 2] for p in pair], axis=1))
        at += width // 2
    return out


def pad_to(array, columns):
    return jnp.pad(array, ((0, 0), (0, columns - array.shape[1])))


def small_rows(gains, biases, in_bias):
    features = gains.shape[1]
    return jnp.concatenate([gains.T, biases.T, in_bias.reshape(features, -1)], axis=1)


def small_back(rows):
    return (rows[:, :2].T, rows[:, 2:8].T, rows[:, 8:].reshape(-1))


def rows_of(index, count):
    return pl.ds(pl.multiple_of(index * count, count), count)


def nt(a, b):
    return lax.dot_general(a, b, (((1,), (1,)), ((), ())), preferred_element_type=jnp.float32)


def tn(a, b):
    return lax.dot_general(a, b, (((0,), (0,)), ((), ())), preferred_element_type=jnp.float32)


def nn(a, b):
    return jnp.dot(a, b, preferred_element_type=jnp.float32)


def fold(values):
    total = values[:8]
    for at in range(8, values.shape[0], 8):
        total = total + values[at : at + 8]
    return total


def norm_parts(values):
    centered = values - jnp.mean(values, axis=-1, keepdims=True)
    inverse = lax.rsqrt(jnp.mean(centered * centered, axis=-1, keepdims=True) + 1e-05)
    return (centered * inverse, inverse)


def norm_grad(grad, gain, normed, inverse):
    scaled = grad * gain
    middle = jnp.mean(scaled, axis=-1, keepdims=True)
    return inverse * (scaled - middle - normed * jnp.mean(scaled * normed, axis=-1, keepdims=True))


def gelu_parts(pre):
    share = 0.5 * (1.0 + lax.erf(pre * 0.7071067811865476))
    slope = share + pre * (0.3989422804014327 * jnp.exp(-0.5 * pre * pre))
    return (pre * share, slope)


class Group:
    def __init__(self, grid, arrays, piece, widths):
        self.arrays, self.piece, self.widths = tuple(arrays), piece, widths
        self.nz = grid.nz
        self.pieces = grid.pieces

    def copies(self, place, refs, targets, sems):
        out = []
        if not self.pieces:
            for ref, target, sem in zip(refs, targets, sems):
                if target is not None:
                    out.append(pltpu.make_async_copy(ref, target, sem))
            return out
        z, x, y, core = (place[i] for i in range(4))
        for kind in range(2):
            half = core if kind == 0 else 1 - core
            for second in range(2):
                for first in range(2):
                    ref = refs[kind * 4 + second * 2 + first]
                    x_at = lax.rem(x + first + half * (second - first), 2)
                    y_at = lax.rem(y + second + half * (first - second), 2)
                    for step in range(self.nz):
                        z_at = lax.rem(z + step, self.nz)
                        row = ((z_at * 2 + x_at) * 2 + y_at) * self.piece
                        rows = pl.ds(pl.multiple_of(row, 16), self.piece)
                        at = 0
                        for width, target, sem in zip(self.widths, targets, sems):
                            source = ref.at[pl.ds(step * self.piece, self.piece), pl.ds(at, width)]
                            at += width
                            if target is None:
                                continue
                            if len(target.shape) == 3:
                                goal = target.at[half, rows, :]
                            else:
                                columns = pl.ds(pl.multiple_of(half * width, 128), width)
                                goal = target.at[rows, columns]
                            out.append(pltpu.make_async_copy(source, goal, sem))
        return out

    def start(self, place, refs, targets, sems):
        for copy in self.copies(place, refs, targets, sems):
            copy.start()


class Whole:
    def __init__(self, grid, unit, piece, widths, near, wide):
        self.arrays, self.piece, self.widths = (unit,), piece, widths
        self.near, self.wide, self.devices = near, wide, grid.count

    def start(self, place, refs, targets, sems):
        (ref,) = refs

        def device(index, carry):
            chip, half = lax.div(index, 2), lax.rem(index, 2)
            source = pl.ds(pl.multiple_of(index * self.piece, 16), self.piece)
            at = 0
            for width, target, sem in zip(self.widths, targets, sems):
                if target is not None:
                    rows = pl.ds(pl.multiple_of(chip * self.piece, 16), self.piece)
                    columns = pl.ds(pl.multiple_of(half * width, 128), width)
                    pltpu.make_async_copy(
                        ref.at[source, pl.ds(at, width)], target.at[rows, columns], sem
                    ).start()
                at += width
            target, sem = targets[-1], sems[-1]
            if target is not None:
                width = self.wide[1]
                columns = pl.ds(pl.multiple_of(half * width, 128), width)
                for step in range(self.wide[0] // self.piece):
                    row = chip * self.wide[0] + step * self.piece
                    rows = pl.ds(pl.multiple_of(row, 16), self.piece)
                    pltpu.make_async_copy(
                        ref.at[source, pl.ds(at + step * width, width)], target.at[rows, columns], sem
                    ).start()
            return carry

        lax.fori_loop(0, self.devices, device, 0)


def start_cls(place, groups, refs, targets, sems):
    if isinstance(groups[0], Whole):
        groups[0].start(place, refs[0], targets, sems)
        return
    for group, held, ends in zip(groups, refs, (slice(0, 3), slice(3, 4))):
        group.start(place, held, targets[ends], sems[ends])


def finish(target, sem):
    pltpu.make_async_copy(target, target, sem).wait()


MIB = 2**20
FAR = pl.BlockSpec(memory_space=pltpu.HBM)
HERE = pl.BlockSpec(memory_space=pltpu.VMEM)
SCALARS = pl.BlockSpec(memory_space=pltpu.SMEM)


def call(kernel, outs, scratch, place, inputs, groups, vmem, flops=0, name=None, changed=()):
    def body(*refs):
        at = 1 + len(inputs)
        held = []
        for group in groups:
            held.append(refs[at : at + len(group.arrays)])
            at += len(group.arrays)
        at += len(changed)
        made = len(outs) + len(changed)
        kernel(refs[0], refs[1 : 1 + len(inputs)], held, refs[at : at + made], refs[at + made :])

    weights = [a for group in groups for a in group.arrays]
    first = 1 + len(inputs) + len(weights)
    size = sum(a.size * a.dtype.itemsize for a in list(inputs) + weights)
    size += sum(o.size * jnp.dtype(o.dtype).itemsize for o in outs)
    return pl.pallas_call(
        body,
        out_shape=tuple(jax.ShapeDtypeStruct(c.shape, c.dtype) for c in changed) + tuple(outs),
        in_specs=[SCALARS] + [HERE] * len(inputs) + [FAR] * (len(weights) + len(changed)),
        out_specs=[FAR] * len(changed) + [HERE] * len(outs),
        scratch_shapes=scratch,
        input_output_aliases={first + n: n for n in range(len(changed))},
        compiler_params=pltpu.CompilerParams(vmem_limit_bytes=(60 if name.startswith("cls_") else vmem) * MIB),
        cost_estimate=pl.CostEstimate(flops=flops, bytes_accessed=size, transcendentals=0),
        name=name,
    )(place, *inputs, *weights, *changed)


def shape_of(dtype, *shape):
    return jax.ShapeDtypeStruct(shape, dtype)


F32, LOW = jnp.float32, jnp.bfloat16


def both_heads(pair):
    first = lax.broadcasted_iota(jnp.int32, pair.shape, 1) < HEAD
    none = jnp.zeros_like(pair)
    return jnp.concatenate([jnp.where(first, pair, none), jnp.where(first, none, pair)])


def pair_probs(queries, keys, allowed):
    scores = nt(queries, keys) * HEAD**-0.5
    scores = jnp.where(allowed, scores, -1e30)
    weights = jnp.exp(scores - jnp.max(scores, axis=-1, keepdims=True))
    return weights * (1.0 / jnp.sum(weights, axis=-1, keepdims=True))


def side_by_side(stacked):
    half = stacked.shape[0] // 2
    return jnp.concatenate([stacked[:half], stacked[half:]], axis=1)


def allowed_pairs(column_ref, row_ref, window):
    same = column_ref[rows_of(window, SEG), :] == row_ref[pl.ds(window, 1), :]
    return jnp.concatenate([same, same])


def seg_attention(place, tokens, doc_column, doc_row, group):
    count, features = tokens.shape
    windows = count // SEG

    def kernel(place_ref, inputs, weights, outs, scratch):
        x_ref, column_ref, row_ref = inputs
        joined_ref, mixed_ref, small_ref, table_ref, mixeds_ref = outs
        qkv, low_ref, sem_qkv, sem_small = scratch
        targets = (qkv, small_ref) if group.pieces else (qkv, small_ref.at[0], small_ref.at[1])
        sems = (sem_qkv, sem_small, sem_small)
        group.start(place_ref, weights[0], targets, sems)
        low_ref[...] = x_ref[...].astype(LOW)
        finish(small_ref, sem_small)
        diagonal = lax.broadcasted_iota(jnp.int32, (SMALL, SMALL), 0) == lax.broadcasted_iota(
            jnp.int32, (SMALL, SMALL), 1
        )
        diagonal = jnp.where(diagonal, 1.0, 0.0).astype(LOW)
        for half in range(2):
            table_ref[half] = nt(diagonal, small_ref[half])
        finish(qkv, sem_qkv)
        width = features // 3

        def project(tile, carry):
            columns = pl.ds(pl.multiple_of(tile * width, width), width)
            for part in range(3):
                at = pl.ds(pl.multiple_of(part * features + tile * width, width), width)
                made = nn(low_ref[...], qkv[:, at])
                if part == 0:
                    made = made + table_ref[0, pl.ds(2, 1), columns]
                if part == 2:
                    made = made + table_ref[0, pl.ds(3, 1), columns]
                joined_ref[:, at] = made.astype(LOW)
            return carry

        lax.fori_loop(0, 3, project, 0)

        def window_step(window, carry):
            rows = rows_of(window, SEG)
            allowed = allowed_pairs(column_ref, row_ref, window)
            for at in range(0, features, 2 * HEAD):
                ends = slice(at, at + 2 * HEAD)
                keys = joined_ref[rows, slice(features + at, features + at + 2 * HEAD)]
                values = joined_ref[rows, slice(2 * features + at, 2 * features + at + 2 * HEAD)]
                probs = pair_probs(both_heads(joined_ref[rows, ends]), keys, allowed)
                mixed = nn(side_by_side(probs.astype(LOW)), both_heads(values))
                mixed_ref[rows, ends] = mixed.astype(LOW)
            return carry

        lax.fori_loop(0, windows, window_step, 0)
        mixeds_ref[...] = first_of_windows(mixed_ref, count)

    return call(
        kernel,
        (
            shape_of(LOW, count, 3 * features),
            shape_of(LOW, count, features),
            shape_of(LOW, 2, features, SMALL),
            shape_of(F32, 2, SMALL, features),
            shape_of(F32, 8, features),
        ),
        [
            pltpu.VMEM((features, 3 * features), LOW),
            pltpu.VMEM((count, features), LOW),
            pltpu.SemaphoreType.DMA,
            pltpu.SemaphoreType.DMA,
        ],
        place,
        (tokens, doc_column, doc_row),
        (group,),
        24,
        2 * count * features * 3 * features,
        "seg_attention",
    )


CHUNK = 32
TILE = 256


def first_of_windows(ref, count):
    rows = [ref[at : at + 16, :][0:1].astype(F32) for at in range(0, count, SEG)]
    return jnp.concatenate(rows + [jnp.zeros((8 - len(rows), ref.shape[1]), F32)])


def seg_inner(place, tokens, mixed, table, in_bias, near):
    count, features = tokens.shape
    hidden = in_bias.shape[1]

    def kernel(place_ref, inputs, weights, outs, scratch):
        x_ref, mixed_ref, table_ref, bias_ref = inputs
        n1_ref, v1_ref, low_ref, act_ref, slope_ref, slopes_ref, lows_ref, acts_ref = outs
        w_out, w_in, hold, sem_out, sem_in = scratch
        near.start(place_ref, weights[0], (w_out, w_in), (sem_out, sem_in))
        finish(w_out, sem_out)

        def branch(tile, carry):
            columns = rows_of(tile, TILE)
            hold[:, columns] = (
                nn(mixed_ref[...], w_out[:, columns])
                + table_ref[0, pl.ds(4, 1), columns]
                + x_ref[:, columns]
            )
            return carry

        lax.fori_loop(0, features // TILE, branch, 0)
        gain, shift = table_ref[0, pl.ds(0, 1), :], table_ref[0, pl.ds(5, 1), :]

        def first(chunk, carry):
            rows = rows_of(chunk, CHUNK)
            normed, inverse = norm_parts(hold[rows, :])
            n1_ref[rows, :] = normed
            v1_ref[rows, :] = inverse
            low_ref[rows, :] = (normed * gain + shift).astype(LOW)
            return carry

        lax.fori_loop(0, count // CHUNK, first, 0)
        finish(w_in, sem_in)

        def inner(tile, carry):
            columns = rows_of(tile, TILE)
            hold[:, pl.ds(0, TILE)] = nn(low_ref[...], w_in[:, columns])
            bias = bias_ref[:, columns]

            def gelu(chunk, inner_carry):
                rows = rows_of(chunk, 2 * CHUNK)
                active, slope = gelu_parts(hold[rows, pl.ds(0, TILE)] + bias)
                act_ref[rows, columns] = active.astype(LOW)
                slope_ref[rows, columns] = slope.astype(LOW)
                return inner_carry

            lax.fori_loop(0, count // (2 * CHUNK), gelu, 0)
            return carry

        lax.fori_loop(0, hidden // TILE, inner, 0)
        slopes_ref[...] = first_of_windows(slope_ref, count)
        lows_ref[...] = first_of_windows(low_ref, count)
        acts_ref[...] = first_of_windows(act_ref, count)

    return call(
        kernel,
        (
            shape_of(F32, count, features),
            shape_of(F32, count, 1),
            shape_of(LOW, count, features),
            shape_of(LOW, count, hidden),
            shape_of(LOW, count, hidden),
            shape_of(F32, 8, hidden),
            shape_of(F32, 8, features),
            shape_of(F32, 8, hidden),
        ),
        [
            pltpu.VMEM((features, features), LOW),
            pltpu.VMEM((features, hidden), LOW),
            pltpu.VMEM((count, features), F32),
            pltpu.SemaphoreType.DMA,
            pltpu.SemaphoreType.DMA,
        ],
        place,
        (tokens, mixed, table, in_bias),
        (near,),
        32,
        2 * count * features * (features + hidden),
        "seg_inner",
    )


def seg_outer(place, n1, v1, active, table, teacher, weight, wide):
    count, features = n1.shape
    hidden = active.shape[1]
    windows = count // SEG

    def kernel(place_ref, inputs, weights, outs, scratch):
        n1_ref, v1_ref, act_ref, table_ref, teacher_ref, weight_ref = inputs
        out_ref, cls_ref, n2_ref, v2_ref, n1s_ref, v1s_ref, n2s_ref, v2s_ref, err_ref = outs
        w_fc2, hold, sem_fc2 = scratch
        wide.start(place_ref, weights[0], (w_fc2,), (sem_fc2,))
        finish(w_fc2, sem_fc2)

        def second(tile, carry):
            columns = rows_of(tile, TILE)
            hold[:, columns] = nn(act_ref[...], w_fc2[:, columns])
            return carry

        lax.fori_loop(0, features // TILE, second, 0)
        gain, shift = table_ref[0, pl.ds(0, 1), :], table_ref[0, pl.ds(5, 1), :]
        last_bias = table_ref[0, pl.ds(6, 1), :]
        gain2, shift2 = table_ref[0, pl.ds(1, 1), :], table_ref[0, pl.ds(7, 1), :]

        def result(chunk, err):
            rows = rows_of(chunk, CHUNK)
            start = n1_ref[rows, :] * gain + shift
            normed, inverse = norm_parts(start + (hold[rows, :] + last_bias))
            n2_ref[rows, :] = normed
            v2_ref[rows, :] = inverse
            made = normed * gain2 + shift2
            out_ref[rows, :] = made
            misfit = made - teacher_ref[rows, :]
            return err + fold(weight_ref[rows, :] * misfit * misfit)

        err = lax.fori_loop(0, count // CHUNK, result, jnp.zeros((8, features), F32))
        err_ref[...] = jnp.sum(jnp.sum(err, axis=1, keepdims=True), axis=0, keepdims=True)
        cls_ref[...] = jnp.zeros_like(cls_ref)
        for window in range(windows):
            slot = 12 + place_ref[4] + window
            cls_ref[window : window + 1, :] = (
                out_ref[window * SEG : window * SEG + 1, :] + table_ref[1, pl.ds(slot, 1), :]
            )
        n1s_ref[...] = first_of_windows(n1_ref, count)
        v1s_ref[...] = first_of_windows(v1_ref, count)
        n2s_ref[...] = first_of_windows(n2_ref, count)
        v2s_ref[...] = first_of_windows(v2_ref, count)

    return call(
        kernel,
        (
            shape_of(F32, count, features),
            shape_of(F32, 8, features),
            shape_of(F32, count, features),
            shape_of(F32, count, 1),
            shape_of(F32, 8, features),
            shape_of(F32, 8, 1),
            shape_of(F32, 8, features),
            shape_of(F32, 8, 1),
            shape_of(F32, 1, 1),
        ),
        [
            pltpu.VMEM((hidden, features), LOW),
            pltpu.VMEM((count, features), F32),
            pltpu.SemaphoreType.DMA,
        ],
        place,
        (n1, v1, active, table, teacher, weight),
        (wide,),
        32,
        2 * count * features * hidden,
        "seg_outer",
    )


def cls_project(place, cls_rows, table, groups):
    count, features = cls_rows.shape

    def kernel(place_ref, inputs, weights, outs, scratch):
        x_ref, table_ref = inputs
        (joined_ref,) = outs
        qkv, sem = scratch
        start_cls(place_ref, groups, weights, (qkv, None, None, None), (sem,) * 4)
        low = x_ref[...].astype(LOW)
        finish(qkv, sem)
        for part in range(3):
            for at in range(0, features, TILE):
                start = part * features + at
                made = nn(low, qkv[:, start : start + TILE])
                if part == 0:
                    made = made + table_ref[1, 2:3, at : at + TILE]
                if part == 2:
                    made = made + table_ref[1, 3:4, at : at + TILE]
                joined_ref[:, start : start + TILE] = made.astype(LOW).astype(F32)

    return call(
        kernel,
        (shape_of(F32, count, 3 * features),),
        [pltpu.VMEM((features, 3 * features), LOW), pltpu.SemaphoreType.DMA],
        place,
        (cls_rows, table),
        groups,
        12,
        2 * count * features * 3 * features,
        "cls_project",
    )


def cls_middle(place, cls_rows, joined, both, teacher, weight, table, in_bias, err, groups):
    count, features = cls_rows.shape
    hidden = in_bias.shape[1]
    keys_count = both.shape[0]

    def kernel(place_ref, inputs, weights, outs, scratch):
        x_ref, joined_ref, both_ref, teacher_ref, weight_ref, table_ref, bias_ref, err_ref = inputs
        result_ref, query_ref, parts_ref, resid_ref, left_ref, right_ref = outs
        w_out, w_in, w_fc2, sem_out, sem_in, sem_fc2 = scratch
        start_cls(
            place_ref, groups, weights, (None, w_out, w_in, w_fc2), (None, sem_out, sem_in, sem_fc2)
        )
        heads = features // HEAD
        head_of = lax.broadcasted_iota(jnp.int32, (count, features), 1) // HEAD

        def spread(rows):
            return jnp.concatenate([jnp.where(head_of == h, rows, 0.0) for h in range(heads)])

        def gather_heads(rows):
            total = jnp.zeros((count, features), F32)
            for h in range(heads):
                total = total + jnp.where(head_of == h, rows[h * count : (h + 1) * count], 0.0)
            return total

        keys, values = both_ref[:, :features], both_ref[:, features:]
        queries = spread(joined_ref[:, :features]).astype(LOW)
        scores = nt(queries, keys) * HEAD**-0.5
        exps = jnp.exp(scores - jnp.max(scores, axis=-1, keepdims=True))
        probs = exps / jnp.sum(exps, axis=-1, keepdims=True)
        mixed = gather_heads(nn(probs.astype(LOW), values)).astype(LOW)
        x = x_ref[...]

        def row(index):
            return table_ref[1, index : index + 1, :]

        finish(w_out, sem_out)
        n1, v1 = norm_parts(x + (nn(mixed, w_out[...]) + row(4)))
        first = n1 * row(0) + row(5)
        first_low = first.astype(LOW)
        finish(w_in, sem_in)
        finish(w_fc2, sem_fc2)
        second = jnp.zeros((count, features), F32)
        slopes = []
        for at in range(0, hidden, features):
            ends = slice(at, at + features)
            active, slope = gelu_parts(nn(first_low, w_in[:, ends]) + bias_ref[:, ends])
            active = active.astype(LOW)
            slopes.append(slope)
            left_ref[:, slice(2 * features + at, 3 * features + at)] = active.astype(F32)
            second = second + nn(active, w_fc2[ends, :])
        n2, v2 = norm_parts(first + (second + row(6)))
        result = n2 * row(1) + row(7)
        result_ref[...] = result
        grad = weight_ref[...] * (result - teacher_ref[...])
        grad_sum2 = norm_grad(grad, row(1), n2, v2)
        grad_second = grad_sum2.astype(LOW)
        grad_first = grad_sum2
        for step, at in enumerate(range(0, hidden, features)):
            ends = slice(at, at + features)
            grad_pre = (slopes[step] * nt(grad_second, w_fc2[ends, :])).astype(LOW)
            right_ref[:, slice(features + at, 2 * features + at)] = grad_pre.astype(F32)
            grad_first = grad_first + nt(grad_pre, w_in[:, ends])
        grad_sum1 = norm_grad(grad_first, row(0), n1, v1)
        grad_branch = grad_sum1.astype(LOW)
        resid_ref[...] = grad_sum1
        grad_mixed = spread(nt(grad_branch, w_out[...]).astype(LOW).astype(F32)).astype(LOW)
        grad_probs = nt(grad_mixed, values)
        grad_scores = probs * (grad_probs - jnp.sum(probs * grad_probs, axis=-1, keepdims=True))
        grad_scores = grad_scores.astype(LOW)
        query_ref[...] = (gather_heads(nn(grad_scores, keys)) * HEAD**-0.5).astype(LOW).astype(F32)
        parts_ref[:, :features] = (tn(grad_scores, queries) * HEAD**-0.5).astype(LOW)
        parts_ref[:, features:] = tn(probs.astype(LOW), grad_mixed).astype(LOW)
        left_ref[:, :features] = mixed.astype(F32)
        left_ref[:, features : 2 * features] = first_low.astype(F32)
        right_ref[:, :features] = grad_branch.astype(F32)
        right_ref[:, features + hidden : 2 * features + hidden] = grad_second.astype(F32)
        vectors = [grad_first * n1, grad_first, grad * n2, grad]
        vectors = [jnp.sum(v, axis=0, keepdims=True) for v in vectors]
        right_ref[:, 2 * features + hidden : 3 * features + hidden] = jnp.concatenate(
            vectors + [jnp.zeros((count - 4, features), F32)]
        )
        misfit = result - teacher_ref[...]
        total = jnp.sum(fold(grad * misfit), axis=1, keepdims=True)
        total = jnp.sum(total, axis=0, keepdims=True) + err_ref[...]
        high = total.astype(LOW).astype(F32)
        middle = (total - high).astype(LOW).astype(F32)
        rest = total - high - middle
        lane = lax.broadcasted_iota(jnp.int32, (count, SMALL), 1)
        line = lax.broadcasted_iota(jnp.int32, (count, SMALL), 0)
        value = jnp.where(lane == 0, high, jnp.where(lane == 1, middle, rest))
        right_ref[:, 3 * features + hidden :] = jnp.where((line == 0) & (lane < 3), value, 0.0)

    return call(
        kernel,
        (
            shape_of(F32, count, features),
            shape_of(F32, count, features),
            shape_of(LOW, keys_count, 2 * features),
            shape_of(F32, count, features),
            shape_of(F32, count, 2 * features + hidden),
            shape_of(F32, count, 3 * features + hidden + SMALL),
        ),
        [
            pltpu.VMEM((features, features), LOW),
            pltpu.VMEM((features, hidden), LOW),
            pltpu.VMEM((hidden, features), LOW),
            pltpu.SemaphoreType.DMA,
            pltpu.SemaphoreType.DMA,
            pltpu.SemaphoreType.DMA,
        ],
        place,
        (cls_rows, joined, both, teacher, weight, table, in_bias, err),
        groups,
        24,
        4 * count * features * (features + 2 * hidden),
        "cls_middle",
    )


def cls_finish(place, query, parts, resid, result, cls_rows, left, right, kept, lefts, table, changed, groups, near, wide):
    count, features = query.shape
    windows = parts.shape[0] // lax.axis_size("fsdp")
    hidden = kept[4].shape[1]
    changed = tuple(changed)
    columns = 8 * features + 2 * hidden

    def kernel(place_ref, inputs, weights, outs, scratch):
        query_ref, parts_ref, resid_ref, result_ref, cls_ref, left_ref, right_ref = inputs[:7]
        n1_ref, v1_ref, n2_ref, v2_ref, slope_ref, mixeds_ref, lows_ref, acts_ref, table_ref = inputs[7:]
        factors_ref, sums_ref, bias_ref = outs[len(changed) :]
        qkv, w_out, w_in, w_fc2, flat, tall, joined_ref, made, sem, sem_out, sem_in, sem_fc2, flat_sem, tall_sem = scratch
        start_cls(place_ref, groups, weights, (qkv, None, None, None), (sem,) * 4)
        wide.start(place_ref, weights[-1], (w_fc2,), (sem_fc2,))
        near.start(place_ref, weights[-2], (w_out, w_in), (sem_out, sem_in))
        whole = [outs[0], outs[2]]
        copies = []
        for window in range(windows):
            eight, sixteen = pl.ds(window * SEG, 8), pl.ds(window * SEG, 16)
            for number, ref in enumerate(whole):
                copies.append((ref.at[eight, :], tall.at[number, window], tall_sem))
            copies.append((outs[1].at[sixteen, :], flat.at[window], flat_sem))
        for source, goal, done in copies:
            pltpu.make_async_copy(source, goal, done).start()
        both = parts_ref[...].astype(F32)
        total = both[:windows]
        for at in range(windows, both.shape[0], windows):
            total = total + both[at : at + windows]
        joined_ref[...] = jnp.zeros_like(joined_ref)
        joined_ref[:, :features] = query_ref[...]
        joined_ref[:windows, features:] = total.astype(LOW).astype(F32)
        finish(qkv, sem)
        grad = nt(joined_ref[...].astype(LOW), qkv[...]) + resid_ref[...]
        made[...] = jnp.zeros_like(made)

        def top(at, values):
            made[:windows, at : at + values.shape[1]] = values[:windows]

        def bottom(at, values):
            made[windows : 2 * windows, at : at + values.shape[1]] = values[:windows]

        wide_left = 2 * features + hidden
        top(0, mixeds_ref[...])
        top(features, lows_ref[...])
        top(2 * features, acts_ref[...])
        top(2 * wide_left, right_ref[:, wide_left:])
        top(2 * wide_left + features + SMALL, grad.astype(LOW).astype(F32))
        bottom(0, cls_ref[...].astype(LOW).astype(F32))
        bottom(features, left_ref[...])
        bottom(features + wide_left, joined_ref[...])
        bottom(4 * features + wide_left, right_ref[:, :wide_left])

        def row(index):
            return table_ref[0, index : index + 1, :]

        def sums(values):
            return jnp.sum(values, axis=0, keepdims=True)

        sums_ref[1:2, :] = sums(grad * n2_ref[...])
        sums_ref[7:8, :] = sums(grad)
        grad_sum2 = norm_grad(grad, row(1), n2_ref[...], v2_ref[...])
        grad_second = grad_sum2.astype(LOW)
        sums_ref[6:7, :] = sums(grad_second.astype(F32))
        grad_first = grad_sum2
        finish(w_fc2, sem_fc2)
        finish(w_in, sem_in)
        for at in range(0, hidden, features):
            ends = slice(at, at + features)
            grad_pre = (slope_ref[:, ends] * nt(grad_second, w_fc2[ends, :])).astype(LOW)
            top(wide_left + features + at, grad_pre.astype(F32))
            bias_ref[:, ends] = sums(grad_pre.astype(F32))
            grad_first = grad_first + nt(grad_pre, w_in[:, ends])
        sums_ref[0:1, :] = sums(grad_first * n1_ref[...])
        sums_ref[5:6, :] = sums(grad_first)
        grad_sum1 = norm_grad(grad_first, row(0), n1_ref[...], v1_ref[...])
        grad_branch = grad_sum1.astype(LOW)
        sums_ref[4:5, :] = sums(grad_branch.astype(F32))
        sums_ref[2:4, :] = jnp.zeros((2, features), F32)
        finish(w_out, sem_out)
        grad_mixed = nt(grad_branch, w_out[...]).astype(LOW).astype(F32)
        top(wide_left, grad_branch.astype(F32))
        top(wide_left + features + hidden, grad_second.astype(F32))
        factors_ref[...] = made[...].astype(LOW)
        finish(tall, tall_sem)
        finish(flat, flat_sem)
        top8 = lax.broadcasted_iota(jnp.int32, (8, features), 0) == 0
        top16 = lax.broadcasted_iota(jnp.int32, (16, features), 0) == 0
        for window in range(windows):
            line = slice(window, window + 1)
            for number, values in enumerate((result_ref[line, :], grad_sum1[line])):
                tall[number, window] = jnp.where(top8, values, tall[number, window])
            held = jnp.where(top16, grad_mixed[line], flat[window].astype(F32))
            flat[window] = held.astype(LOW)
        for source, goal, done in copies:
            pltpu.make_async_copy(goal, source, done).start()
        finish(tall, tall_sem)
        finish(flat, flat_sem)

    return call(
        kernel,
        (
            shape_of(LOW, 2 * windows, columns),
            shape_of(F32, 8, features),
            shape_of(F32, 1, hidden),
        ),
        [
            pltpu.VMEM((features, 3 * features), LOW),
            pltpu.VMEM((features, features), LOW),
            pltpu.VMEM((features, hidden), LOW),
            pltpu.VMEM((hidden, features), LOW),
            pltpu.VMEM((windows, 16, features), LOW),
            pltpu.VMEM((2, windows, 8, features), F32),
            pltpu.VMEM((count, 3 * features), F32),
            pltpu.VMEM((2 * windows, columns), F32),
        ]
        + [pltpu.SemaphoreType.DMA] * 6,
        place,
        (query, parts, resid, result, cls_rows, left, right) + tuple(kept) + tuple(lefts) + (table,),
        tuple(groups) + (near, wide),
        28,
        2 * count * features * (4 * features + 2 * hidden),
        "cls_finish",
        changed,
    )


def seg_feed_back(place, kept, teacher, weight, table, near, wide):
    first_out, n1, v1, slope, n2, v2 = kept
    count, features = first_out.shape
    hidden = slope.shape[1]

    def kernel(place_ref, inputs, weights, outs, scratch):
        first_ref, n1_ref, v1_ref, slope_ref, n2_ref, v2_ref, teacher_ref, weight_ref, table_ref = inputs
        second_ref, pre_ref, branch_ref, mixed_ref, resid_ref, sums_ref, bias_ref = outs
        w_out, w_in, w_fc2, sum2, sem_out, sem_in, sem_fc2 = scratch
        near.start(place_ref, weights[0], (w_out, w_in), (sem_out, sem_in))
        wide.start(place_ref, weights[1], (w_fc2,), (sem_fc2,))
        gain1, gain2 = table_ref[0, pl.ds(0, 1), :], table_ref[0, pl.ds(1, 1), :]
        nothing = jnp.zeros((8, features), F32)

        def last(chunk, carry):
            total_gain, total_shift, total_second = carry
            rows = rows_of(chunk, CHUNK)
            grad = weight_ref[rows, :] * (first_ref[rows, :] - teacher_ref[rows, :])
            normed = n2_ref[rows, :]
            total_gain = total_gain + fold(grad * normed)
            total_shift = total_shift + fold(grad)
            grad = norm_grad(grad, gain2, normed, v2_ref[rows, :])
            sum2[rows, :] = grad
            low = grad.astype(LOW)
            second_ref[rows, :] = low
            return (total_gain, total_shift, total_second + fold(low.astype(F32)))

        total_gain, total_shift, total_second = lax.fori_loop(
            0, count // CHUNK, last, (nothing,) * 3
        )
        sums_ref[1:2, :] = jnp.sum(total_gain, axis=0, keepdims=True)
        sums_ref[7:8, :] = jnp.sum(total_shift, axis=0, keepdims=True)
        sums_ref[6:7, :] = jnp.sum(total_second, axis=0, keepdims=True)
        finish(w_fc2, sem_fc2)

        def inner(tile, carry):
            columns = rows_of(tile, TILE)
            grad = (nt(second_ref[...], w_fc2[columns, :]) * slope_ref[:, columns].astype(F32)).astype(LOW)
            pre_ref[:, columns] = grad
            bias_ref[:, columns] = jnp.sum(fold(grad.astype(F32)), axis=0, keepdims=True)
            return carry

        lax.fori_loop(0, hidden // TILE, inner, 0)
        finish(w_in, sem_in)

        def middle(tile, carry):
            columns = rows_of(tile, TILE)
            sum2[:, columns] = nt(pre_ref[...], w_in[columns, :]) + sum2[:, columns]
            return carry

        lax.fori_loop(0, features // TILE, middle, 0)

        def first(chunk, carry):
            total_gain, total_shift, total_branch = carry
            rows = rows_of(chunk, CHUNK)
            grad, normed = sum2[rows, :], n1_ref[rows, :]
            total_gain = total_gain + fold(grad * normed)
            total_shift = total_shift + fold(grad)
            grad = norm_grad(grad, gain1, normed, v1_ref[rows, :])
            resid_ref[rows, :] = grad
            low = grad.astype(LOW)
            branch_ref[rows, :] = low
            return (total_gain, total_shift, total_branch + fold(low.astype(F32)))

        total_gain, total_shift, total_branch = lax.fori_loop(
            0, count // CHUNK, first, (nothing,) * 3
        )
        sums_ref[0:1, :] = jnp.sum(total_gain, axis=0, keepdims=True)
        sums_ref[5:6, :] = jnp.sum(total_shift, axis=0, keepdims=True)
        sums_ref[4:5, :] = jnp.sum(total_branch, axis=0, keepdims=True)
        sums_ref[2:4, :] = jnp.zeros((2, features), F32)
        finish(w_out, sem_out)

        def before(tile, carry):
            columns = rows_of(tile, TILE)
            mixed_ref[:, columns] = nt(branch_ref[...], w_out[columns, :]).astype(LOW)
            return carry

        lax.fori_loop(0, features // TILE, before, 0)

    return call(
        kernel,
        (
            shape_of(LOW, count, features),
            shape_of(LOW, count, hidden),
            shape_of(LOW, count, features),
            shape_of(LOW, count, features),
            shape_of(F32, count, features),
            shape_of(F32, 8, features),
            shape_of(F32, 1, hidden),
        ),
        [
            pltpu.VMEM((features, features), LOW),
            pltpu.VMEM((features, hidden), LOW),
            pltpu.VMEM((hidden, features), LOW),
            pltpu.VMEM((count, features), F32),
            pltpu.SemaphoreType.DMA,
            pltpu.SemaphoreType.DMA,
            pltpu.SemaphoreType.DMA,
        ],
        place,
        (first_out, n1, v1, slope, n2, v2, teacher, weight, table),
        (near, wide),
        48,
        2 * count * features * (features + 2 * hidden),
        "seg_feed_back",
    )


def seg_attention_back(place, joined, grad_mixed, resid, doc_column, doc_row, group):
    count, features = resid.shape
    windows = count // SEG

    def kernel(place_ref, inputs, weights, outs, scratch):
        joined_ref, mixed_ref, resid_ref, column_ref, row_ref = inputs
        grad_ref, rows_ref, sums_ref = outs
        qkv, sem = scratch
        group.start(place_ref, weights[0], (qkv,) + (None,) * (len(group.widths) - 1), (sem, None, None))
        sums_ref[...] = jnp.zeros_like(sums_ref)

        def window_step(window, carry):
            rows = rows_of(window, SEG)
            allowed = allowed_pairs(column_ref, row_ref, window)
            for at in range(0, features, 2 * HEAD):
                ends = slice(at, at + 2 * HEAD)
                key_ends = slice(features + at, features + at + 2 * HEAD)
                value_ends = slice(2 * features + at, 2 * features + at + 2 * HEAD)
                queries, keys = both_heads(joined_ref[rows, ends]), joined_ref[rows, key_ends]
                probs = pair_probs(queries, keys, allowed)
                grads = both_heads(mixed_ref[rows, ends])
                grad_values = tn(probs.astype(LOW), grads).astype(LOW)
                grad_probs = nt(grads, joined_ref[rows, value_ends])
                grad_scores = probs * (
                    grad_probs - jnp.sum(probs * grad_probs, axis=-1, keepdims=True)
                )
                grad_scores = grad_scores.astype(LOW)
                grad_query = nn(side_by_side(grad_scores), both_heads(keys)) * HEAD**-0.5
                grad_query = grad_query.astype(LOW)
                grad_ref[rows, ends] = grad_query
                grad_ref[rows, key_ends] = (tn(grad_scores, queries) * HEAD**-0.5).astype(LOW)
                grad_ref[rows, value_ends] = grad_values
                sums_ref[0, :, ends] += fold(grad_query.astype(F32))
                sums_ref[1, :, ends] += fold(grad_values.astype(F32))
            return carry

        lax.fori_loop(0, windows, window_step, 0)
        finish(qkv, sem)

        def before(tile, carry):
            columns = rows_of(tile, TILE)
            rows_ref[:, columns] = nt(grad_ref[...], qkv[columns, :]) + resid_ref[:, columns]
            return carry

        lax.fori_loop(0, features // TILE, before, 0)

    return call(
        kernel,
        (
            shape_of(LOW, count, 3 * features),
            shape_of(F32, count, features),
            shape_of(F32, 2, 8, features),
        ),
        [pltpu.VMEM((features, 3 * features), LOW), pltpu.SemaphoreType.DMA],
        place,
        (joined, grad_mixed, resid, doc_column, doc_row),
        (group,),
        24,
        2 * count * features * 3 * features,
        "seg_attention_back",
    )


def weight_grads(grid, place, factors, vectors=None):
    count, rows = factors[0][0].shape
    piece = rows // (grid.count // 2)
    widths = [right.shape[1] // 2 for left, right in factors]
    extra = 0 if vectors is None else SMALL
    half_width = sum(widths) + extra
    tile = 384 if rows % 384 == 0 and 384 % piece == 0 else rows
    flat = [a for pair in factors for a in pair] + ([] if vectors is None else [vectors])

    def kernel(place_ref, inputs, weights, outs, scratch):
        z, x, y, core = (place_ref[i] for i in range(4))

        def put(made, start, half, at, width):
            columns = slice(at, at + width)
            if not grid.pieces:
                outs[half][pl.ds(start, made.shape[0]), columns] = made
                return
            for step in range(made.shape[0] // piece):
                index = (lax.div(start, piece) if not isinstance(start, int) else start // piece) + step
                y_off = lax.rem(index + y, 2)
                x_off = lax.rem(lax.div(index, 2) + x, 2)
                z_off = lax.rem(lax.div(index, 4) - z + grid.nz, grid.nz)
                first, second = (x_off, y_off) if half == 0 else (y_off, x_off)
                goal = pl.multiple_of(((second * 2 + first) * grid.nz + z_off) * piece, 16)
                block = made[step * piece : (step + 1) * piece]

                @pl.when(core == half)
                def _():
                    outs[0][pl.ds(goal, piece), columns] = block

                @pl.when(core != half)
                def _():
                    outs[1][pl.ds(goal, piece), columns] = block

        at = 0
        for number, width in enumerate(widths):
            left, right = inputs[2 * number], inputs[2 * number + 1]

            def step(index, carry, left=left, right=right, width=width, at=at):
                start = pl.multiple_of(index * tile, tile)
                scratch[0][...] = left[:, pl.ds(start, tile)].T
                for half in range(2):
                    made = nn(scratch[0][...], right[:, half * width : (half + 1) * width])
                    put(made.astype(LOW), start, half, at, width)
                return carry

            lax.fori_loop(0, rows // tile, step, 0)
            at += width
        if vectors is not None:
            chosen = lax.broadcasted_iota(jnp.int32, (vectors.shape[0], SMALL), 0)
            chosen = chosen == lax.broadcasted_iota(jnp.int32, (vectors.shape[0], SMALL), 1)
            chosen = jnp.where(chosen, 1.0, 0.0).astype(LOW)
            made = tn(inputs[-1][...].astype(LOW), chosen).astype(LOW)
            put(made, 0, 0, at, SMALL)
            put(jnp.zeros_like(made), 0, 1, at, SMALL)

    return call(
        kernel,
        (shape_of(LOW, rows, half_width), shape_of(LOW, rows, half_width)),
        [pltpu.VMEM((tile, count), LOW)],
        place,
        flat,
        (),
        40,
        2 * count * rows * 2 * half_width,
        "weight_grads",
    )


def cls_weight_grads(place, factors, grid, features, hidden, slots, tokens):
    count = factors.shape[0]
    share, wide = features // grid.count, hidden // grid.count
    windows = count // grid.count // 2

    def kernel(place_ref, inputs, weights, outs, scratch):
        (all_ref,) = inputs
        qkv_ref, out_ref, in_ref, fc2_ref, gains_ref, biases_ref, bias_ref, pos_ref = outs[:8]
        more_out_ref, more_in_ref, more_fc2_ref, loss_ref = outs[8:]
        index = place_ref[5]

        def own(at, width, part, lower):
            source = lax.broadcasted_iota(jnp.int32, (width, part), 0)
            goal = lax.broadcasted_iota(jnp.int32, (width, part), 1) + index * part
            chosen = jnp.where(source == goal, 1.0, 0.0).astype(LOW)
            line = lax.rem(lax.broadcasted_iota(jnp.int32, (count, part), 0), 2 * windows)
            return jnp.where((line >= windows) == lower, nn(all_ref[:, at : at + width], chosen), 0.0)

        def sums(values):
            return jnp.sum(values, axis=0, keepdims=True)

        def columns(at, width):
            return all_ref[:, at : at + width]

        wide_left = 2 * features + hidden
        joined = features + wide_left
        branch = joined + 3 * features
        pre = branch + features
        second = pre + hidden

        def product(at, width, part, lower, right, columns_count):
            return tn(own(at, width, part, lower).astype(LOW), columns(right, columns_count))

        qkv_ref[...] = product(0, features, share, True, joined, 3 * features)
        out_ref[...] = product(features, features, share, True, branch, features)
        in_ref[...] = product(2 * features, features, share, True, pre, hidden)
        fc2_ref[...] = product(3 * features, hidden, wide, True, second, features)
        more_out_ref[...] = product(0, features, share, False, wide_left, features)
        more_in_ref[...] = product(features, features, share, False, wide_left + features, hidden)
        more_fc2_ref[...] = product(
            2 * features, hidden, wide, False, wide_left + features + hidden, features
        )
        vectors = 2 * wide_left
        err = vectors + features
        rows_at = err + SMALL
        line = lax.rem(lax.broadcasted_iota(jnp.int32, (count, SMALL), 0), 2 * windows)
        total = jnp.where(line == 0, columns(err, SMALL).astype(F32), 0.0)
        loss_ref[...] = sums(jnp.sum(total, axis=1, keepdims=True)) * (0.5 / (tokens * features))
        vector = own(vectors, features, share, False)
        line = lax.rem(lax.broadcasted_iota(jnp.int32, vector.shape, 0), 2 * windows)
        rows = [sums(jnp.where(line == v, vector, 0.0)) for v in range(4)]
        gains_ref[0:1, :] = rows[0]
        gains_ref[1:2, :] = rows[2]
        biases_ref[0:1, :] = sums(own(joined, features, share, True))
        biases_ref[1:2, :] = sums(own(joined + 2 * features, features, share, True))
        biases_ref[2:3, :] = sums(own(branch, features, share, True))
        biases_ref[3:4, :] = rows[1]
        biases_ref[4:5, :] = sums(own(second, features, share, True))
        biases_ref[5:6, :] = rows[3]
        bias_ref[...] = sums(own(pre, hidden, wide, True))
        slot = lax.broadcasted_iota(jnp.int32, (slots, count), 0)
        row = lax.broadcasted_iota(jnp.int32, (slots, count), 1)
        window = lax.rem(row, 2 * windows)
        of = lax.rem(lax.div(row, 2 * windows) * windows + window, slots)
        chosen = jnp.where((slot == of) & (window < windows), 1.0, 0.0).astype(LOW)
        pos_ref[...] = nn(chosen, own(rows_at, features, share, False).astype(LOW))

    return call(
        kernel,
        (
            shape_of(F32, share, 3 * features),
            shape_of(F32, share, features),
            shape_of(F32, share, hidden),
            shape_of(F32, wide, features),
            shape_of(F32, 2, share),
            shape_of(F32, 6, share),
            shape_of(F32, 1, wide),
            shape_of(F32, slots, share),
            shape_of(F32, share, features),
            shape_of(F32, share, hidden),
            shape_of(F32, wide, features),
            shape_of(F32, 1, 1),
        ),
        [],
        place,
        (factors,),
        (),
        30 if count <= 256 else 60,
        2 * count * features * 20000 // 24,
        "cls_weight_grads",
    )


def per_device(
    tokens,
    doc_ids,
    teacher,
    seg_qkv,
    seg_out,
    seg_in,
    seg_fc2,
    seg_gains,
    seg_biases,
    seg_in_bias,
    cls_qkv,
    cls_out,
    cls_in,
    cls_fc2,
    cls_gains,
    cls_biases,
    cls_in_bias,
    seg_pos,
):
    rows_count, features = tokens.shape
    windows = rows_count // SEG
    low = jnp.bfloat16
    grid = Grid(features)
    hidden = seg_in.shape[1]
    slot_count = seg_pos.shape[0]
    per_feature = 8 + hidden // features
    fsdp = lax.axis_index("fsdp")
    place = jnp.stack(
        [grid.z, grid.x, grid.y, grid.core, fsdp * windows, grid.index]
    ).astype(jnp.int32)
    validity = (doc_ids >= 0).astype(jnp.float32)
    counts = jnp.sum(validity.reshape(windows, SEG), axis=1)
    own = jnp.arange(seg_qkv.shape[0], dtype=jnp.int32)[:, None] == 0
    small_left = pad_to(small_rows(seg_gains, seg_biases, seg_in_bias), SMALL)
    small_right = jnp.concatenate(
        [
            small_rows(cls_gains, cls_biases, cls_in_bias),
            seg_pos.T,
            jnp.where(own, counts[None, :], 0.0),
        ],
        axis=1,
    )
    small = jnp.concatenate([small_left, pad_to(small_right, SMALL)], axis=1).astype(low)
    half, wide_half = features // 2, hidden // 2
    spreads, begun = grid.spread_all(
        (
            halves(seg_qkv.astype(low), small),
            halves(seg_out.astype(low), seg_in.astype(low)),
            seg_fc2.astype(low),
        )
    )
    cls_groups = grid.everything(
        halves(cls_qkv.astype(low), cls_out.astype(low), cls_in.astype(low)),
        (3 * half, half, wide_half),
        cls_fc2.astype(low),
        begun,
    )
    mine, other = spreads[0]
    group_qkv = grid.share(mine if grid.pieces else spreads[0], 3 * half, SMALL, other=other)
    doc_column, doc_row = doc_ids[:, None], doc_ids.reshape(windows, SEG)
    joined, mixed, small, table, mixeds = seg_attention(place, tokens, doc_column, doc_row, group_qkv)
    near, wide = spreads[1:]
    if grid.pieces:
        others, last, mixed = sync((grid.swap(near), grid.send(wide[1], "second"), mixed))
        group_near = grid.share(near, half, wide_half, other=others)
        wide = wide + (last,)
    else:
        group_near = grid.share(near, half, wide_half)
    group_fc2 = grid.share(wide, half)
    seg_bias = small[0][:, 8:per_feature].astype(jnp.float32).reshape(1, hidden)
    cls_bias = small[1][:, 8:per_feature].astype(jnp.float32).reshape(1, hidden)
    at = per_feature + slot_count
    token_count = jnp.sum(small[1][:, at : at + windows].astype(jnp.float32))
    everything = rows_count * grid.count
    weight = ((2.0 * everything / token_count) * validity)[:, None]
    place_in = lax.broadcasted_iota(jnp.int32, weight.shape, 0) % SEG
    others_weight = jnp.where(place_in == 0, 0.0, weight)

    def cls_only(rows):
        return rows.reshape(windows, SEG, -1)[:, 0]

    def eight(rows):
        return jnp.pad(rows, ((0, 8 - windows), (0, 0)))

    n1, v1, first_low, active, slope, slopes, lows, actives = seg_inner(
        place, tokens, mixed, table, seg_bias, group_near
    )
    first_out, cls_rows, n2, v2, n1s, v1s, n2s, v2s, err = seg_outer(
        place, n1, v1, active, table, teacher, others_weight, group_fc2
    )
    grad_second, grad_pre, grad_branch, grad_mixed, resid, sums, bias_sums = seg_feed_back(
        place,
        (first_out, n1, v1, slope, n2, v2),
        teacher,
        others_weight,
        table,
        group_near,
        group_fc2,
    )
    fc2_way = Delivery(grid, weight_grads(grid, place, [(active, grad_second)]))
    pair = weight_grads(grid, place, [(mixed, grad_branch), (first_low, grad_pre)])
    pair, cls_rows = fc2_way.beside((pair, cls_rows))
    near_way = Delivery(grid, pair)

    (cls_joined,) = cls_project(place, cls_rows, table, cls_groups)
    cls_joined = near_way.beside(cls_joined)
    both = lax.all_gather(
        cls_joined[:windows, features:].astype(low), "fsdp", axis=0, tiled=True
    )
    cls_result, cls_query, parts, cls_resid, left, right = cls_middle(
        place,
        cls_rows,
        cls_joined,
        both,
        eight(cls_only(teacher)),
        eight(cls_only(weight)),
        table,
        cls_bias,
        err,
        cls_groups,
    )
    parts = fc2_way.beside(parts)
    parts = lax.all_to_all(parts, "fsdp", 0, 0, tiled=True)
    output, grad_mixed, resid, factors, more_sums, more_bias = cls_finish(
        place,
        cls_query,
        parts,
        cls_resid,
        cls_result,
        cls_rows,
        left,
        right,
        (n1s, v1s, n2s, v2s, slopes),
        (mixeds, lows, actives),
        table,
        (first_out, grad_mixed, resid),
        cls_groups,
        group_near,
        group_fc2,
    )
    factors = lax.all_gather(factors, AXES, axis=0, tiled=True)

    grad_mixed = fc2_way.beside(grad_mixed)
    grad_joined, grad_tokens, head_sums = seg_attention_back(
        place, joined, grad_mixed, resid, doc_column, doc_row, group_qkv
    )
    grad_joined = near_way.beside(fc2_way.beside(grad_joined))
    sums, bias_sums = sums + more_sums, bias_sums + more_bias
    vectors = jnp.concatenate(
        [
            sums[:2],
            jnp.sum(head_sums, axis=1),
            sums[4:],
            bias_sums.reshape(features, -1).T,
            jnp.zeros((16 - per_feature, features), jnp.float32),
        ]
    )
    pair = weight_grads(grid, place, [(tokens.astype(low), grad_joined)], vectors)
    pair = near_way.beside(fc2_way.beside(pair))
    qkv_way = Delivery(grid, pair)
    for step in range(4 if grid.pieces else 0):
        if step < 2:
            near_way.beside(qkv_way.beside(()))
        else:
            qkv_way.beside(())
    if grid.pieces:
        qkv_way.beside(())
    grad_qkv, grad_near, grad_fc2 = qkv_way.under_way, near_way.under_way, fc2_way.under_way
    cls_grads = cls_weight_grads(place, factors, grid, features, hidden, slot_count, everything)
    extra_out, extra_in, extra_fc2, loss = cls_grads[8:]
    ends = grad_near.shape[1] // 2
    seg_grad_out, seg_grad_in = cut((grad_near[:, :ends], grad_near[:, ends:]), features, hidden)
    ends = grad_qkv.shape[1] // 2
    seg_grad_qkv = cut((grad_qkv[:, :ends], grad_qkv[:, ends:]), 3 * features)[0]
    seg_tail = small_back(grad_qkv[:, 3 * half : 3 * half + per_feature])
    return (
        (output, loss[0, 0], grad_tokens, seg_grad_qkv, seg_grad_out + extra_out)
        + (seg_grad_in + extra_in, grad_fc2 + extra_fc2)
        + seg_tail
        + tuple(cls_grads[:6])
        + (cls_grads[6].reshape(-1), cls_grads[7])
    )


def solution(mesh):
    return jax.shard_map(
        per_device,
        mesh=mesh,
        in_specs=(
            P(("dp", "fsdp"), None),
            P(("dp", "fsdp")),
            P(("dp", "fsdp"), None),
            P(("dp", "fsdp"), None),
            P(("dp", "fsdp"), None),
            P(("dp", "fsdp"), None),
            P(("dp", "fsdp"), None),
            P(None, ("dp", "fsdp")),
            P(None, ("dp", "fsdp")),
            P(("dp", "fsdp")),
            P(("dp", "fsdp"), None),
            P(("dp", "fsdp"), None),
            P(("dp", "fsdp"), None),
            P(("dp", "fsdp"), None),
            P(None, ("dp", "fsdp")),
            P(None, ("dp", "fsdp")),
            P(("dp", "fsdp")),
            P(None, ("dp", "fsdp")),
        ),
        out_specs=(
            P(("dp", "fsdp"), None),
            P(),
            P(("dp", "fsdp"), None),
            P(("dp", "fsdp"), None),
            P(("dp", "fsdp"), None),
            P(("dp", "fsdp"), None),
            P(("dp", "fsdp"), None),
            P(None, ("dp", "fsdp")),
            P(None, ("dp", "fsdp")),
            P(("dp", "fsdp")),
            P(("dp", "fsdp"), None),
            P(("dp", "fsdp"), None),
            P(("dp", "fsdp"), None),
            P(("dp", "fsdp"), None),
            P(None, ("dp", "fsdp")),
            P(None, ("dp", "fsdp")),
            P(("dp", "fsdp")),
            P(None, ("dp", "fsdp")),
        ),
        check_vma=False,
    )
```

time: 601 us -> 423 us (0.70)
  Pallas kernels: 0 us -> 134 us
  matrix products: 90.7 us -> 0 us
  other arithmetic: 103 us -> 33.1 us
  local copies, waits for them, and re-layouts: 99.8 us -> 44.2 us
  waiting for transfers between devices: 163 us -> 116 us
  starting transfers between devices: 107 us -> 60.4 us
  between operations: 23.6 us -> 16.4 us
  blocking collectives: 5.63 us -> 12.5 us
    pallas_call x0 -> x12, Pallas kernels: none -> 134 us  [call(): pl.pallas_call(body, out_shape=tuple((jax.ShapeDtypeStruct(c.shape, c.dty...]
    dot_general x38 -> x0, matrix products: 90.7 us -> none  [the longest x2 22.9 us: finish_forward(): jnp.dot(first_low, weights[2], preferred_element_type=jnp.float32)]
    select_n x32 -> x12, other arithmetic: 49.3 us -> 0.34 us  [the longest x5 0.17 us: pair(): keep = jnp.where(self.even, left, right)]
    ppermute x63 -> x56, waiting for transfers between devices: 161 us -> 116 us  [send(): return lax.ppermute(value, AXES, self.pairs(axis, step))]
    ppermute x63 -> x56, starting transfers between devices: 87.3 us -> 60.3 us  [send(): return lax.ppermute(value, AXES, self.pairs(axis, step))]
    ppermute x5 -> x0, starting transfers between devices: 16.6 us -> none  [total(): value = value + lax.ppermute(value, AXES, swap)]
    convert_element_type x15 -> x0, local copies, waits for them, and re-layouts: 12.3 us -> none  [the longest x2 3.62 us: finish_forward(): hidden_pre = jnp.dot(first_low, weights[2], preferred_element_type=jnp.fl...]
    reduce_sum x22 -> x2, other arithmetic: 9.55 us -> 0.8 us  [the longest x1 0.77 us: per_device(): token_count = jnp.sum(small[1][:, at:at + windows].astype(jnp.float32))]
  transfers between devices with their start and end apart: 70 -> 58, of which waited for: 28 -> 18; matrix products, arithmetic and copies ran while one was open for 26% -> 8% of each run, Pallas kernels for 0% -> 27%
where the time goes in v2:
time: 423 us; the launch traced here: 417 us
  Pallas kernels  134 us (32%)
  waiting for transfers between devices  116 us (27%)
  starting transfers between devices  60.4 us (14%)
  local copies, waits for them, and re-layouts  44.2 us (10%)
  other arithmetic  33.1 us (8%)
  between operations  16.4 us (4%)
  blocking collectives  12.5 us (3%)
    pallas_call x12, Pallas kernels, call(): pl.pallas_call(body, out_shape=tuple((jax.ShapeDtypeStruct(c.shape, c.dty...  134 us
    ppermute x56, waiting for transfers between devices, send(): return lax.ppermute(value, AXES, self.pairs(axis, step))  116 us
    ppermute x56, starting transfers between devices, send(): return lax.ppermute(value, AXES, self.pairs(axis, step))  60.3 us
    unnamed x186, local copies, waits for them, and re-layouts  34.2 us
    convert_element_type x12, other arithmetic, total(): return made.astype(jnp.bfloat16)  14.5 us
  transfers between devices with their start and end apart: 58, of which 18 were waited for; matrix products, arithmetic and copies ran while one was open for 8% of the time, Pallas kernels for 27%

profile of v2, /device:TPU:0, one launch (start us, length us, event | category | flops | bytes accessed | tf_op | source)
XLA Modules:
  0.0 417.4 jit_solution(7623425971342925272)
XLA Ops:
  19.0 4.7 %collective-permute-start.1 = (bf16[48,1280]{1,0:T(8,128)(2,1)S(1)}, bf16[48,1280]{1,0:T(8,128)(2,1)S(1)}, u32[]{:S(2)}, u32[]{:S(2)}) collective-permute-start(bf16[48,1280]{1,0:T(8,128)(2,1)S(1)} %maximum_select_fusion.6), channel_id=1, source_target_pairs={{0,24},{1,25},{2,26},{3,27},{4,28},{5,29},{6,30},{7,31},{8,0},{9,1... | collective-permute-start | bytes 368648 | tf_op jit(solution)/shard_map/ppermute | solution.py:60
  27.4 7.9 %collective-permute-done.2 = bf16[48,1280]{1,0:T(8,128)(2,1)S(1)} collective-permute-done((bf16[48,1280]{1,0:T(8,128)(2,1)S(1)}, bf16[48,1280]{1,0:T(8,128)(2,1)S(1)}, u32[]{:S(2)}, u32[]{:S(2)}) %collective-permute-start.2) | collective-permute-done | bytes 122912 | tf_op jit(solution)/shard_map/ppermute | solution.py:60
  45.1 11.1 %collective-permute-done.8 = bf16[48,1920]{1,0:T(8,128)(2,1)S(1)} collective-permute-done((bf16[48,1920]{1,0:T(8,128)(2,1)S(1)}, bf16[48,1920]{1,0:T(8,128)(2,1)S(1)}, u32[]{:S(2)}, u32[]{:S(2)}) %collective-permute-start.8) | collective-permute-done | bytes 184352 | tf_op jit(solution)/shard_map/ppermute | solution.py:60
  62.8 7.3 %collective-permute-done.15 = bf16[192,384]{1,0:T(8,128)(2,1)S(1)} collective-permute-done((bf16[192,384]{1,0:T(8,128)(2,1)S(1)}, bf16[192,384]{1,0:T(8,128)(2,1)S(1)}, u32[]{:S(2)}, u32[]{:S(2)}) %collective-permute-start.15) | collective-permute-done | bytes 147488 | tf_op jit(solution)/shard_map/ppermute | solution.py:60
  70.1 6.2 %collective-permute-start.17 = (bf16[192,384]{1,0:T(8,128)(2,1)S(1)}, bf16[192,384]{1,0:T(8,128)(2,1)S(1)}, u32[]{:S(2)}, u32[]{:S(2)}) collective-permute-start(bf16[192,384]{1,0:T(8,128)(2,1)S(1)} %maximum_select_fusion.3), channel_id=1, source_target_pairs={{0,8},{1,9},{2,10},{3,11},{4,12},{5,13},{6,14},{7,15},{8,16},{9,17... | collective-permute-start | bytes 442376 | tf_op jit(solution)/shard_map/ppermute | solution.py:60
  76.3 8.6 %collective-permute-done.16 = bf16[192,384]{1,0:T(8,128)(2,1)S(1)} collective-permute-done((bf16[192,384]{1,0:T(8,128)(2,1)S(1)}, bf16[192,384]{1,0:T(8,128)(2,1)S(1)}, u32[]{:S(2)}, u32[]{:S(2)}) %collective-permute-start.16) | collective-permute-done | bytes 147488 | tf_op jit(solution)/shard_map/ppermute | solution.py:60
  93.1 19.8 %collective-permute-done.25.refs_8_.refs_19_.refs_27_ = bf16[768,384]{1,0:T(8,128)(2,1)S(1)} collective-permute-done((bf16[768,384]{1,0:T(8,128)(2,1)S(1)}, bf16[768,384]{1,0:T(8,128)(2,1)S(1)}, u32[]{:S(2)}, u32[]{:S(2)}) %collective-permute-start.25) | collective-permute-done | bytes 589856 | tf_op jit(solution)/shard_map/ppermute | solution.py:60
  112.8 2.6 collective-permute-done.26.refs_9_.refs_20_.refs_28_
  115.5 6.4 %collective-permute-start.27 = (bf16[192,1920]{1,0:T(8,128)(2,1)}, bf16[192,1920]{1,0:T(8,128)(2,1)}, u32[]{:S(2)}, u32[]{:S(2)}) collective-permute-start(bf16[192,1920]{1,0:T(8,128)(2,1)} %collective-permute-done.24.refs_8_.refs_13_.refs_21_), channel_id=1, source_target_pairs={{0,1},{1,0},{2,3},{3,2},{4,5},{5,4},{6,7},{7,6},{8,9},{9,8},{10,11... | collective-permute-start | bytes 2211848 | tf_op jit(solution)/shard_map/ppermute | solution.py:60
  133.0 9.3 %seg_attention.1 = (bf16[512,2304]{1,0:T(8,128)(2,1)S(1)}, bf16[512,768]{1,0:T(8,128)(2,1)S(1)}, bf16[2,768,128]{2,1,0:T(8,128)(2,1)S(1)}, f32[2,128,768]{2,1,0:T(8,128)S(1)}, f32[8,768]{1,0:T(8,128)S(1)}) custom-call(s32[6]{0:T(128)S(1)} %stack.27.refs_0_, f32[512,768]{1,0:T(8,128)S(1)} %copy-done.17, s32[512,1]{1,0:T(8,128)S(1)} %copy.108.refs_2_.refs_4_, ...), custom_call_target="tpu_custom_call" | custom-call | flops 1811939328 | bytes 9859072 | tf_op jit(solution)/shard_map/seg_attention/pallas_call | solution.py:439
  153.0 16.1 %seg_inner.1 = (f32[512,768]{1,0:T(8,128)S(1)}, f32[512,1]{1,0:T(8,128)S(1)}, bf16[512,768]{1,0:T(8,128)(2,1)S(1)}, bf16[512,3072]{1,0:T(8,128)(2,1)S(1)}, bf16[...) custom-call(s32[6]{0:T(128)S(1)} %stack.27.refs_0_, ...), custom_call_target="tpu_custom_call" | custom-call | flops 3019898880 | bytes 17930240 | tf_op jit(solution)/shard_map/seg_inner/pallas_call | solution.py:439
  171.9 11.7 %seg_outer.1 = (f32[512,768]{1,0:T(8,128)}, f32[8,768]{1,0:T(8,128)S(1)}, f32[512,768]{1,0:T(8,128)S(1)}, f32[512,1]{1,0:T(8,128)S(1)}, f32[8,768]{1,0:T(8,128)S...) custom-call(s32[6]{0:T(128)S(1)} %stack.27.refs_0_, ...), custom_call_target="tpu_custom_call" | custom-call | flops 2415919104 | bytes 15022148 | tf_op jit(solution)/shard_map/seg_outer/pallas_call | solution.py:439
  185.8 21.6 %seg_feed_back.1 = (bf16[512,768]{1,0:T(8,128)(2,1)}, bf16[512,3072]{1,0:T(8,128)(2,1)}, bf16[512,768]{1,0:T(8,128)(2,1)}, bf16[512,768]{1,0:T(8,128)(2,1)}, f32...) custom-call(s32[6]{0:T(128)S(1)} %stack.27.refs_0_, f32[512,768]{1,0:T(8,128)} %get-tuple-element.173.refs_1_.refs_34_, ...), custom_call_target="tpu_custom_call" | custom-call | flops 5435817984 | bytes 27961344 | tf_op jit(solution)/shard_map/seg_feed_back/pallas_call | solution.py:439
  208.6 7.4 %weight_grads.4 = (bf16[3072,384]{1,0:T(8,128)(2,1)S(1)}, bf16[3072,384]{1,0:T(8,128)(2,1)S(1)}) custom-call(s32[6]{0:T(128)S(1)} %stack.27.refs_0_, bf16[512,3072]{1,0:T(8,128)(2,1)S(1)} %get-tuple-element.170.refs_3_.refs_1_, bf16[512,768]{1,0:T(8,128)(2,1)S(1)} %copy-done.62), custom_call_target="tpu_custom_call" | custom-call | flops 2415919104 | bytes 8650752 | tf_op jit(solution)/shard_map/weight_grads/pallas_call | solution.py:439
  216.2 8.1 %weight_grads.3 = (bf16[768,1920]{1,0:T(8,128)(2,1)S(1)}, bf16[768,1920]{1,0:T(8,128)(2,1)}) custom-call(s32[6]{0:T(128)S(1)} %stack.27.refs_0_, bf16[512,768]{1,0:T(8,128)(2,1)S(1)} %copy-done.65, bf16[512,768]{1,0:T(8,128)(2,1)S(1)} %copy-done.61, bf16[512,768]{1,0:T(8,128)(2,1)S(1)} %copy-done.67, bf16[512,3072]{1,0:T(8,128)(2,1)S(1)} %copy-done.58), custom_call_target="tpu_custom_call" | custom-call | flops 3019898880 | bytes 11403264 | tf_op jit(solution)/shard_map/weight_grads/pallas_call | solution.py:439
  232.4 4.5 %cls_project.1.refs_2_ = f32[8,2304]{1,0:T(8,128)} custom-call(s32[6]{0:T(128)} %copy-done.49, f32[8,768]{1,0:T(8,128)} %copy-done.46, f32[2,128,768]{2,1,0:T(8,128)} %copy-done, bf16[1536,4608]{1,0:T(8,128)(2,1)} %all-gather.4.cloned.1.call-done.refs_3_.refs_9_.refs_17_), custom_call_target="tpu_custom_call" | custom-call | flops 28311552 | bytes 15040512 | tf_op jit(solution)/shard_map/cls_project/pallas_call | solution.py:439
  237.7 6.0 %all-gather = bf16[4,4,1536]{2,1,0:T(4,128)(2,1)S(1)} all-gather(bf16[1,4,1536]{2,1,0:T(4,128)(2,1)S(1)} %fusion.5), channel_id=1, replica_groups=mesh['dp'=8,'fsdp'=4] {'fsdp'}, dimensions={0}, use_global_device_ids=true | all-gather | bytes 61440 | tf_op jit(solution)/shard_map/all_gather | solution.py:1440
  244.4 12.5 %cls_middle.1 = (f32[8,768]{1,0:T(8,128)}, f32[8,768]{1,0:T(8,128)}, bf16[16,1536]{1,0:T(8,128)(2,1)}, f32[8,768]{1,0:T(8,128)}, f32[8,4608]{1,0:T(8,128)}, /*index=5*/f32[8,5504]{1,0:T(8,128)}) custom-call(s32[6]{0:T(128)} %copy-done.49, f32[8,768]{1,0:T(8,128)} %copy-done.46, f32[8,2304]{1,0:T(8,128)} %cls_project.1.refs_2_, ...), custom_call_target="tpu_custom_call" | custom-call | flops 169869312 | bytes 15573028 | tf_op jit(solution)/shard_map/cls_middle/pallas_call | solution.py:439
  257.8 6.5 %all_to_all.11 = bf16[4,4,1536]{2,1,0:T(4,128)(2,1)S(1)} all-to-all(bf16[4,4,1536]{2,1,0:T(4,128)(2,1)S(1)} %all_to_all.7), channel_id=1, replica_groups=mesh['dp'=8,'fsdp'=4] {'fsdp'}, dimensions={0} | all-to-all | bytes 98304 | tf_op jit(solution)/shard_map/all_to_all | solution.py:1456
  264.9 11.8 %cls_finish.1 = (f32[512,768]{1,0:T(8,128)}, bf16[512,768]{1,0:T(8,128)(2,1)}, f32[512,768]{1,0:T(8,128)}, bf16[8,12288]{1,0:T(8,128)(2,1)}, f32[8,768]{1,0:T(8,128)}, /*index=5*/f32[1,3072]{1,0:T(1,128)}) custom-call(s32[6]{0:T(128)} %copy-done.49, ...), custom_call_target="tpu_custom_call", output_to_operand_aliasing={{0}: (34, {}), {1}: (35, {}), {2}: (36, {})} | custom-call | flops 113246208 | bytes 26558528 | tf_op jit(solution)/shard_map/cls_finish/pallas_call | solution.py:439
  282.6 15.8 %collective-permute-done.38 = bf16[768,384]{1,0:T(8,128)(2,1)S(1)} collective-permute-done((bf16[768,384]{1,0:T(8,128)(2,1)S(1)}, bf16[768,384]{1,0:T(8,128)(2,1)S(1)}, u32[]{:S(2)}, u32[]{:S(2)}) %collective-permute-start.38) | collective-permute-done | bytes 589856 | tf_op jit(solution)/shard_map/ppermute | solution.py:60
  302.7 2.8 collective-permute-start.41
  305.6 17.8 %seg_attention_back.1 = (bf16[512,2304]{1,0:T(8,128)(2,1)S(1)}, f32[512,768]{1,0:T(8,128)}, f32[2,8,768]{2,1,0:T(8,128)S(1)}) custom-call(s32[6]{0:T(128)S(1)} %copy-done.50, bf16[512,2304]{1,0:T(8,128)(2,1)S(1)} %copy-done.11, bf16[512,768]{1,0:T(8,128)(2,1)S(1)} %copy-done.9, f32[512,768]{1,0:T(8,128)S(1)} %copy-done.2, s32[512,1]{1,0:T(8,128)S(1)} %copy-done.23, ...), custom_call_target="tpu_custom_call" | custom-call | flops 1811939328 | bytes 12636160 | tf_op jit(solution)/shard_map/seg_attention_back/pallas_call | solution.py:439
  325.0 2.8 add_convert_fusion.3
  333.4 5.0 %weight_grads.5 = (bf16[768,1280]{1,0:T(8,128)(2,1)S(1)}, bf16[768,1280]{1,0:T(8,128)(2,1)S(1)}) custom-call(s32[6]{0:T(128)S(1)} %copy-done.50, bf16[512,768]{1,0:T(8,128)(2,1)S(1)} %copy-done.24, bf16[512,2304]{1,0:T(8,128)(2,1)S(1)} %copy-done.60, f32[16,768]{1,0:T(8,128)S(1)} %concatenate.125.refs_3_), custom_call_target="tpu_custom_call" | custom-call | flops 2013265920 | bytes 7127040 | tf_op jit(solution)/shard_map/weight_grads/pallas_call | solution.py:439
  338.4 10.7 %collective-permute-done.44 = bf16[192,1920]{1,0:T(8,128)(2,1)} collective-permute-done((bf16[192,1920]{1,0:T(8,128)(2,1)}, bf16[192,1920]{1,0:T(8,128)(2,1)}, u32[]{:S(2)}, u32[]{:S(2)}) %collective-permute-start.44) | collective-permute-done | bytes 737312 | tf_op jit(solution)/shard_map/ppermute | solution.py:60
  357.9 3.2 collective-permute-done.52
  361.1 7.3 %collective-permute-done.53 = bf16[48,1920]{1,0:T(8,128)(2,1)S(1)} collective-permute-done((bf16[48,1920]{1,0:T(8,128)(2,1)S(1)}, bf16[48,1920]{1,0:T(8,128)(2,1)S(1)}, u32[]{:S(2)}, u32[]{:S(2)}) %collective-permute-start.53) | collective-permute-done | bytes 184352 | tf_op jit(solution)/shard_map/ppermute | solution.py:60
  371.3 8.1 %collective-permute-done.47 = bf16[192,1280]{1,0:T(8,128)(2,1)S(1)} collective-permute-done((bf16[192,1280]{1,0:T(8,128)(2,1)S(1)}, bf16[192,1280]{1,0:T(8,128)(2,1)S(1)}, u32[]{:S(2)}, u32[]{:S(2)}) %collective-permute-start.47) | collective-permute-done | bytes 491552 | tf_op jit(solution)/shard_map/ppermute | solution.py:60
  379.7 3.5 collective-permute-start.48
  388.3 4.2 %collective-permute-done.49 = bf16[48,1280]{1,0:T(8,128)(2,1)S(1)} collective-permute-done((bf16[48,1280]{1,0:T(8,128)(2,1)S(1)}, bf16[48,1280]{1,0:T(8,128)(2,1)S(1)}, u32[]{:S(2)}, u32[]{:S(2)}) %collective-permute-start.49) | collective-permute-done | bytes 122912 | tf_op jit(solution)/shard_map/ppermute | solution.py:60
  396.9 8.4 %cls_weight_grads.1 = (f32[24,2304]{1,0:T(8,128)}, f32[24,768]{1,0:T(8,128)}, f32[24,3072]{1,0:T(8,128)}, f32[96,768]{1,0:T(8,128)}, f32[2,24]{1,0:T(2,128)}, /*...) custom-call(s32[6]{0:T(128)} %copy-done.49, ...), custom_call_target="tpu_custom_call" | custom-call | flops 327680000 | bytes 7842436 | tf_op jit(solution)/shard_map/cls_weight_grads/pallas_call | solution.py:439
  (388 shorter events, 121.1 us)
Async XLA Ops:
  7.2 225.2 %all-gather.4.cloned.1.call-start = ((), (), s32[]{:S(2)}) async-start(), calls=%async_computation.1 | async-start | bytes 14598144 | tf_op jit(solution)/shard_map/all_gather | solution.py:164
  35.3 20.9 %collective-permute-start.5 = (bf16[192,1280]{1,0:T(8,128)(2,1)S(1)}, bf16[192,1280]{1,0:T(8,128)(2,1)S(1)}, u32[]{:S(2)}, u32[]{:S(2)}) collective-permute-start(bf16[192,1280]{1,0:T(8,128)(2,1)S(1)} %pad_maximum_fusion.refs_4_.refs_6_), channel_id=1, source_target_pairs={{0,4},{1,3},{2,6},{3,1},{4,0},{5,7},{6,2},{7,5},{8,12},{9,11},{10,... | collective-permute-start | bytes 1474568 | tf_op jit(solution)/shard_map/ppermute | solution.py:60
  36.9 19.3 %collective-permute-start.6 = (bf16[192,1280]{1,0:T(8,128)(2,1)S(1)}, bf16[192,1280]{1,0:T(8,128)(2,1)S(1)}, u32[]{:S(2)}, u32[]{:S(2)}) collective-permute-start(bf16[192,1280]{1,0:T(8,128)(2,1)S(1)} %pad_maximum_fusion.refs_4_.refs_6_), channel_id=1, source_target_pairs={{0,2},{1,5},{2,0},{3,7},{4,6},{5,1},{6,4},{7,3},{8,10},{9,13},{10,... | collective-permute-start | bytes 1474568 | tf_op jit(solution)/shard_map/ppermute | solution.py:60
  39.7 16.5 %collective-permute-start.8 = (bf16[48,1920]{1,0:T(8,128)(2,1)S(1)}, bf16[48,1920]{1,0:T(8,128)(2,1)S(1)}, u32[]{:S(2)}, u32[]{:S(2)}) collective-permute-start(bf16[48,1920]{1,0:T(8,128)(2,1)S(1)} %maximum_select_fusion.1), channel_id=1, source_target_pairs={{0,16},{1,17},{2,18},{3,19},{4,20},{5,21},{6,22},{7,23},{8,24},{9,... | collective-permute-start | bytes 552968 | tf_op jit(solution)/shard_map/ppermute | solution.py:60
  40.8 15.4 %collective-permute-start.9 = (bf16[48,1920]{1,0:T(8,128)(2,1)S(1)}, bf16[48,1920]{1,0:T(8,128)(2,1)S(1)}, u32[]{:S(2)}, u32[]{:S(2)}) collective-permute-start(bf16[48,1920]{1,0:T(8,128)(2,1)S(1)} %maximum_select_fusion.1), channel_id=1, source_target_pairs={{0,8},{1,9},{2,10},{3,11},{4,12},{5,13},{6,14},{7,15},{8,16},{9,17... | collective-permute-start | bytes 552968 | tf_op jit(solution)/shard_map/ppermute | solution.py:60
  56.2 340.6 %all-gather.6.cloned.1.call-start = ((), (), s32[]{:S(2)}) async-start(), calls=%async_computation.2 | async-start | bytes 6488064 | tf_op jit(solution)/shard_map/all_gather | solution.py:1474
  59.2 26.3 %collective-permute-start.13 = (bf16[192,1920]{1,0:T(8,128)(2,1)}, bf16[192,1920]{1,0:T(8,128)(2,1)}, u32[]{:S(2)}, u32[]{:S(2)}) collective-permute-start(bf16[192,1920]{1,0:T(8,128)(2,1)} %constant_dynamic-update-slice_fusion.refs_5_.refs_10_.refs_18_), channel_id=1, source_target_pairs={{0,4},{1,3},{2,6},{3,1},{4,0},{5,7},{6,2},{7,5},{8,12},{9,11},{10,... | collective-permute-start | bytes 2211848 | tf_op jit(solution)/shard_map/ppermute | solution.py:60
  59.7 25.7 %collective-permute-start.14 = (bf16[192,1920]{1,0:T(8,128)(2,1)}, bf16[192,1920]{1,0:T(8,128)(2,1)}, u32[]{:S(2)}, u32[]{:S(2)}) collective-permute-start(bf16[192,1920]{1,0:T(8,128)(2,1)} %constant_dynamic-update-slice_fusion.refs_5_.refs_10_.refs_18_), channel_id=1, source_target_pairs={{0,2},{1,5},{2,0},{3,7},{4,6},{5,1},{6,4},{7,3},{8,10},{9,13},{10,... | collective-permute-start | bytes 2211848 | tf_op jit(solution)/shard_map/ppermute | solution.py:60
  60.2 25.2 %collective-permute-start.12 = (bf16[192,1280]{1,0:T(8,128)(2,1)S(1)}, bf16[192,1280]{1,0:T(8,128)(2,1)S(1)}, u32[]{:S(2)}, u32[]{:S(2)}) collective-permute-start(bf16[192,1280]{1,0:T(8,128)(2,1)S(1)} %collective-permute-done.5.refs_5_.refs_7_), channel_id=1, source_target_pairs={{0,2},{1,5},{2,0},{3,7},{4,6},{5,1},{6,4},{7,3},{8,10},{9,13},{10,... | collective-permute-start | bytes 1474568 | tf_op jit(solution)/shard_map/ppermute | solution.py:60
  61.8 23.1 %collective-permute-start.16 = (bf16[192,384]{1,0:T(8,128)(2,1)S(1)}, bf16[192,384]{1,0:T(8,128)(2,1)S(1)}, u32[]{:S(2)}, u32[]{:S(2)}) collective-permute-start(bf16[192,384]{1,0:T(8,128)(2,1)S(1)} %maximum_select_fusion.3), channel_id=1, source_target_pairs={{0,16},{1,17},{2,18},{3,19},{4,20},{5,21},{6,22},{7,23},{8,24},{9,... | collective-permute-start | bytes 442376 | tf_op jit(solution)/shard_map/ppermute | solution.py:60
  70.1 14.9 %collective-permute-start.17 = (bf16[192,384]{1,0:T(8,128)(2,1)S(1)}, bf16[192,384]{1,0:T(8,128)(2,1)S(1)}, u32[]{:S(2)}, u32[]{:S(2)}) collective-permute-start(bf16[192,384]{1,0:T(8,128)(2,1)S(1)} %maximum_select_fusion.3), channel_id=1, source_target_pairs={{0,8},{1,9},{2,10},{3,11},{4,12},{5,13},{6,14},{7,15},{8,16},{9,17... | collective-permute-start | bytes 442376 | tf_op jit(solution)/shard_map/ppermute | solution.py:60
  85.5 30.0 %collective-permute-start.24 = (bf16[192,1920]{1,0:T(8,128)(2,1)}, bf16[192,1920]{1,0:T(8,128)(2,1)}, u32[]{:S(2)}, u32[]{:S(2)}) collective-permute-start(bf16[192,1920]{1,0:T(8,128)(2,1)} %collective-permute-done.13.refs_6_.refs_11_.refs_19_), channel_id=1, source_target_pairs={{0,2},{1,5},{2,0},{3,7},{4,6},{5,1},{6,4},{7,3},{8,10},{9,13},{10,... | collective-permute-start | bytes 2211848 | tf_op jit(solution)/shard_map/ppermute | solution.py:60
  86.1 26.7 %collective-permute-start.25 = (bf16[768,384]{1,0:T(8,128)(2,1)S(1)}, bf16[768,384]{1,0:T(8,128)(2,1)S(1)}, u32[]{:S(2)}, u32[]{:S(2)}) collective-permute-start(bf16[768,384]{1,0:T(8,128)(2,1)S(1)} %constant_dynamic-update-slice_fusion.4.refs_7_.refs_18_.refs_26_), channel_id=1, source_target_pairs={{0,4},{1,3},{2,6},{3,1},{4,0},{5,7},{6,2},{7,5},{8,12},{9,11},{10,... | collective-permute-start | bytes 1769480 | tf_op jit(solution)/shard_map/ppermute | solution.py:60
  87.6 27.9 %collective-permute-start.26 = (bf16[768,384]{1,0:T(8,128)(2,1)S(1)}, bf16[768,384]{1,0:T(8,128)(2,1)S(1)}, u32[]{:S(2)}, u32[]{:S(2)}) collective-permute-start(bf16[768,384]{1,0:T(8,128)(2,1)S(1)} %constant_dynamic-update-slice_fusion.4.refs_7_.refs_18_.refs_26_), channel_id=1, source_target_pairs={{0,2},{1,5},{2,0},{3,7},{4,6},{5,1},{6,4},{7,3},{8,10},{9,13},{10,... | collective-permute-start | bytes 1769480 | tf_op jit(solution)/shard_map/ppermute | solution.py:60
  91.7 55.9 %collective-permute-start.11 = (bf16[192,1920]{1,0:T(8,128)(2,1)}, bf16[192,1920]{1,0:T(8,128)(2,1)}, u32[]{:S(2)}, u32[]{:S(2)}) collective-permute-start(bf16[192,1920]{1,0:T(8,128)(2,1)} %constant_dynamic-update-slice_fusion.refs_5_.refs_10_.refs_18_), channel_id=1, source_target_pairs={{0,1},{1,0},{2,3},{3,2},{4,5},{5,4},{6,7},{7,6},{8,9},{9,8},{10,11... | collective-permute-start | bytes 2211848 | tf_op jit(solution)/shard_map/ppermute | solution.py:60
  92.7 55.0 %collective-permute-start.18 = (bf16[192,1920]{1,0:T(8,128)(2,1)}, bf16[192,1920]{1,0:T(8,128)(2,1)}, u32[]{:S(2)}, u32[]{:S(2)}) collective-permute-start(bf16[192,1920]{1,0:T(8,128)(2,1)} %collective-permute-done.13.refs_6_.refs_11_.refs_19_), channel_id=1, source_target_pairs={{0,1},{1,0},{2,3},{3,2},{4,5},{5,4},{6,7},{7,6},{8,9},{9,8},{10,11... | collective-permute-start | bytes 2211848 | tf_op jit(solution)/shard_map/ppermute | solution.py:60
  112.8 35.4 %collective-permute-start.19 = (bf16[192,1920]{1,0:T(8,128)(2,1)}, bf16[192,1920]{1,0:T(8,128)(2,1)}, u32[]{:S(2)}, u32[]{:S(2)}) collective-permute-start(bf16[192,1920]{1,0:T(8,128)(2,1)} %collective-permute-done.14.refs_7_.refs_12_.refs_20_), channel_id=1, source_target_pairs={{0,1},{1,0},{2,3},{3,2},{4,5},{5,4},{6,7},{7,6},{8,9},{9,8},{10,11... | collective-permute-start | bytes 2211848 | tf_op jit(solution)/shard_map/ppermute | solution.py:60
  115.5 32.8 %collective-permute-start.27 = (bf16[192,1920]{1,0:T(8,128)(2,1)}, bf16[192,1920]{1,0:T(8,128)(2,1)}, u32[]{:S(2)}, u32[]{:S(2)}) collective-permute-start(bf16[192,1920]{1,0:T(8,128)(2,1)} %collective-permute-done.24.refs_8_.refs_13_.refs_21_), channel_id=1, source_target_pairs={{0,1},{1,0},{2,3},{3,2},{4,5},{5,4},{6,7},{7,6},{8,9},{9,8},{10,11... | collective-permute-start | bytes 2211848 | tf_op jit(solution)/shard_map/ppermute | solution.py:60
  122.1 26.2 %collective-permute-start.28 = (bf16[768,384]{1,0:T(8,128)(2,1)S(1)}, bf16[768,384]{1,0:T(8,128)(2,1)S(1)}, u32[]{:S(2)}, u32[]{:S(2)}) collective-permute-start(bf16[768,384]{1,0:T(8,128)(2,1)S(1)} %collective-permute-done.25.refs_8_.refs_19_.refs_27_), channel_id=1, source_target_pairs={{0,2},{1,5},{2,0},{3,7},{4,6},{5,1},{6,4},{7,3},{8,10},{9,13},{10,... | collective-permute-start | bytes 1769480 | tf_op jit(solution)/shard_map/ppermute | solution.py:60
  147.6 24.2 %collective-permute-start.29 = (bf16[768,384]{1,0:T(8,128)(2,1)S(1)}, bf16[768,384]{1,0:T(8,128)(2,1)}, u32[]{:S(2)}, u32[]{:S(2)}) collective-permute-start(bf16[768,384]{1,0:T(8,128)(2,1)S(1)} %constant_dynamic-update-slice_fusion.4.refs_7_.refs_18_.refs_26_), channel_id=1, source_target_pairs={{0,1},{1,0},{2,3},{3,2},{4,5},{5,4},{6,7},{7,6},{8,9},{9,8},{10,11... | collective-permute-start | bytes 1769480 | tf_op jit(solution)/shard_map/ppermute | solution.py:60
  147.7 24.1 %collective-permute-start.30 = (bf16[768,384]{1,0:T(8,128)(2,1)S(1)}, bf16[768,384]{1,0:T(8,128)(2,1)}, u32[]{:S(2)}, u32[]{:S(2)}) collective-permute-start(bf16[768,384]{1,0:T(8,128)(2,1)S(1)} %collective-permute-done.25.refs_8_.refs_19_.refs_27_), channel_id=1, source_target_pairs={{0,1},{1,0},{2,3},{3,2},{4,5},{5,4},{6,7},{7,6},{8,9},{9,8},{10,11... | collective-permute-start | bytes 1769480 | tf_op jit(solution)/shard_map/ppermute | solution.py:60
  148.2 23.6 %collective-permute-start.31 = (bf16[768,384]{1,0:T(8,128)(2,1)S(1)}, bf16[768,384]{1,0:T(8,128)(2,1)}, u32[]{:S(2)}, u32[]{:S(2)}) collective-permute-start(bf16[768,384]{1,0:T(8,128)(2,1)S(1)} %collective-permute-done.26.refs_9_.refs_20_.refs_28_), channel_id=1, source_target_pairs={{0,1},{1,0},{2,3},{3,2},{4,5},{5,4},{6,7},{7,6},{8,9},{9,8},{10,11... | collective-permute-start | bytes 1769480 | tf_op jit(solution)/shard_map/ppermute | solution.py:60
  148.3 23.6 %collective-permute-start.32 = (bf16[768,384]{1,0:T(8,128)(2,1)S(1)}, bf16[768,384]{1,0:T(8,128)(2,1)}, u32[]{:S(2)}, u32[]{:S(2)}) collective-permute-start(bf16[768,384]{1,0:T(8,128)(2,1)S(1)} %collective-permute-done.28.refs_10_.refs_21_.refs_29_), channel_id=1, source_target_pairs={{0,1},{1,0},{2,3},{3,2},{4,5},{5,4},{6,7},{7,6},{8,9},{9,8},{10,11... | collective-permute-start | bytes 1769480 | tf_op jit(solution)/shard_map/ppermute | solution.py:60
  226.2 30.7 %collective-permute-start.37 = (bf16[1536,384]{1,0:T(8,128)(2,1)}, bf16[1536,384]{1,0:T(8,128)(2,1)}, u32[]{:S(2)}, u32[]{:S(2)}) collective-permute-start(bf16[1536,384]{1,0:T(8,128)(2,1)} %add_convert_fusion.1), channel_id=1, source_target_pairs={{0,2},{1,5},{2,0},{3,7},{4,6},{5,1},{6,4},{7,3},{8,10},{9,13},{10,... | collective-permute-start | bytes 3538952 | tf_op jit(solution)/shard_map/ppermute | solution.py:60
  278.7 46.2 %collective-permute-start.42 = (bf16[384,1920]{1,0:T(8,128)(2,1)S(1)}, bf16[384,1920]{1,0:T(8,128)(2,1)S(1)}, u32[]{:S(2)}, u32[]{:S(2)}) collective-permute-start(bf16[384,1920]{1,0:T(8,128)(2,1)S(1)} %add_convert_fusion), channel_id=1, source_target_pairs={{0,2},{1,5},{2,0},{3,7},{4,6},{5,1},{6,4},{7,3},{8,10},{9,13},{10,... | collective-permute-start | bytes 4423688 | tf_op jit(solution)/shard_map/ppermute | solution.py:60
  280.7 17.7 %collective-permute-start.38 = (bf16[768,384]{1,0:T(8,128)(2,1)S(1)}, bf16[768,384]{1,0:T(8,128)(2,1)S(1)}, u32[]{:S(2)}, u32[]{:S(2)}) collective-permute-start(bf16[768,384]{1,0:T(8,128)(2,1)S(1)} %add_convert_fusion.4), channel_id=1, source_target_pairs={{0,4},{1,3},{2,6},{3,1},{4,0},{5,7},{6,2},{7,5},{8,12},{9,11},{10,... | collective-permute-start | bytes 1769480 | tf_op jit(solution)/shard_map/ppermute | solution.py:60
  300.2 24.6 %collective-permute-start.39 = (bf16[192,384]{1,0:T(8,128)(2,1)S(1)}, bf16[192,384]{1,0:T(8,128)(2,1)S(1)}, u32[]{:S(2)}, u32[]{:S(2)}) collective-permute-start(bf16[192,384]{1,0:T(8,128)(2,1)S(1)} %get-tuple-element.373), channel_id=1, source_target_pairs={{0,8},{1,9},{2,10},{3,11},{4,12},{5,13},{6,14},{7,15},{8,16},{9,17... | collective-permute-start | bytes 442376 | tf_op jit(solution)/shard_map/ppermute | solution.py:60
  300.4 24.5 %collective-permute-start.40 = (bf16[192,384]{1,0:T(8,128)(2,1)S(1)}, bf16[192,384]{1,0:T(8,128)(2,1)S(1)}, u32[]{:S(2)}, u32[]{:S(2)}) collective-permute-start(bf16[192,384]{1,0:T(8,128)(2,1)S(1)} %get-tuple-element.372), channel_id=1, source_target_pairs={{0,16},{1,17},{2,18},{3,19},{4,20},{5,21},{6,22},{7,23},{8,24},{9,... | collective-permute-start | bytes 442376 | tf_op jit(solution)/shard_map/ppermute | solution.py:60
  302.7 22.3 %collective-permute-start.41 = (bf16[192,384]{1,0:T(8,128)(2,1)S(1)}, bf16[192,384]{1,0:T(8,128)(2,1)S(1)}, u32[]{:S(2)}, u32[]{:S(2)}) collective-permute-start(bf16[192,384]{1,0:T(8,128)(2,1)S(1)} %get-tuple-element.371), channel_id=1, source_target_pairs={{0,24},{1,25},{2,26},{3,27},{4,28},{5,29},{6,30},{7,31},{8,0},{9,1... | collective-permute-start | bytes 442376 | tf_op jit(solution)/shard_map/ppermute | solution.py:60
  327.8 21.3 %collective-permute-start.44 = (bf16[192,1920]{1,0:T(8,128)(2,1)}, bf16[192,1920]{1,0:T(8,128)(2,1)}, u32[]{:S(2)}, u32[]{:S(2)}) collective-permute-start(bf16[192,1920]{1,0:T(8,128)(2,1)} %add_convert_fusion.3), channel_id=1, source_target_pairs={{0,4},{1,3},{2,6},{3,1},{4,0},{5,7},{6,2},{7,5},{8,12},{9,11},{10,... | collective-permute-start | bytes 2211848 | tf_op jit(solution)/shard_map/ppermute | solution.py:60
  352.2 16.1 %collective-permute-start.53 = (bf16[48,1920]{1,0:T(8,128)(2,1)S(1)}, bf16[48,1920]{1,0:T(8,128)(2,1)S(1)}, u32[]{:S(2)}, u32[]{:S(2)}) collective-permute-start(bf16[48,1920]{1,0:T(8,128)(2,1)S(1)} %get-tuple-element.369), channel_id=1, source_target_pairs={{0,16},{1,17},{2,18},{3,19},{4,20},{5,21},{6,22},{7,23},{8,24},{9,... | collective-permute-start | bytes 552968 | tf_op jit(solution)/shard_map/ppermute | solution.py:60
  354.1 14.2 %collective-permute-start.54 = (bf16[48,1920]{1,0:T(8,128)(2,1)S(1)}, bf16[48,1920]{1,0:T(8,128)(2,1)S(1)}, u32[]{:S(2)}, u32[]{:S(2)}) collective-permute-start(bf16[48,1920]{1,0:T(8,128)(2,1)S(1)} %get-tuple-element.368), channel_id=1, source_target_pairs={{0,24},{1,25},{2,26},{3,27},{4,28},{5,29},{6,30},{7,31},{8,0},{9,1... | collective-permute-start | bytes 552968 | tf_op jit(solution)/shard_map/ppermute | solution.py:60
  (113 other events, 1701.4 us)
Sparse Core Ops, SparseCore 0:
  56.4 119.4 all-gather.3
  276.8 81.0 all-gather.5

commit v3 on v2

v3 whole, which is shorter than its diff:
```python
import jax
import jax.numpy as jnp
from jax import lax
from jax.experimental import pallas as pl
from jax.experimental.pallas import tpu as pltpu
from jax.sharding import PartitionSpec as P

HEAD = 64
SEG = 128
SMALL = 128
TABLE = 48

AXES = ("dp", "fsdp")


class Grid:
    def __init__(self, features):
        fsdp, dp = lax.axis_size("fsdp"), lax.axis_size("dp")
        self.ny = fsdp // 2
        self.nx = self.ny
        self.nz = dp // self.nx
        self.count = fsdp * dp
        me = lax.axis_index("dp")
        chip = lax.axis_index("fsdp")
        self.z, self.x = me // self.nx, me % self.nx
        self.y, self.core = chip // 2, chip % 2
        self.even = self.core == 0
        self.index = me * fsdp + chip
        self.pieces = self.nx == 2 and 2 * features // self.count % 16 == 0
        self.first = jnp.where(self.even, self.x, self.y)
        self.second = jnp.where(self.even, self.y, self.x)

    def pairs(self, axis, step):
        out = []
        for i in range(self.count):
            c, y = i % 2, i // 2 % self.ny
            x, z = i // (2 * self.ny) % self.nx, i // (2 * self.ny * self.nx)
            along = axis
            if axis == "first":
                along = "x" if c == 0 else "y"
            if axis == "second":
                along = "y" if c == 0 else "x"
            if along == "core":
                c = (c + step) % 2
            if along == "y":
                y = (y + step) % self.ny
            if along == "x":
                x = (x + step) % self.nx
            if along == "z":
                z = (z + step) % self.nz
            out.append((i, ((z * self.nx + x) * self.ny + y) * 2 + c))
        return out

    def size(self, axis):
        return {"core": 2, "z": self.nz}.get(axis, self.nx)

    def place(self, axis):
        return {"core": self.core, "z": self.z, "first": self.first, "second": self.second}[axis]

    def send(self, value, axis, step=1):
        return lax.ppermute(value, AXES, self.pairs(axis, step))

    def gather_axis(self, rows, axis):
        n, place = self.size(axis), self.place(axis)
        parts = [rows] + [self.send(rows, axis, n - k) for k in range(1, n)]
        if n == 1:
            return rows
        if n == 2:
            return jnp.where(
                place == 0, jnp.concatenate(parts), jnp.concatenate([parts[1], parts[0]])
            )
        ring = jnp.concatenate(parts + parts[:-1])
        step = rows.shape[0]
        return lax.dynamic_slice_in_dim(ring, (n - place) % n * step, n * step, 0)

    def scatter_axis(self, blocks, axis):
        n, place = self.size(axis), self.place(axis)
        total = lax.dynamic_index_in_dim(blocks, place, 0, keepdims=False).astype(jnp.float32)
        for k in range(1, n):
            block = lax.dynamic_index_in_dim(blocks, (place + k) % n, 0, keepdims=False)
            total = total + self.send(block, axis, k).astype(jnp.float32)
        return total.astype(jnp.bfloat16)

    def gather(self, ends):
        rows, half = ends[0].shape
        pair = self.pair(ends)
        mine = self.gather_axis(pair, "z")
        mine = self.gather_axis(mine, "first")
        mine = self.gather_axis(mine, "second")
        other = self.send(mine, "core")
        left = jnp.where(self.even, mine, other)
        right = jnp.where(self.even, other, mine)
        left = left.reshape(self.ny, self.nx, self.nz, 2 * rows, half).transpose(2, 1, 0, 3, 4)
        right = right.reshape(self.nx, self.ny, self.nz, 2 * rows, half).transpose(2, 0, 1, 3, 4)
        return (left.reshape(-1, half), right.reshape(-1, half))

    def pair(self, ends):
        keep, away = ends
        came = self.send(away, "core")
        return jnp.where(self.even, jnp.concatenate([keep, came]), jnp.concatenate([came, keep]))

    def along(self, rows):
        return [self.send(rows, "z", self.nz - k) for k in range(1, self.nz)]

    def line(self, rows, came):
        return jnp.concatenate([rows] + list(came))

    def plane(self, here):
        return (self.send(here, "first"), self.send(here, "second"))

    def swap(self, parts):
        return tuple(self.send(part, "core") for part in parts)

    def whole(self, ends, *widths):
        left, right = self.gather(ends)
        out, at = [], 0
        for width in widths:
            parts = [p[:, at : at + width] for p in (left, right)]
            out += parts if width == SMALL else [jnp.concatenate(parts, axis=1)]
            at += width
        return Group(self, out, None, widths)

    def grouped(self, mine, other, *widths):
        return Group(self, tuple(mine) + tuple(other), mine[0].shape[0] // self.nz, widths)

    def everything(self, near, widths, wide, after):
        near, wide = self.pair(near), self.pair(wide)
        rows = near.shape[0]
        stacks = [wide[at : at + rows] for at in range(0, wide.shape[0], rows)]
        unit = jnp.concatenate([near] + stacks, axis=1)
        unit, _ = sync((unit, after))
        unit = lax.all_gather(unit, AXES, axis=0, tiled=True)
        return (Whole(self, unit, rows, widths, near.shape[1], wide.shape),)

    def deliver(self, keep, away):
        terms = [keep, (yield self.send(away, "core"))]

        def total(start, stop):
            made = terms[0][start:stop].astype(jnp.float32)
            for term in terms[1:]:
                made = made + term[start:stop].astype(jnp.float32)
            return made.astype(jnp.bfloat16)

        half = keep.shape[0] // 2
        for axis in ("second", "first"):
            terms.append((yield self.send(total(half, 2 * half), axis)))
            half = half // 2
        rows = 2 * half // self.nz
        steps = [total(k * rows, (k + 1) * rows) for k in range(1, self.nz)]
        terms += list((yield [self.send(step, "z", k + 1) for k, step in enumerate(steps)]))
        mine = total(0, rows)
        rows = mine.shape[0] // 2
        keep = jnp.where(self.even, mine[:rows], mine[rows:])
        came = yield self.send(jnp.where(self.even, mine[rows:], mine[:rows]), "core")
        yield jnp.where(
            self.even,
            jnp.concatenate([keep, came], axis=1),
            jnp.concatenate([came, keep], axis=1),
        ).astype(jnp.float32)

    def settle(self, mine):
        rows = mine.shape[0] // 2
        keep = jnp.where(self.even, mine[:rows], mine[rows:])
        came = self.send(jnp.where(self.even, mine[rows:], mine[:rows]), "core")
        return jnp.where(
            self.even,
            jnp.concatenate([keep, came], axis=1),
            jnp.concatenate([came, keep], axis=1),
        ).astype(jnp.float32)

    def scatter(self, left, right):
        half = left.shape[1]
        rows = left.shape[0] // self.count
        places = (self.nz, self.nx, self.ny, 2 * rows, half)
        left = left.reshape(places).transpose(2, 1, 0, 3, 4)
        right = right.reshape(places).transpose(1, 2, 0, 3, 4)
        keep = jnp.where(self.even, left, right).astype(jnp.float32)
        away = jnp.where(self.even, right, left).astype(jnp.bfloat16)
        mine = (keep + self.send(away, "core").astype(jnp.float32)).astype(jnp.bfloat16)
        mine = self.scatter_axis(mine, "second")
        mine = self.scatter_axis(mine, "first")
        mine = self.scatter_axis(mine, "z")
        return self.settle(mine)

    def total(self, value):
        value = value.reshape(1, 1)
        for axis in ("core", "y", "x", "z"):
            n = {"core": 2, "y": self.ny, "x": self.nx, "z": self.nz}[axis]
            if n & (n - 1):
                value = sum([value] + [self.send(value, axis, k) for k in range(1, n)])
                continue
            bit = 1
            while bit < n:
                swap = []
                for i in range(self.count):
                    c, y = i % 2, i // 2 % self.ny
                    x, z = i // (2 * self.ny) % self.nx, i // (2 * self.ny * self.nx)
                    to = {"core": c, "y": y, "x": x, "z": z}
                    to[axis] ^= bit
                    swap.append(
                        (i, ((to["z"] * self.nx + to["x"]) * self.ny + to["y"]) * 2 + to["core"])
                    )
                value = value + lax.ppermute(value, AXES, swap)
                bit *= 2
        return value[0, 0]


def sync(values):
    return lax.optimization_barrier(values)


class Delivery:
    def __init__(self, grid, pair):
        if grid.pieces:
            self.steps = grid.deliver(*pair)
            self.under_way = next(self.steps)
        else:
            self.steps, self.under_way = None, grid.scatter(*pair)


def phase(values, land=(), start=()):
    ways = list(land) + [way for way in start if way not in land]
    values, came = sync((values, [way.under_way for way in ways]))
    for way, value in zip(ways, came):
        way.under_way = value
        if way in start and way.steps:
            way.under_way = way.steps.send(value)
    return values


def cut(pair, *widths):
    out, at = [], 0
    for width in widths:
        out.append(jnp.concatenate([p[:, at : at + width // 2] for p in pair], axis=1))
        at += width // 2
    return out


def small_back(rows):
    return (rows[:, :2].T, rows[:, 2:8].T, rows[:, 8:].reshape(-1))


def rows_of(index, count):
    return pl.ds(pl.multiple_of(index * count, count), count)


def nt(a, b):
    return lax.dot_general(a, b, (((1,), (1,)), ((), ())), preferred_element_type=jnp.float32)


def tn(a, b):
    return lax.dot_general(a, b, (((0,), (0,)), ((), ())), preferred_element_type=jnp.float32)


def nn(a, b):
    return jnp.dot(a, b, preferred_element_type=jnp.float32)


def fold(values):
    total = values[:8]
    for at in range(8, values.shape[0], 8):
        total = total + values[at : at + 8]
    return total


def norm_parts(values):
    centered = values - jnp.mean(values, axis=-1, keepdims=True)
    inverse = lax.rsqrt(jnp.mean(centered * centered, axis=-1, keepdims=True) + 1e-05)
    return (centered * inverse, inverse)


def norm_grad(grad, gain, normed, inverse):
    scaled = grad * gain
    middle = jnp.mean(scaled, axis=-1, keepdims=True)
    return inverse * (scaled - middle - normed * jnp.mean(scaled * normed, axis=-1, keepdims=True))


def gelu_parts(pre):
    share = 0.5 * (1.0 + lax.erf(pre * 0.7071067811865476))
    slope = share + pre * (0.3989422804014327 * jnp.exp(-0.5 * pre * pre))
    return (pre * share, slope)


class Group:
    def __init__(self, grid, arrays, piece, widths):
        self.arrays, self.piece, self.widths = tuple(arrays), piece, widths
        self.nz = grid.nz
        self.pieces = grid.pieces

    def copies(self, place, refs, targets, sems):
        out = []
        if not self.pieces:
            for ref, target, sem in zip(refs, targets, sems):
                if target is not None:
                    out.append(pltpu.make_async_copy(ref, target, sem))
            return out
        z, x, y, core = (place[i] for i in range(4))
        for kind in range(2):
            half = core if kind == 0 else 1 - core
            for second in range(2):
                for first in range(2):
                    ref = refs[kind * 4 + second * 2 + first]
                    x_at = lax.rem(x + first + half * (second - first), 2)
                    y_at = lax.rem(y + second + half * (first - second), 2)
                    for step in range(self.nz):
                        z_at = lax.rem(z + step, self.nz)
                        row = ((z_at * 2 + x_at) * 2 + y_at) * self.piece
                        rows = pl.ds(pl.multiple_of(row, 16), self.piece)
                        at = 0
                        for width, target, sem in zip(self.widths, targets, sems):
                            source = ref.at[pl.ds(step * self.piece, self.piece), pl.ds(at, width)]
                            at += width
                            if target is None:
                                continue
                            if len(target.shape) == 3:
                                goal = target.at[half, rows, :]
                            else:
                                columns = pl.ds(pl.multiple_of(half * width, 128), width)
                                goal = target.at[rows, columns]
                            out.append(pltpu.make_async_copy(source, goal, sem))
        return out

    def start(self, place, refs, targets, sems):
        for copy in self.copies(place, refs, targets, sems):
            copy.start()


class Whole:
    def __init__(self, grid, unit, piece, widths, near, wide):
        self.arrays, self.piece, self.widths = (unit,), piece, widths
        self.near, self.wide, self.devices = near, wide, grid.count

    def start(self, place, refs, targets, sems):
        (ref,) = refs

        def device(index, carry):
            chip, half = lax.div(index, 2), lax.rem(index, 2)
            source = pl.ds(pl.multiple_of(index * self.piece, 16), self.piece)
            at = 0
            for width, target, sem in zip(self.widths, targets, sems):
                if target is not None:
                    rows = pl.ds(pl.multiple_of(chip * self.piece, 16), self.piece)
                    columns = pl.ds(pl.multiple_of(half * width, 128), width)
                    pltpu.make_async_copy(
                        ref.at[source, pl.ds(at, width)], target.at[rows, columns], sem
                    ).start()
                at += width
            target, sem = targets[-1], sems[-1]
            if target is not None:
                width = self.wide[1]
                columns = pl.ds(pl.multiple_of(half * width, 128), width)
                for step in range(self.wide[0] // self.piece):
                    row = chip * self.wide[0] + step * self.piece
                    rows = pl.ds(pl.multiple_of(row, 16), self.piece)
                    pltpu.make_async_copy(
                        ref.at[source, pl.ds(at + step * width, width)], target.at[rows, columns], sem
                    ).start()
            return carry

        lax.fori_loop(0, self.devices, device, 0)


def start_cls(place, groups, refs, targets, sems):
    if isinstance(groups[0], Whole):
        groups[0].start(place, refs[0], targets, sems)
        return
    for group, held, ends in zip(groups, refs, (slice(0, 3), slice(3, 4))):
        group.start(place, held, targets[ends], sems[ends])


def finish(target, sem):
    pltpu.make_async_copy(target, target, sem).wait()


MIB = 2**20
VMEM_MIB = 60
FAR = pl.BlockSpec(memory_space=pltpu.HBM)
HERE = pl.BlockSpec(memory_space=pltpu.VMEM)
SCALARS = pl.BlockSpec(memory_space=pltpu.SMEM)


LARGE = 2**18


class Traffic:
    def __init__(self, far_in, far_out):
        self.far_in, self.far_out = far_in, far_out
        self.waited, self.sent = set(), set()

    def begin(self):
        for far, near, sem in self.far_in.values():
            pltpu.make_async_copy(far, near, sem).start()

    def need(self, *numbers):
        for number in numbers:
            if number in self.far_in and number not in self.waited:
                self.waited.add(number)
                _, near, sem = self.far_in[number]
                finish(near, sem)

    def flush(self, number, *index):
        if number in self.far_out:
            self.sent.add(number)
            far, near, sem = self.far_out[number]
            if index:
                far, near = far.at[index], near.at[index]
            pltpu.make_async_copy(near, far, sem).start()

    def end(self):
        self.need(*self.far_in)
        for number in self.far_out:
            if number not in self.sent:
                self.flush(number)
        for _, near, sem in self.far_out.values():
            finish(near, sem)


def call(kernel, outs, scratch, place, inputs, groups, vmem, flops=0, name=None, changed=()):
    def large(value):
        return value.size * jnp.dtype(value.dtype).itemsize >= LARGE

    weights = [a for group in groups for a in group.arrays]
    places = [n for n, value in enumerate(inputs) if large(value)]
    goals = [n for n, value in enumerate(outs) if large(value)]
    moved = [inputs[n] for n in places] + [outs[n] for n in goals]
    buffers = [pltpu.VMEM(value.shape, value.dtype) for value in moved]
    buffers += [pltpu.SemaphoreType.DMA] * len(moved)

    def body(*refs):
        at = 1 + len(inputs)
        near_in = list(refs[1:at])
        held = []
        for group in groups:
            held.append(refs[at : at + len(group.arrays)])
            at += len(group.arrays)
        at += len(changed)
        made = len(outs) + len(changed)
        near_out = list(refs[at : at + made])
        own = refs[at + made : at + made + len(scratch)]
        extra = refs[at + made + len(scratch) :]
        far_in, far_out = {}, {}
        for spot, number in enumerate(places):
            far_in[number] = (near_in[number], extra[spot], extra[len(moved) + spot])
            near_in[number] = extra[spot]
        for spot, number in enumerate(goals):
            spot += len(places)
            index = number + len(changed)
            far_out[index] = (near_out[index], extra[spot], extra[len(moved) + spot])
            near_out[index] = extra[spot]
        traffic = Traffic(far_in, far_out)
        traffic.begin()
        kernel(refs[0], near_in, held, near_out, own, traffic)
        traffic.end()

    first = 1 + len(inputs) + len(weights)
    size = sum(a.size * a.dtype.itemsize for a in list(inputs) + weights)
    size += sum(o.size * jnp.dtype(o.dtype).itemsize for o in outs)
    return pl.pallas_call(
        body,
        out_shape=tuple(jax.ShapeDtypeStruct(c.shape, c.dtype) for c in changed) + tuple(outs),
        in_specs=[SCALARS]
        + [FAR if large(value) else HERE for value in inputs]
        + [FAR] * (len(weights) + len(changed)),
        out_specs=[FAR] * len(changed) + [FAR if large(value) else HERE for value in outs],
        scratch_shapes=list(scratch) + buffers,
        input_output_aliases={first + n: n for n in range(len(changed))},
        compiler_params=pltpu.CompilerParams(vmem_limit_bytes=vmem * MIB),
        cost_estimate=pl.CostEstimate(flops=flops, bytes_accessed=size, transcendentals=0),
        name=name,
    )(place, *inputs, *weights, *changed)


def shape_of(dtype, *shape):
    return jax.ShapeDtypeStruct(shape, dtype)


F32, LOW = jnp.float32, jnp.bfloat16


def both_heads(pair):
    first = lax.broadcasted_iota(jnp.int32, pair.shape, 1) < HEAD
    none = jnp.zeros_like(pair)
    return jnp.concatenate([jnp.where(first, pair, none), jnp.where(first, none, pair)])


def pair_probs(queries, keys, allowed):
    scores = nt(queries, keys) * HEAD**-0.5
    scores = jnp.where(allowed, scores, -1e30)
    weights = jnp.exp(scores - jnp.max(scores, axis=-1, keepdims=True))
    return weights * (1.0 / jnp.sum(weights, axis=-1, keepdims=True))


def side_by_side(stacked):
    half = stacked.shape[0] // 2
    return jnp.concatenate([stacked[:half], stacked[half:]], axis=1)


def allowed_pairs(column_ref, row_ref, window):
    same = column_ref[rows_of(window, SEG), :] == row_ref[pl.ds(window, 1), :]
    return jnp.concatenate([same, same])


def pack(place, near, wide, small, doc_row):
    rows, features = near[0][0].shape[0], near[1][0].shape[1]
    lists = [[a for a in group] for group in near] + [[a] for a in wide]
    flat = [a for group in lists for a in group]
    shapes = []
    for number, group in enumerate(lists):
        width = sum(a.shape[1] // 2 for a in group) + (SMALL if number == 0 else 0)
        shapes.append((group[0].shape[0], width))
    del features

    def kernel(place_ref, inputs, weights, outs, scratch, traffic):
        core = place_ref[3]
        held = list(inputs[: len(flat)])
        traffic.need(*range(len(flat)))
        seg_gains, seg_biases, seg_bias, cls_gains, cls_biases, cls_bias, pos, doc_ref = inputs[len(flat) :]

        def chosen(count, first):
            source = lax.broadcasted_iota(jnp.int32, (count, SMALL), 0)
            goal = lax.broadcasted_iota(jnp.int32, (count, SMALL), 1)
            return jnp.where(source + first == goal, 1.0, 0.0).astype(LOW)

        each = seg_bias.shape[1] // rows

        def table(lots, bias):
            out = jnp.zeros((rows, SMALL), F32)
            for lot, first in zip(lots, (0, 8 + each)):
                out = out + tn(lot.astype(LOW), chosen(lot.shape[0], first))
            line = lax.broadcasted_iota(jnp.int32, (rows, bias.shape[1]), 0)
            spot = lax.broadcasted_iota(jnp.int32, (rows, bias.shape[1]), 1)
            lane = lax.broadcasted_iota(jnp.int32, (rows, SMALL), 1)
            for part in range(each):
                held = jnp.where(spot == line * each + part, bias[...], 0.0)
                held = jnp.sum(held, axis=1, keepdims=True)
                out = jnp.where(lane == 8 + part, held, out)
            return out

        counts = jnp.sum(jnp.where(doc_ref[...] >= 0, 1.0, 0.0), axis=1, keepdims=True)
        lane = lax.broadcasted_iota(jnp.int32, (doc_ref.shape[0], rows), 1)
        counts = jnp.where(lane == 0, counts, 0.0)
        seg_lot = jnp.concatenate([seg_gains[...], seg_biases[...]])
        cls_lot = jnp.concatenate([cls_gains[...], cls_biases[...]])
        tables = (
            table((seg_lot,), seg_bias),
            table((cls_lot, jnp.concatenate([pos[...], counts])), cls_bias),
        )
        at = 0
        for number, group in enumerate(lists):
            ends = ([], [])
            for _ in group:
                half = held[at].shape[1] // 2
                ends[0].append(held[at][:, :half])
                ends[1].append(held[at][:, half:])
                at += 1
            if number == 0:
                ends[0].append(tables[0])
                ends[1].append(tables[1])
            left, right = (jnp.concatenate(e, axis=1) if len(e) > 1 else e[0] for e in ends)
            outs[2 * number][...] = jnp.where(core == 0, left, right).astype(LOW)
            outs[2 * number + 1][...] = jnp.where(core == 0, right, left).astype(LOW)

    made = call(
        kernel,
        [shape_of(LOW, *shape) for shape in shapes for _ in range(2)],
        [],
        place,
        flat + list(small) + [doc_row],
        (),
        VMEM_MIB,
        0,
        "pack",
    )
    return [(made[n], made[n + 1]) for n in range(0, len(made), 2)]


def seg_attention(place, tokens, doc_column, doc_row, group):
    count, features = tokens.shape
    windows = count // SEG

    def kernel(place_ref, inputs, weights, outs, scratch, traffic):
        x_ref, column_ref, row_ref = inputs
        joined_ref, mixed_ref, small_ref, table_ref, mixeds_ref = outs
        qkv, low_ref, sem_qkv, sem_small = scratch
        targets = (qkv, small_ref) if group.pieces else (qkv, small_ref.at[0], small_ref.at[1])
        sems = (sem_qkv, sem_small, sem_small)
        group.start(place_ref, weights[0], targets, sems)
        traffic.need(0)
        low_ref[...] = x_ref[...].astype(LOW)
        finish(small_ref, sem_small)
        traffic.flush(2)
        diagonal = lax.broadcasted_iota(jnp.int32, (TABLE, SMALL), 0) == lax.broadcasted_iota(
            jnp.int32, (TABLE, SMALL), 1
        )
        diagonal = jnp.where(diagonal, 1.0, 0.0).astype(LOW)
        for half in range(2):
            table_ref[half] = nt(diagonal, small_ref[half])
        traffic.flush(3)
        finish(qkv, sem_qkv)
        width = features // 3

        def project(tile, carry):
            columns = pl.ds(pl.multiple_of(tile * width, width), width)
            for part in range(3):
                at = pl.ds(pl.multiple_of(part * features + tile * width, width), width)
                made = nn(low_ref[...], qkv[:, at])
                if part == 0:
                    made = made + table_ref[0, pl.ds(2, 1), columns]
                if part == 2:
                    made = made + table_ref[0, pl.ds(3, 1), columns]
                joined_ref[:, at] = made.astype(LOW)
                traffic.flush(0, slice(None), at)
            return carry

        lax.fori_loop(0, 3, project, 0)

        def window_step(window, carry):
            rows = rows_of(window, SEG)
            allowed = allowed_pairs(column_ref, row_ref, window)
            for at in range(0, features, 2 * HEAD):
                ends = slice(at, at + 2 * HEAD)
                keys = joined_ref[rows, slice(features + at, features + at + 2 * HEAD)]
                values = joined_ref[rows, slice(2 * features + at, 2 * features + at + 2 * HEAD)]
                probs = pair_probs(both_heads(joined_ref[rows, ends]), keys, allowed)
                mixed = nn(side_by_side(probs.astype(LOW)), both_heads(values))
                mixed_ref[rows, ends] = mixed.astype(LOW)
            traffic.flush(1, rows, slice(None))
            return carry

        lax.fori_loop(0, windows, window_step, 0)
        mixeds_ref[...] = first_of_windows(mixed_ref, count)

    return call(
        kernel,
        (
            shape_of(LOW, count, 3 * features),
            shape_of(LOW, count, features),
            shape_of(LOW, 2, features, SMALL),
            shape_of(F32, 2, TABLE, features),
            shape_of(F32, 8, features),
        ),
        [
            pltpu.VMEM((features, 3 * features), LOW),
            pltpu.VMEM((count, features), LOW),
            pltpu.SemaphoreType.DMA,
            pltpu.SemaphoreType.DMA,
        ],
        place,
        (tokens, doc_column, doc_row),
        (group,),
        VMEM_MIB,
        2 * count * features * 3 * features,
        "seg_attention",
    )


CHUNK = 128
TILE = 256


def first_of_windows(ref, count):
    rows = [ref[at : at + 16, :][0:1].astype(F32) for at in range(0, count, SEG)]
    return jnp.concatenate(rows + [jnp.zeros((8 - len(rows), ref.shape[1]), F32)])


class Sums:
    def __init__(self, grid, place, outs, numbers, traffic, piece, turned):
        self.grid, self.place, self.outs, self.numbers = grid, place, outs, numbers
        self.traffic, self.piece, self.turned = traffic, piece, turned

    def put(self, made, start, half, at):
        columns = slice(at, at + made.shape[1])
        if not self.grid.pieces:
            number = self.numbers[half]
            rows = pl.ds(start, made.shape[0])
            self.outs[number][rows, columns] = made
            self.traffic.flush(number, rows, columns)
            return
        z, x, y, core = (self.place[i] for i in range(4))
        nz, piece = self.grid.nz, self.piece
        first_index = start // piece if isinstance(start, int) else lax.div(start, piece)
        for step in range(made.shape[0] // piece):
            index = first_index + step
            y_off = lax.rem(index + y, 2)
            x_off = lax.rem(lax.div(index, 2) + x, 2)
            z_off = lax.rem(lax.div(index, 4) - z + nz, nz)
            first, second = (x_off, y_off) if half == 0 else (y_off, x_off)
            goal = pl.multiple_of(((second * 2 + first) * nz + z_off) * piece, 16)
            block = made[step * piece : (step + 1) * piece]
            for slot, own in enumerate((core == half, core != half)):

                @pl.when(own)
                def _(slot=slot, block=block, goal=goal):
                    number = self.numbers[slot]
                    self.outs[number][pl.ds(goal, piece), columns] = block
                    self.traffic.flush(number, pl.ds(goal, piece), columns)

    def product(self, left, right, at):
        rows, width = left.shape[1], right.shape[1] // 2
        tile = self.turned.shape[0]
        block = min(width, 768)

        def step(index, carry):
            start = pl.multiple_of(index * tile, tile)
            self.turned[...] = left[:, pl.ds(start, tile)].T
            for half in range(2):
                for column in range(0, width, block):
                    begin = half * width + column
                    end = min(begin + block, (half + 1) * width)
                    made = nn(self.turned[...], right[:, begin:end])
                    self.put(made.astype(LOW), start, half, at + column)
            return carry

        lax.fori_loop(0, rows // tile, step, 0)

    def small(self, vectors, at):
        chosen = lax.broadcasted_iota(jnp.int32, (vectors.shape[0], SMALL), 0)
        chosen = chosen == lax.broadcasted_iota(jnp.int32, (vectors.shape[0], SMALL), 1)
        made = tn(vectors.astype(LOW), jnp.where(chosen, 1.0, 0.0).astype(LOW)).astype(LOW)
        self.put(made, 0, 0, at)
        self.put(jnp.zeros_like(made), 0, 1, at)


TILE_ROWS = 384


def seg_block(grid, place, tokens, mixed, table, in_bias, teacher, weight, near, wide):
    count, features = tokens.shape
    hidden = in_bias.shape[1]
    windows = count // SEG

    def kernel(place_ref, inputs, weights, outs, scratch, traffic):
        x_ref, mixed_ref, table_ref, bias_ref, teacher_ref, weight_ref = inputs
        out_ref, cls_ref, grad_mixed_ref, resid_ref, sums_ref, bias_sums_ref, err_ref = outs[:7]
        n1s_ref, v1s_ref, n2s_ref, v2s_ref, slopes_ref, lows_ref, acts_ref = outs[7:14]
        w_out, w_in, w_fc2, hold, n1_ref, n2_ref, v1_ref, v2_ref = scratch[:8]
        low_ref, act_ref, slope_ref, second_ref, pre_ref, branch_ref, turned = scratch[8:15]
        sem_out, sem_in, sem_fc2 = scratch[15:]
        near.start(place_ref, weights[0], (w_out, w_in), (sem_out, sem_in))
        wide.start(place_ref, weights[1], (w_fc2,), (sem_fc2,))
        fc2_sums = Sums(grid, place_ref, outs, (14, 15), traffic, 2 * hidden // grid.count, turned)
        near_sums = Sums(grid, place_ref, outs, (16, 17), traffic, 2 * features // grid.count, turned)
        traffic.need(0, 1, 2, 3)
        finish(w_out, sem_out)

        def row(index):
            return table_ref[0, pl.ds(index, 1), :]

        def branch(tile, carry):
            columns = rows_of(tile, TILE)
            hold[:, columns] = (
                nn(mixed_ref[...], w_out[:, columns])
                + table_ref[0, pl.ds(4, 1), columns]
                + x_ref[:, columns]
            )
            return carry

        lax.fori_loop(0, features // TILE, branch, 0)
        gain, shift = row(0), row(5)

        def first(chunk, carry):
            rows = rows_of(chunk, CHUNK)
            normed, inverse = norm_parts(hold[rows, :])
            n1_ref[rows, :] = normed
            v1_ref[rows, :] = inverse
            low_ref[rows, :] = (normed * gain + shift).astype(LOW)
            return carry

        lax.fori_loop(0, count // CHUNK, first, 0)
        finish(w_in, sem_in)

        def inner(tile, carry):
            columns = rows_of(tile, TILE)
            hold[:, pl.ds(0, TILE)] = nn(low_ref[...], w_in[:, columns])
            bias = bias_ref[:, columns]

            def gelu(chunk, inner_carry):
                rows = rows_of(chunk, 64)
                active, slope = gelu_parts(hold[rows, pl.ds(0, TILE)] + bias)
                act_ref[rows, columns] = active.astype(LOW)
                slope_ref[rows, columns] = slope.astype(LOW)
                return inner_carry

            lax.fori_loop(0, count // 64, gelu, 0)
            return carry

        lax.fori_loop(0, hidden // TILE, inner, 0)
        finish(w_fc2, sem_fc2)

        def second(tile, carry):
            columns = rows_of(tile, TILE)
            hold[:, columns] = nn(act_ref[...], w_fc2[:, columns])
            return carry

        lax.fori_loop(0, features // TILE, second, 0)
        traffic.need(4, 5)
        last_bias, gain2, shift2 = row(6), row(1), row(7)
        nothing = jnp.zeros((8, features), F32)

        def result(chunk, carry):
            err, total_gain, total_shift, total_second = carry
            rows = rows_of(chunk, CHUNK)
            start = n1_ref[rows, :] * gain + shift
            normed, inverse = norm_parts(start + (hold[rows, :] + last_bias))
            n2_ref[rows, :] = normed
            v2_ref[rows, :] = inverse
            made = normed * gain2 + shift2
            out_ref[rows, :] = made
            traffic.flush(0, rows, slice(None))
            misfit = made - teacher_ref[rows, :]
            grad = weight_ref[rows, :] * misfit
            err = err + fold(grad * misfit)
            total_gain = total_gain + fold(grad * normed)
            total_shift = total_shift + fold(grad)
            grad = norm_grad(grad, gain2, normed, inverse)
            hold[rows, :] = grad
            low = grad.astype(LOW)
            second_ref[rows, :] = low
            return (err, total_gain, total_shift, total_second + fold(low.astype(F32)))

        err, total_gain, total_shift, total_second = lax.fori_loop(
            0, count // CHUNK, result, (nothing,) * 4
        )

        def sums(values):
            return jnp.sum(values, axis=0, keepdims=True)

        err_ref[...] = sums(jnp.sum(err, axis=1, keepdims=True))
        sums_ref[1:2, :] = sums(total_gain)
        sums_ref[7:8, :] = sums(total_shift)
        sums_ref[6:7, :] = sums(total_second)
        cls_ref[...] = jnp.zeros_like(cls_ref)
        for window in range(windows):
            slot = 12 + place_ref[4] + window
            cls_ref[window : window + 1, :] = (
                out_ref[window * SEG : window * SEG + 1, :] + table_ref[1, pl.ds(slot, 1), :]
            )
        held = (n1_ref, v1_ref, n2_ref, v2_ref, slope_ref, low_ref, act_ref)
        for goal, source in zip(outs[7:14], held):
            goal[...] = first_of_windows(source, count)
        fc2_sums.product(act_ref, second_ref, 0)

        def before_inner(tile, carry):
            columns = rows_of(tile, TILE)
            grad = nt(second_ref[...], w_fc2[columns, :]) * slope_ref[:, columns].astype(F32)
            grad = grad.astype(LOW)
            pre_ref[:, columns] = grad
            bias_sums_ref[:, columns] = sums(fold(grad.astype(F32)))
            return carry

        lax.fori_loop(0, hidden // TILE, before_inner, 0)
        near_sums.product(low_ref, pre_ref, features // 2)

        def middle(tile, carry):
            columns = rows_of(tile, TILE)
            hold[:, columns] = nt(pre_ref[...], w_in[columns, :]) + hold[:, columns]
            return carry

        lax.fori_loop(0, features // TILE, middle, 0)

        def before_first(chunk, carry):
            total_gain, total_shift, total_branch = carry
            rows = rows_of(chunk, CHUNK)
            grad, normed = hold[rows, :], n1_ref[rows, :]
            total_gain = total_gain + fold(grad * normed)
            total_shift = total_shift + fold(grad)
            grad = norm_grad(grad, gain, normed, v1_ref[rows, :])
            resid_ref[rows, :] = grad
            traffic.flush(3, rows, slice(None))
            low = grad.astype(LOW)
            branch_ref[rows, :] = low
            return (total_gain, total_shift, total_branch + fold(low.astype(F32)))

        total_gain, total_shift, total_branch = lax.fori_loop(
            0, count // CHUNK, before_first, (nothing,) * 3
        )
        sums_ref[0:1, :] = sums(total_gain)
        sums_ref[5:6, :] = sums(total_shift)
        sums_ref[4:5, :] = sums(total_branch)
        sums_ref[2:4, :] = jnp.zeros((2, features), F32)

        def before(tile, carry):
            columns = rows_of(tile, TILE)
            grad_mixed_ref[:, columns] = nt(branch_ref[...], w_out[columns, :]).astype(LOW)
            traffic.flush(2, slice(None), columns)
            return carry

        lax.fori_loop(0, features // TILE, before, 0)
        near_sums.product(mixed_ref, branch_ref, 0)

    return call(
        kernel,
        (
            shape_of(F32, count, features),
            shape_of(F32, 8, features),
            shape_of(LOW, count, features),
            shape_of(F32, count, features),
            shape_of(F32, 8, features),
            shape_of(F32, 1, hidden),
            shape_of(F32, 1, 1),
            shape_of(F32, 8, features),
            shape_of(F32, 8, 1),
            shape_of(F32, 8, features),
            shape_of(F32, 8, 1),
            shape_of(F32, 8, hidden),
            shape_of(F32, 8, features),
            shape_of(F32, 8, hidden),
        )
        + (shape_of(LOW, hidden, features // 2),) * 2
        + (shape_of(LOW, features, (features + hidden) // 2),) * 2,
        [
            pltpu.VMEM((features, features), LOW),
            pltpu.VMEM((features, hidden), LOW),
            pltpu.VMEM((hidden, features), LOW),
            pltpu.VMEM((count, features), F32),
            pltpu.VMEM((count, features), F32),
            pltpu.VMEM((count, features), F32),
            pltpu.VMEM((count, 1), F32),
            pltpu.VMEM((count, 1), F32),
            pltpu.VMEM((count, features), LOW),
            pltpu.VMEM((count, hidden), LOW),
            pltpu.VMEM((count, hidden), LOW),
            pltpu.VMEM((count, features), LOW),
            pltpu.VMEM((count, hidden), LOW),
            pltpu.VMEM((count, features), LOW),
            pltpu.VMEM((TILE_ROWS, count), LOW),
            pltpu.SemaphoreType.DMA,
            pltpu.SemaphoreType.DMA,
            pltpu.SemaphoreType.DMA,
        ],
        place,
        (tokens, mixed, table, in_bias, teacher, weight),
        (near, wide),
        VMEM_MIB,
        6 * count * features * (features + 2 * hidden),
        "seg_block",
    )


def cls_block(place, gathered, table, in_bias, err, kept, lefts, changed, groups, near, wide):
    count, features = gathered.shape[0], table.shape[2]
    windows = count // lax.axis_size("fsdp")
    hidden = in_bias.shape[1]
    heads = features // HEAD
    changed = tuple(changed)
    columns = 8 * features + 2 * hidden
    wide_left = 2 * features + hidden

    def kernel(place_ref, inputs, weights, outs, scratch, traffic):
        all_ref, table_ref, bias_ref, err_ref = inputs[:4]
        n1_ref, v1_ref, n2_ref, v2_ref, slope_ref, mixeds_ref, lows_ref, acts_ref = inputs[4:]
        factors_ref, sums_ref, bias_sums_ref = outs[len(changed) :]
        qkv, c_out, c_in, c_fc2, w_out, w_in, w_fc2, flat, tall, made, hold = scratch[:11]
        sem, c_sem_out, c_sem_in, c_sem_fc2, sem_out, sem_in, sem_fc2, flat_sem, tall_sem = scratch[11:]
        base = place_ref[4]
        start_cls(
            place_ref, groups, weights, (qkv, c_out, c_in, c_fc2), (sem, c_sem_out, c_sem_in, c_sem_fc2)
        )
        wide.start(place_ref, weights[-1], (w_fc2,), (sem_fc2,))
        near.start(place_ref, weights[-2], (w_out, w_in), (sem_out, sem_in))
        whole = [outs[0], outs[2]]
        copies = []
        for window in range(windows):
            eight, sixteen = pl.ds(window * SEG, 8), pl.ds(window * SEG, 16)
            for number, ref in enumerate(whole):
                copies.append((ref.at[eight, :], tall.at[number, window], tall_sem))
            copies.append((outs[1].at[sixteen, :], flat.at[window], flat_sem))
        for source, goal, done in copies:
            pltpu.make_async_copy(source, goal, done).start()
        traffic.need(*range(len(inputs)))
        made[...] = jnp.zeros_like(made)
        head_of = lax.broadcasted_iota(jnp.int32, (count, features), 1) // HEAD
        none = jnp.zeros((8 - windows, 1), F32)

        def mine(values):
            width = values.shape[1]
            hold[:, :width] = values
            rows = [hold[pl.ds(base + window, 1), :width] for window in range(windows)]
            return jnp.concatenate(rows + [jnp.broadcast_to(none, (8 - windows, width))])

        def top(at, values):
            made[:windows, at : at + values.shape[1]] = values[:windows]

        def bottom(at, values):
            made[windows : 2 * windows, at : at + values.shape[1]] = mine(values)[:windows]

        def spread(rows):
            return jnp.concatenate([jnp.where(head_of == h, rows, 0.0) for h in range(heads)])

        def gather_heads(rows):
            total = jnp.zeros((count, features), F32)
            for h in range(heads):
                total = total + jnp.where(head_of == h, rows[h * count : (h + 1) * count], 0.0)
            return total

        def row(half, index):
            return table_ref[half, index : index + 1, :]

        def sums(values):
            return jnp.sum(values, axis=0, keepdims=True)

        def rounded(values):
            return values.astype(LOW).astype(F32)

        top(0, mixeds_ref[...])
        top(features, lows_ref[...])
        top(2 * features, acts_ref[...])
        x = all_ref[:, :features]
        low = x.astype(LOW)
        finish(qkv, sem)
        queries = rounded(nn(low, qkv[:, :features]) + row(1, 2))
        keys = nn(low, qkv[:, features : 2 * features]).astype(LOW)
        values = (nn(low, qkv[:, 2 * features :]) + row(1, 3)).astype(LOW)
        queries = spread(queries).astype(LOW)
        scores = nt(queries, keys) * HEAD**-0.5
        exps = jnp.exp(scores - jnp.max(scores, axis=-1, keepdims=True))
        probs = exps / jnp.sum(exps, axis=-1, keepdims=True)
        mixed = gather_heads(nn(probs.astype(LOW), values)).astype(LOW)
        finish(c_out, c_sem_out)
        n1, v1 = norm_parts(x + (nn(mixed, c_out[...]) + row(1, 4)))
        first = n1 * row(1, 0) + row(1, 5)
        first_low = first.astype(LOW)
        bottom(0, rounded(x))
        bottom(features, mixed.astype(F32))
        bottom(2 * features, first_low.astype(F32))
        finish(c_in, c_sem_in)
        finish(c_fc2, c_sem_fc2)
        second = jnp.zeros((count, features), F32)
        slopes = []
        for at in range(0, hidden, features):
            ends = slice(at, at + features)
            active, slope = gelu_parts(nn(first_low, c_in[:, ends]) + bias_ref[:, ends])
            active = active.astype(LOW)
            slopes.append(slope)
            bottom(3 * features + at, active.astype(F32))
            second = second + nn(active, c_fc2[ends, :])
        n2, v2 = norm_parts(first + (second + row(1, 6)))
        result = n2 * row(1, 1) + row(1, 7)
        misfit = result - all_ref[:, features : 2 * features]
        grad = all_ref[:, 2 * features : 2 * features + 1] * misfit
        leader = jnp.where(base == 0, 1.0, 0.0)
        total = leader * sums(jnp.sum(grad * misfit, axis=1, keepdims=True)) + err_ref[...]
        high = rounded(total)
        middle = rounded(total - high)
        lane = lax.broadcasted_iota(jnp.int32, (8, SMALL), 1)
        line = lax.broadcasted_iota(jnp.int32, (8, SMALL), 0)
        value = jnp.where(lane == 0, high, jnp.where(lane == 1, middle, total - high - middle))
        top(2 * wide_left + features, jnp.where((line == 0) & (lane < 3), value, 0.0))
        grad_sum2 = norm_grad(grad, row(1, 1), n2, v2)
        grad_second = grad_sum2.astype(LOW)
        grad_first = grad_sum2
        rights = features + wide_left + 3 * features
        for step, at in enumerate(range(0, hidden, features)):
            ends = slice(at, at + features)
            grad_pre = (slopes[step] * nt(grad_second, c_fc2[ends, :])).astype(LOW)
            bottom(rights + features + at, grad_pre.astype(F32))
            grad_first = grad_first + nt(grad_pre, c_in[:, ends])
        vectors = [grad_first * n1, grad_first, grad * n2, grad]
        vectors = [leader * sums(v) for v in vectors]
        top(2 * wide_left, jnp.concatenate(vectors))
        grad_sum1 = norm_grad(grad_first, row(1, 0), n1, v1)
        grad_branch = grad_sum1.astype(LOW)
        bottom(rights, grad_branch.astype(F32))
        bottom(rights + features + hidden, grad_second.astype(F32))
        grad_mixed = spread(rounded(nt(grad_branch, c_out[...]))).astype(LOW)
        grad_probs = nt(grad_mixed, values)
        grad_scores = probs * (grad_probs - jnp.sum(probs * grad_probs, axis=-1, keepdims=True))
        grad_scores = grad_scores.astype(LOW)
        grad_query = (gather_heads(nn(grad_scores, keys)) * HEAD**-0.5).astype(LOW)
        grad_keys = (tn(grad_scores, queries) * HEAD**-0.5).astype(LOW)
        grad_values = tn(probs.astype(LOW), grad_mixed).astype(LOW)
        grad = grad_sum1
        for part, values_grad in enumerate((grad_query, grad_keys, grad_values)):
            ends = slice(part * features, (part + 1) * features)
            bottom(features + wide_left + part * features, values_grad.astype(F32))
            grad = grad + nt(values_grad, qkv[:, ends])
        grad, result = mine(grad), mine(result)
        top(2 * wide_left + features + SMALL, rounded(grad))
        sums_ref[1:2, :] = sums(grad * n2_ref[...])
        sums_ref[7:8, :] = sums(grad)
        grad_sum2 = norm_grad(grad, row(0, 1), n2_ref[...], v2_ref[...])
        grad_second = grad_sum2.astype(LOW)
        sums_ref[6:7, :] = sums(grad_second.astype(F32))
        grad_first = grad_sum2
        finish(w_fc2, sem_fc2)
        finish(w_in, sem_in)
        for at in range(0, hidden, features):
            ends = slice(at, at + features)
            grad_pre = (slope_ref[:, ends] * nt(grad_second, w_fc2[ends, :])).astype(LOW)
            top(wide_left + features + at, grad_pre.astype(F32))
            bias_sums_ref[:, ends] = sums(grad_pre.astype(F32))
            grad_first = grad_first + nt(grad_pre, w_in[:, ends])
        sums_ref[0:1, :] = sums(grad_first * n1_ref[...])
        sums_ref[5:6, :] = sums(grad_first)
        grad_sum1 = norm_grad(grad_first, row(0, 0), n1_ref[...], v1_ref[...])
        grad_branch = grad_sum1.astype(LOW)
        sums_ref[4:5, :] = sums(grad_branch.astype(F32))
        sums_ref[2:4, :] = jnp.zeros((2, features), F32)
        finish(w_out, sem_out)
        grad_mixed = rounded(nt(grad_branch, w_out[...]))
        top(wide_left, grad_branch.astype(F32))
        top(wide_left + features + hidden, grad_second.astype(F32))
        factors_ref[...] = made[...].astype(LOW)
        finish(tall, tall_sem)
        finish(flat, flat_sem)
        top8 = lax.broadcasted_iota(jnp.int32, (8, features), 0) == 0
        top16 = lax.broadcasted_iota(jnp.int32, (16, features), 0) == 0
        for window in range(windows):
            line = slice(window, window + 1)
            for number, lines in enumerate((result[line], grad_sum1[line])):
                tall[number, window] = jnp.where(top8, lines, tall[number, window])
            held = jnp.where(top16, grad_mixed[line], flat[window].astype(F32))
            flat[window] = held.astype(LOW)
        for source, goal, done in copies:
            pltpu.make_async_copy(goal, source, done).start()
        finish(tall, tall_sem)
        finish(flat, flat_sem)

    return call(
        kernel,
        (
            shape_of(LOW, 2 * windows, columns),
            shape_of(F32, 8, features),
            shape_of(F32, 1, hidden),
        ),
        [
            pltpu.VMEM((features, 3 * features), LOW),
            pltpu.VMEM((features, features), LOW),
            pltpu.VMEM((features, hidden), LOW),
            pltpu.VMEM((hidden, features), LOW),
            pltpu.VMEM((features, features), LOW),
            pltpu.VMEM((features, hidden), LOW),
            pltpu.VMEM((hidden, features), LOW),
            pltpu.VMEM((windows, 16, features), LOW),
            pltpu.VMEM((2, windows, 8, features), F32),
            pltpu.VMEM((2 * windows, columns), F32),
            pltpu.VMEM((count, features), F32),
        ]
        + [pltpu.SemaphoreType.DMA] * 9,
        place,
        (gathered, table, in_bias, err) + tuple(kept) + tuple(lefts),
        tuple(groups) + (near, wide),
        VMEM_MIB,
        4 * count * features * (4 * features + 2 * hidden),
        "cls_block",
        changed,
    )


def seg_attention_back(grid, place, joined, grad_mixed, resid, doc_column, doc_row, tokens, sums, group):
    count, features = resid.shape
    windows = count // SEG
    half_width = 3 * features // 2 + SMALL

    def kernel(place_ref, inputs, weights, outs, scratch, traffic):
        joined_ref, mixed_ref, resid_ref, column_ref, row_ref, x_ref, one_ref, two_ref, bias_ref = inputs
        rows_ref, keep_ref, away_ref = outs
        qkv, grad_ref, low_ref, sums_ref, turned, sem = scratch
        group.start(place_ref, weights[0], (qkv,) + (None,) * (len(group.widths) - 1), (sem, None, None))
        sums_ref[...] = jnp.zeros_like(sums_ref)
        traffic.need(0, 1, 3, 4)

        def window_step(window, carry):
            rows = rows_of(window, SEG)
            allowed = allowed_pairs(column_ref, row_ref, window)
            for at in range(0, features, 2 * HEAD):
                ends = slice(at, at + 2 * HEAD)
                key_ends = slice(features + at, features + at + 2 * HEAD)
                value_ends = slice(2 * features + at, 2 * features + at + 2 * HEAD)
                queries, keys = both_heads(joined_ref[rows, ends]), joined_ref[rows, key_ends]
                probs = pair_probs(queries, keys, allowed)
                grads = both_heads(mixed_ref[rows, ends])
                grad_values = tn(probs.astype(LOW), grads).astype(LOW)
                grad_probs = nt(grads, joined_ref[rows, value_ends])
                grad_scores = probs * (
                    grad_probs - jnp.sum(probs * grad_probs, axis=-1, keepdims=True)
                )
                grad_scores = grad_scores.astype(LOW)
                grad_query = nn(side_by_side(grad_scores), both_heads(keys)) * HEAD**-0.5
                grad_query = grad_query.astype(LOW)
                grad_ref[rows, ends] = grad_query
                grad_ref[rows, key_ends] = (tn(grad_scores, queries) * HEAD**-0.5).astype(LOW)
                grad_ref[rows, value_ends] = grad_values
                sums_ref[0, :, ends] += fold(grad_query.astype(F32))
                sums_ref[1, :, ends] += fold(grad_values.astype(F32))
            return carry

        lax.fori_loop(0, windows, window_step, 0)
        traffic.need(5)
        low_ref[...] = x_ref[...].astype(LOW)
        made = Sums(grid, place_ref, outs, (1, 2), traffic, 2 * features // grid.count, turned)
        made.product(low_ref, grad_ref, 0)
        held = one_ref[...] + two_ref[...]
        heads = [jnp.sum(sums_ref[n], axis=0, keepdims=True) for n in range(2)]
        rest = jnp.zeros((8 - bias_ref.shape[0], features), F32)
        made.small(jnp.concatenate([held[:2]] + heads + [held[4:], bias_ref[...], rest]), half_width - SMALL)
        traffic.need(2)
        finish(qkv, sem)

        def before(tile, carry):
            columns = rows_of(tile, TILE)
            rows_ref[:, columns] = nt(grad_ref[...], qkv[columns, :]) + resid_ref[:, columns]
            traffic.flush(0, slice(None), columns)
            return carry

        lax.fori_loop(0, features // TILE, before, 0)

    return call(
        kernel,
        (shape_of(F32, count, features),) + (shape_of(LOW, features, half_width),) * 2,
        [
            pltpu.VMEM((features, 3 * features), LOW),
            pltpu.VMEM((count, 3 * features), LOW),
            pltpu.VMEM((count, features), LOW),
            pltpu.VMEM((2, 8, features), F32),
            pltpu.VMEM((TILE_ROWS, count), LOW),
            pltpu.SemaphoreType.DMA,
        ],
        place,
        (joined, grad_mixed, resid, doc_column, doc_row, tokens) + tuple(sums),
        (group,),
        VMEM_MIB,
        4 * count * features * 3 * features,
        "seg_attention_back",
    )


def cls_weight_grads(place, factors, grid, features, hidden, slots, tokens):
    count = factors.shape[0]
    share, wide = features // grid.count, hidden // grid.count
    windows = count // grid.count // 2

    def kernel(place_ref, inputs, weights, outs, scratch, traffic):
        (all_ref,) = inputs
        traffic.need(0)
        qkv_ref, out_ref, in_ref, fc2_ref, gains_ref, biases_ref, bias_ref, pos_ref = outs[:8]
        more_out_ref, more_in_ref, more_fc2_ref, loss_ref = outs[8:]
        index = place_ref[5]

        def own(at, width, part, lower):
            source = lax.broadcasted_iota(jnp.int32, (width, part), 0)
            goal = lax.broadcasted_iota(jnp.int32, (width, part), 1) + index * part
            chosen = jnp.where(source == goal, 1.0, 0.0).astype(LOW)
            line = lax.rem(lax.broadcasted_iota(jnp.int32, (count, part), 0), 2 * windows)
            return jnp.where((line >= windows) == lower, nn(all_ref[:, at : at + width], chosen), 0.0)

        def sums(values):
            return jnp.sum(values, axis=0, keepdims=True)

        def columns(at, width):
            return all_ref[:, at : at + width]

        wide_left = 2 * features + hidden
        joined = features + wide_left
        branch = joined + 3 * features
        pre = branch + features
        second = pre + hidden

        def product(at, width, part, lower, right, columns_count):
            return tn(own(at, width, part, lower).astype(LOW), columns(right, columns_count))

        qkv_ref[...] = product(0, features, share, True, joined, 3 * features)
        out_ref[...] = product(features, features, share, True, branch, features)
        in_ref[...] = product(2 * features, features, share, True, pre, hidden)
        fc2_ref[...] = product(3 * features, hidden, wide, True, second, features)
        more_out_ref[...] = product(0, features, share, False, wide_left, features)
        more_in_ref[...] = product(features, features, share, False, wide_left + features, hidden)
        more_fc2_ref[...] = product(
            2 * features, hidden, wide, False, wide_left + features + hidden, features
        )
        vectors = 2 * wide_left
        err = vectors + features
        rows_at = err + SMALL
        line = lax.rem(lax.broadcasted_iota(jnp.int32, (count, SMALL), 0), 2 * windows)
        total = jnp.where(line == 0, columns(err, SMALL).astype(F32), 0.0)
        loss_ref[...] = sums(jnp.sum(total, axis=1, keepdims=True)) * (0.5 / (tokens * features))
        vector = own(vectors, features, share, False)
        line = lax.rem(lax.broadcasted_iota(jnp.int32, vector.shape, 0), 2 * windows)
        rows = [sums(jnp.where(line == v, vector, 0.0)) for v in range(4)]
        gains_ref[0:1, :] = rows[0]
        gains_ref[1:2, :] = rows[2]
        biases_ref[0:1, :] = sums(own(joined, features, share, True))
        biases_ref[1:2, :] = sums(own(joined + 2 * features, features, share, True))
        biases_ref[2:3, :] = sums(own(branch, features, share, True))
        biases_ref[3:4, :] = rows[1]
        biases_ref[4:5, :] = sums(own(second, features, share, True))
        biases_ref[5:6, :] = rows[3]
        bias_ref[...] = sums(own(pre, hidden, wide, True))
        slot = lax.broadcasted_iota(jnp.int32, (slots, count), 0)
        row = lax.broadcasted_iota(jnp.int32, (slots, count), 1)
        window = lax.rem(row, 2 * windows)
        of = lax.rem(lax.div(row, 2 * windows) * windows + window, slots)
        chosen = jnp.where((slot == of) & (window < windows), 1.0, 0.0).astype(LOW)
        pos_ref[...] = nn(chosen, own(rows_at, features, share, False).astype(LOW))

    return call(
        kernel,
        (
            shape_of(F32, share, 3 * features),
            shape_of(F32, share, features),
            shape_of(F32, share, hidden),
            shape_of(F32, wide, features),
            shape_of(F32, 2, share),
            shape_of(F32, 6, share),
            shape_of(F32, 1, wide),
            shape_of(F32, slots, share),
            shape_of(F32, share, features),
            shape_of(F32, share, hidden),
            shape_of(F32, wide, features),
            shape_of(F32, 1, 1),
        ),
        [],
        place,
        (factors,),
        (),
        VMEM_MIB,
        2 * count * features * 20000 // 24,
        "cls_weight_grads",
    )


def per_device(
    tokens,
    doc_ids,
    teacher,
    seg_qkv,
    seg_out,
    seg_in,
    seg_fc2,
    seg_gains,
    seg_biases,
    seg_in_bias,
    cls_qkv,
    cls_out,
    cls_in,
    cls_fc2,
    cls_gains,
    cls_biases,
    cls_in_bias,
    seg_pos,
):
    rows_count, features = tokens.shape
    windows = rows_count // SEG
    low = jnp.bfloat16
    grid = Grid(features)
    hidden = seg_in.shape[1]
    slot_count = seg_pos.shape[0]
    per_feature = 8 + hidden // features
    fsdp = lax.axis_index("fsdp")
    place = jnp.stack(
        [grid.z, grid.x, grid.y, grid.core, fsdp * windows, grid.index]
    ).astype(jnp.int32)
    validity = (doc_ids >= 0).astype(jnp.float32)
    doc_column, doc_row = doc_ids[:, None], doc_ids.reshape(windows, SEG)
    half, wide_half = features // 2, hidden // 2
    packed = pack(
        place,
        ((seg_qkv,), (seg_out, seg_in), (cls_qkv, cls_out, cls_in)),
        (seg_fc2, cls_fc2),
        (
            seg_gains,
            seg_biases,
            seg_in_bias[None],
            cls_gains,
            cls_biases,
            cls_in_bias[None],
            seg_pos,
        ),
        doc_row,
    )
    ends_qkv, ends_near, ends_cls, ends_fc2, ends_cls_fc2 = packed
    cls_widths = (3 * half, half, wide_half)
    if grid.pieces:
        one, two, three = (grid.pair(ends) for ends in (ends_qkv, ends_near, ends_fc2))
        came, two = sync((grid.along(one), two))
        one = grid.line(one, came)
        ones, came, three = sync((grid.plane(one), grid.along(two), three))
        two = grid.line(two, came)
        last, twos, came = sync(
            (grid.send(ones[0], "second"), grid.plane(two), grid.along(three))
        )
        cls_groups = grid.everything(ends_cls, cls_widths, ends_cls_fc2, ones)
        one, three = (one,) + tuple(ones) + (last,), grid.line(three, came)
        group_qkv = grid.grouped(one, grid.swap(one), 3 * half, SMALL)
        two = (two,) + tuple(twos)
        under_way = (grid.swap(two), grid.send(twos[0], "second"), grid.plane(three))
    else:
        group_qkv = grid.whole(ends_qkv, 3 * half, SMALL)
        group_near = grid.whole(ends_near, half, wide_half)
        group_fc2 = grid.whole(ends_fc2, half)
        cls_groups = (grid.whole(ends_cls, *cls_widths), grid.whole(ends_cls_fc2, half))
    joined, mixed, small, table, mixeds = seg_attention(place, tokens, doc_column, doc_row, group_qkv)
    seg_bias = small[0][:, 8:per_feature].astype(jnp.float32).reshape(1, hidden)
    cls_bias = small[1][:, 8:per_feature].astype(jnp.float32).reshape(1, hidden)
    at = per_feature + slot_count
    token_count = jnp.sum(small[1][:, at : at + windows].astype(jnp.float32))
    everything = rows_count * grid.count
    weight = ((2.0 * everything / token_count) * validity)[:, None]
    place_in = lax.broadcasted_iota(jnp.int32, weight.shape, 0) % SEG
    others_weight = jnp.where(place_in == 0, 0.0, weight)

    mixed, seg_bias, cls_bias, weight, others_weight = sync(
        (mixed, seg_bias, cls_bias, weight, others_weight)
    )
    if grid.pieces:
        mixed, (others, last, threes) = sync((mixed, under_way))
        two, three = two + (last,), (three,) + tuple(threes)
        mixed, (more, others_fc2, last) = sync(
            (mixed, (grid.send(last, "core"), grid.swap(three), grid.send(threes[0], "second")))
        )
        group_near = grid.grouped(two, tuple(others) + (more,), half, wide_half)
        mixed, more = sync((mixed, grid.send(last, "core")))
        group_fc2 = grid.grouped(three + (last,), tuple(others_fc2) + (more,), half)
    def cls_only(rows):
        return rows.reshape(windows, SEG, -1)[:, 0]

    made = seg_block(
        grid, place, tokens, mixed, table, seg_bias, teacher, others_weight, group_near, group_fc2
    )
    first_out, cls_rows, grad_mixed, resid, sums, bias_sums, err = made[:7]
    n1s, v1s, n2s, v2s, slopes, lows, actives = made[7:14]
    fc2_way, near_way = Delivery(grid, made[14:16]), Delivery(grid, made[16:])
    gathered = [cls_rows[:windows], cls_only(teacher), jnp.broadcast_to(cls_only(weight), (windows, SMALL))]
    gathered = lax.all_gather(jnp.concatenate(gathered, axis=1), "fsdp", axis=0, tiled=True)
    gathered = phase(gathered, (fc2_way, near_way), (fc2_way, near_way))
    output, grad_mixed, resid, factors, more_sums, more_bias = cls_block(
        place,
        gathered,
        table,
        cls_bias,
        err,
        (n1s, v1s, n2s, v2s, slopes),
        (mixeds, lows, actives),
        (first_out, grad_mixed, resid),
        cls_groups,
        group_near,
        group_fc2,
    )
    grad_mixed, factors = phase((grad_mixed, factors), (fc2_way, near_way), (fc2_way, near_way))
    factors = lax.all_gather(factors, AXES, axis=0, tiled=True)
    grad_tokens, *pair = seg_attention_back(
        grid,
        place,
        joined,
        grad_mixed,
        resid,
        doc_column,
        doc_row,
        tokens,
        (sums, more_sums, (bias_sums + more_bias).reshape(features, -1).T),
        group_qkv,
    )
    pair = phase(pair, (fc2_way, near_way), (fc2_way, near_way))
    ways = (Delivery(grid, pair), fc2_way, near_way)
    qkv_way = ways[0]
    if grid.pieces:
        phase((), (qkv_way,), (qkv_way,))
        phase((), (qkv_way,), (qkv_way,))
        phase((), ways, ways)
    cls_grads = cls_weight_grads(place, factors, grid, features, hidden, slot_count, everything)
    if grid.pieces:
        cls_grads = phase(cls_grads, ways, ways)
        phase((), (qkv_way,), (qkv_way,))
    grad_qkv, grad_near, grad_fc2 = qkv_way.under_way, near_way.under_way, fc2_way.under_way
    extra_out, extra_in, extra_fc2, loss = cls_grads[8:]
    ends = grad_near.shape[1] // 2
    seg_grad_out, seg_grad_in = cut((grad_near[:, :ends], grad_near[:, ends:]), features, hidden)
    ends = grad_qkv.shape[1] // 2
    seg_grad_qkv = cut((grad_qkv[:, :ends], grad_qkv[:, ends:]), 3 * features)[0]
    seg_tail = small_back(grad_qkv[:, 3 * half : 3 * half + per_feature])
    return (
        (output, loss[0, 0], grad_tokens, seg_grad_qkv, seg_grad_out + extra_out)
        + (seg_grad_in + extra_in, grad_fc2 + extra_fc2)
        + seg_tail
        + tuple(cls_grads[:6])
        + (cls_grads[6].reshape(-1), cls_grads[7])
    )


def solution(mesh):
    return jax.shard_map(
        per_device,
        mesh=mesh,
        in_specs=(
            P(("dp", "fsdp"), None),
            P(("dp", "fsdp")),
            P(("dp", "fsdp"), None),
            P(("dp", "fsdp"), None),
            P(("dp", "fsdp"), None),
            P(("dp", "fsdp"), None),
            P(("dp", "fsdp"), None),
            P(None, ("dp", "fsdp")),
            P(None, ("dp", "fsdp")),
            P(("dp", "fsdp")),
            P(("dp", "fsdp"), None),
            P(("dp", "fsdp"), None),
            P(("dp", "fsdp"), None),
            P(("dp", "fsdp"), None),
            P(None, ("dp", "fsdp")),
            P(None, ("dp", "fsdp")),
            P(("dp", "fsdp")),
            P(None, ("dp", "fsdp")),
        ),
        out_specs=(
            P(("dp", "fsdp"), None),
            P(),
            P(("dp", "fsdp"), None),
            P(("dp", "fsdp"), None),
            P(("dp", "fsdp"), None),
            P(("dp", "fsdp"), None),
            P(("dp", "fsdp"), None),
            P(None, ("dp", "fsdp")),
            P(None, ("dp", "fsdp")),
            P(("dp", "fsdp")),
            P(("dp", "fsdp"), None),
            P(("dp", "fsdp"), None),
            P(("dp", "fsdp"), None),
            P(("dp", "fsdp"), None),
            P(None, ("dp", "fsdp")),
            P(None, ("dp", "fsdp")),
            P(("dp", "fsdp")),
            P(None, ("dp", "fsdp")),
        ),
        check_vma=False,
    )
```

time: 423 us -> 360 us (0.85)
  local copies, waits for them, and re-layouts: 44.2 us -> 12.9 us
  waiting for transfers between devices: 116 us -> 87.1 us
  starting transfers between devices: 60.4 us -> 78.3 us
  Pallas kernels: 134 us -> 121 us
  blocking collectives: 12.5 us -> 7.16 us
    unnamed x186 -> x58, local copies, waits for them, and re-layouts: 34.2 us -> 3.2 us
    ppermute x56, waiting for transfers between devices: 116 us -> 87 us  [send(): return lax.ppermute(value, AXES, self.pairs(axis, step))]
    ppermute x56, starting transfers between devices: 60.3 us -> 78.2 us  [send(): return lax.ppermute(value, AXES, self.pairs(axis, step))]
    pallas_call x12 -> x6, Pallas kernels: 134 us -> 121 us  [call(): pl.pallas_call(body, out_shape=tuple((jax.ShapeDtypeStruct(c.shape, c.dty...]
    convert_element_type x12, other arithmetic: 14.5 us -> 23.7 us  [total(): return made.astype(jnp.bfloat16)]
    all_to_all x1 -> x0, blocking collectives: 6.46 us -> none  [per_device(): parts = lax.all_to_all(parts, 'fsdp', 0, 0, tiled=True)]
    another operation x9 -> x0, other arithmetic: 4.92 us -> none
  transfers between devices with their start and end apart: 58 -> 58, of which waited for: 18 -> 19; matrix products, arithmetic and copies ran while one was open for 8% -> 11% of each run, Pallas kernels for 27% -> 33%
where the time goes in v3:
time: 360 us; the launch traced here: 355 us
  Pallas kernels  121 us (34%)
  waiting for transfers between devices  87.1 us (24%)
  starting transfers between devices  78.3 us (22%)
  other arithmetic  33.4 us (9%)
  between operations  15.9 us (4%)
  local copies, waits for them, and re-layouts  12.9 us (4%)
  blocking collectives  7.16 us (2%)
    pallas_call x6, Pallas kernels, call(): pl.pallas_call(body, out_shape=tuple((jax.ShapeDtypeStruct(c.shape, c.dty...  121 us
    ppermute x56, waiting for transfers between devices, send(): return lax.ppermute(value, AXES, self.pairs(axis, step))  87 us
    ppermute x56, starting transfers between devices, send(): return lax.ppermute(value, AXES, self.pairs(axis, step))  78.2 us
    convert_element_type x12, other arithmetic, total(): return made.astype(jnp.bfloat16)  23.7 us
  transfers between devices with their start and end apart: 58, of which 19 were waited for; matrix products, arithmetic and copies ran while one was open for 11% of the time, Pallas kernels for 33%

profile of v3, /device:TPU:0, one launch (start us, length us, event | category | flops | bytes accessed | tf_op | source)
XLA Modules:
  0.0 355.3 jit_solution(16521802714082446637)
XLA Ops:
  7.9 3.6 %pack.1 = (bf16[24,1280]{1,0:T(8,128)(2,1)}, bf16[24,1280]{1,0:T(8,128)(2,1)}, bf16[24,1920]{1,0:T(8,128)(2,1)}, bf16[24,1920]{1,0:T(8,128)(2,1)}, bf16[24,3072]...) custom-call(s32[6]{0:T(128)} %stack.27.refs_0_, ...), custom_call_target="tpu_custom_call" | custom-call | bytes 2672384 | tf_op jit(solution)/shard_map/pack/pallas_call | solution.py:458
  14.1 3.0 collective-permute-start.3
  17.0 2.6 collective-permute-start.2
  25.2 2.9 collective-permute-done.2
  32.2 2.9 collective-permute-start.9
  37.6 4.2 %collective-permute-done.9 = bf16[48,1920]{1,0:T(8,128)(2,1)S(1)} collective-permute-done((bf16[48,1920]{1,0:T(8,128)(2,1)S(1)}, bf16[48,1920]{1,0:T(8,128)(2,1)S(1)}, u32[]{:S(2)}, u32[]{:S(2)}) %collective-permute-start.9) | collective-permute-done | bytes 184352 | tf_op jit(solution)/shard_map/ppermute | solution.py:61
  41.8 5.9 %collective-permute-done.8 = bf16[48,1920]{1,0:T(8,128)(2,1)S(1)} collective-permute-done((bf16[48,1920]{1,0:T(8,128)(2,1)S(1)}, bf16[48,1920]{1,0:T(8,128)(2,1)S(1)}, u32[]{:S(2)}, u32[]{:S(2)}) %collective-permute-start.8) | collective-permute-done | bytes 184352 | tf_op jit(solution)/shard_map/ppermute | solution.py:61
  50.6 4.4 %collective-permute-start.16 = (bf16[192,384]{1,0:T(8,128)(2,1)S(1)}, bf16[192,384]{1,0:T(8,128)(2,1)S(1)}, u32[]{:S(2)}, u32[]{:S(2)}) collective-permute-start(bf16[192,384]{1,0:T(8,128)(2,1)S(1)} %maximum_select_fusion.3), channel_id=1, source_target_pairs={{0,8},{1,9},{2,10},{3,11},{4,12},{5,13},{6,14},{7,15},{8,16},{9,17... | collective-permute-start | bytes 442376 | tf_op jit(solution)/shard_map/ppermute | solution.py:61
  57.0 3.4 collective-permute-done.16
  62.0 7.2 %collective-permute-done.15 = bf16[192,384]{1,0:T(8,128)(2,1)S(1)} collective-permute-done((bf16[192,384]{1,0:T(8,128)(2,1)S(1)}, bf16[192,384]{1,0:T(8,128)(2,1)S(1)}, u32[]{:S(2)}, u32[]{:S(2)}) %collective-permute-start.15) | collective-permute-done | bytes 147488 | tf_op jit(solution)/shard_map/ppermute | solution.py:61
  69.2 5.3 %collective-permute-done.14 = bf16[192,384]{1,0:T(8,128)(2,1)S(1)} collective-permute-done((bf16[192,384]{1,0:T(8,128)(2,1)S(1)}, bf16[192,384]{1,0:T(8,128)(2,1)S(1)}, u32[]{:S(2)}, u32[]{:S(2)}) %collective-permute-start.14) | collective-permute-done | bytes 147488 | tf_op jit(solution)/shard_map/ppermute | solution.py:61
  78.9 12.2 %seg_attention.1 = (bf16[512,2304]{1,0:T(8,128)(2,1)}, bf16[512,768]{1,0:T(8,128)(2,1)}, bf16[2,768,128]{2,1,0:T(8,128)(2,1)}, f32[2,48,768]{2,1,0:T(8,128)}, f32[8,768]{1,0:T(8,128)}) custom-call(s32[6]{0:T(128)} %stack.27.refs_0_, f32[512,768]{1,0:T(8,128)} %refs_6_.3, s32[512,1]{1,0:T(8,128)} %copy.55.refs_2_.refs_4_, s32[4,128]{1,0:T(4,128)} %bitcast.32, ...), custom_call_target="tpu_custom_call" | custom-call | flops 1811939328 | bytes 9367552 | tf_op jit(solution)/shard_map/seg_attention/pallas_call | solution.py:458
  97.0 9.8 %collective-permute-done.26.refs_17_.refs_24_ = bf16[768,384]{1,0:T(8,128)(2,1)} collective-permute-done((bf16[768,384]{1,0:T(8,128)(2,1)S(1)}, bf16[768,384]{1,0:T(8,128)(2,1)}, u32[]{:S(2)}, u32[]{:S(2)}) %collective-permute-start.26) | collective-permute-done | bytes 589856 | tf_op jit(solution)/shard_map/ppermute | solution.py:61
  106.8 6.4 %collective-permute-done.25.refs_16_.refs_23_ = bf16[768,384]{1,0:T(8,128)(2,1)S(1)} collective-permute-done((bf16[768,384]{1,0:T(8,128)(2,1)S(1)}, bf16[768,384]{1,0:T(8,128)(2,1)S(1)}, u32[]{:S(2)}, u32[]{:S(2)}) %collective-permute-start.25) | collective-permute-done | bytes 589856 | tf_op jit(solution)/shard_map/ppermute | solution.py:61
  117.6 7.2 %collective-permute-done.31.refs_18_.refs_25_ = bf16[768,384]{1,0:T(8,128)(2,1)} collective-permute-done((bf16[768,384]{1,0:T(8,128)(2,1)S(1)}, bf16[768,384]{1,0:T(8,128)(2,1)}, u32[]{:S(2)}, u32[]{:S(2)}) %collective-permute-start.31) | collective-permute-done | bytes 589856 | tf_op jit(solution)/shard_map/ppermute | solution.py:61
  128.7 49.1 %seg_block.1 = (f32[512,768]{1,0:T(8,128)}, f32[8,768]{1,0:T(8,128)}, bf16[512,768]{1,0:T(8,128)(2,1)}, f32[512,768]{1,0:T(8,128)}, f32[8,768]{1,0:T(8,128)}, /*...) custom-call(s32[6]{0:T(128)} %stack.27.refs_0_, ...), custom_call_target="tpu_custom_call" | custom-call | flops 16307453952 | bytes 29739076 | tf_op jit(solution)/shard_map/seg_block/pallas_call | solution.py:458
  180.3 7.2 %all-gather = f32[4,4,1664]{2,1,0:T(4,128)S(1)} all-gather(f32[1,4,1664]{2,1,0:T(4,128)S(1)} %maximum_bitcast_fusion), channel_id=1, replica_groups=mesh['dp'=8,'fsdp'=4] {'fsdp'}, dimensions={0}, use_global_device_ids=true | all-gather | bytes 133120 | tf_op jit(solution)/shard_map/all_gather | solution.py:1424
  188.2 3.9 %add_convert_fusion = bf16[384,1920]{1,0:T(8,128)(2,1)} fusion(bf16[768,1920]{1,0:T(8,128)(2,1)S(1)} %collective-permute-done.34, bf16[768,1920]{1,0:T(8,128)(2,1)} %get-tuple-element.215), kind=kLoop, calls=%fused_computation | loop fusion | flops 2949120 | bytes 4423680 | tf_op jit(solution)/shard_map/convert_element_type | solution.py:142
  193.1 2.6 add_convert_fusion.1
  196.8 20.7 %cls_block.1 = (f32[512,768]{1,0:T(8,128)}, bf16[512,768]{1,0:T(8,128)(2,1)}, f32[512,768]{1,0:T(8,128)}, bf16[8,12288]{1,0:T(8,128)(2,1)}, f32[8,768]{1,0:T(8,128)}, /*index=5*/f32[1,3072]{1,0:T(1,128)}) custom-call(s32[6]{0:T(128)} %stack.27.refs_0_, f32[16,1664]{1,0:T(8,128)} %reshape.91.refs_1_, ...), custom_call_target="tpu_custom_call", output_to_operand_aliasing={{0}: (30, {}), {1}: (31, {}), {2}: (32, {})} | custom-call | flops 452984832 | bytes 25714756 | tf_op jit(solution)/shard_map/cls_block/pallas_call | solution.py:458
  217.5 7.0 %collective-permute-done.37 = bf16[1536,384]{1,0:T(8,128)(2,1)} collective-permute-done((bf16[1536,384]{1,0:T(8,128)(2,1)}, bf16[1536,384]{1,0:T(8,128)(2,1)}, u32[]{:S(2)}, u32[]{:S(2)}) %collective-permute-start.37) | collective-permute-done | bytes 1179680 | tf_op jit(solution)/shard_map/ppermute | solution.py:61
  224.5 2.5 add_convert_fusion.3
  228.0 2.4 add_convert_fusion.4
  232.7 25.7 %seg_attention_back.1 = (f32[512,768]{1,0:T(8,128)}, bf16[768,1280]{1,0:T(8,128)(2,1)}, bf16[768,1280]{1,0:T(8,128)(2,1)}) custom-call(s32[6]{0:T(128)} %stack.27.refs_0_, bf16[512,2304]{1,0:T(8,128)(2,1)} %get-tuple-element.230.refs_1_, bf16[512,768]{1,0:T(8,128)(2,1)} %get-tuple-element.231.refs_2_, f32[512,768]{1,0:T(8,128)} %get-tuple-element.232.refs_3_, ...), custom_call_target="tpu_custom_call" | custom-call | flops 3623878656 | bytes 15794176 | tf_op jit(solution)/shard_map/seg_attention_back/pallas_call | solution.py:458
  258.5 4.2 %collective-permute-done.41 = bf16[768,1280]{1,0:T(8,128)(2,1)S(1)} collective-permute-done((bf16[768,1280]{1,0:T(8,128)(2,1)}, bf16[768,1280]{1,0:T(8,128)(2,1)S(1)}, u32[]{:S(2)}, u32[]{:S(2)}) %collective-permute-start.41) | collective-permute-done | bytes 1966112 | tf_op jit(solution)/shard_map/ppermute | solution.py:61
  267.6 7.3 %collective-permute-start.46 = (bf16[192,384]{1,0:T(8,128)(2,1)S(1)}, bf16[192,384]{1,0:T(8,128)(2,1)S(1)}, u32[]{:S(2)}, u32[]{:S(2)}) collective-permute-start(bf16[192,384]{1,0:T(8,128)(2,1)S(1)} %get-tuple-element.347), channel_id=1, source_target_pairs={{0,24},{1,25},{2,26},{3,27},{4,28},{5,29},{6,30},{7,31},{8,0},{9,1... | collective-permute-start | bytes 442376 | tf_op jit(solution)/shard_map/ppermute | solution.py:61
  274.8 4.4 %collective-permute-start.45 = (bf16[192,384]{1,0:T(8,128)(2,1)S(1)}, bf16[192,384]{1,0:T(8,128)(2,1)S(1)}, u32[]{:S(2)}, u32[]{:S(2)}) collective-permute-start(bf16[192,384]{1,0:T(8,128)(2,1)S(1)} %get-tuple-element.348), channel_id=1, source_target_pairs={{0,16},{1,17},{2,18},{3,19},{4,20},{5,21},{6,22},{7,23},{8,24},{9,... | collective-permute-start | bytes 442376 | tf_op jit(solution)/shard_map/ppermute | solution.py:61
  283.4 15.7 %collective-permute-start.49 = (bf16[48,1920]{1,0:T(8,128)(2,1)S(1)}, bf16[48,1920]{1,0:T(8,128)(2,1)S(1)}, u32[]{:S(2)}, u32[]{:S(2)}) collective-permute-start(bf16[48,1920]{1,0:T(8,128)(2,1)S(1)} %get-tuple-element.344), channel_id=1, source_target_pairs={{0,24},{1,25},{2,26},{3,27},{4,28},{5,29},{6,30},{7,31},{8,0},{9,1... | collective-permute-start | bytes 552968 | tf_op jit(solution)/shard_map/ppermute | solution.py:61
  299.1 7.1 %collective-permute-start.48 = (bf16[48,1920]{1,0:T(8,128)(2,1)S(1)}, bf16[48,1920]{1,0:T(8,128)(2,1)S(1)}, u32[]{:S(2)}, u32[]{:S(2)}) collective-permute-start(bf16[48,1920]{1,0:T(8,128)(2,1)S(1)} %get-tuple-element.345), channel_id=1, source_target_pairs={{0,16},{1,17},{2,18},{3,19},{4,20},{5,21},{6,22},{7,23},{8,24},{9,... | collective-permute-start | bytes 552968 | tf_op jit(solution)/shard_map/ppermute | solution.py:61
  306.7 12.0 %collective-permute-done.44 = bf16[192,384]{1,0:T(8,128)(2,1)S(1)} collective-permute-done((bf16[192,384]{1,0:T(8,128)(2,1)S(1)}, bf16[192,384]{1,0:T(8,128)(2,1)S(1)}, u32[]{:S(2)}, u32[]{:S(2)}) %collective-permute-start.44) | collective-permute-done | bytes 147488 | tf_op jit(solution)/shard_map/ppermute | solution.py:61
  318.8 7.0 %collective-permute-done.48 = bf16[48,1920]{1,0:T(8,128)(2,1)S(1)} collective-permute-done((bf16[48,1920]{1,0:T(8,128)(2,1)S(1)}, bf16[48,1920]{1,0:T(8,128)(2,1)S(1)}, u32[]{:S(2)}, u32[]{:S(2)}) %collective-permute-start.48) | collective-permute-done | bytes 184352 | tf_op jit(solution)/shard_map/ppermute | solution.py:61
  331.9 9.2 %cls_weight_grads.1 = (f32[24,2304]{1,0:T(8,128)}, f32[24,768]{1,0:T(8,128)}, f32[24,3072]{1,0:T(8,128)}, f32[96,768]{1,0:T(8,128)}, f32[2,24]{1,0:T(2,128)}, /*...) custom-call(s32[6]{0:T(128)} %stack.27.refs_0_, ...), custom_call_target="tpu_custom_call" | custom-call | flops 327680000 | bytes 7842436 | tf_op jit(solution)/shard_map/cls_weight_grads/pallas_call | solution.py:458
  (206 shorter events, 70.3 us)
Async XLA Ops:
  7.2 189.6 %all-gather.4.cloned.1.call-start = ((), (), s32[]{:S(2)}) async-start(), calls=%async_computation | async-start | bytes 14598144 | tf_op jit(solution)/shard_map/all_gather | solution.py:132
  29.1 18.7 %collective-permute-start.6 = (bf16[192,1280]{1,0:T(8,128)(2,1)}, bf16[192,1280]{1,0:T(8,128)(2,1)}, u32[]{:S(2)}, u32[]{:S(2)}) collective-permute-start(bf16[192,1280]{1,0:T(8,128)(2,1)} %pad_maximum_fusion.refs_4_.refs_10_), channel_id=1, source_target_pairs={{0,2},{1,5},{2,0},{3,7},{4,6},{5,1},{6,4},{7,3},{8,10},{9,13},{10,... | collective-permute-start | bytes 1474568 | tf_op jit(solution)/shard_map/ppermute | solution.py:61
  30.7 17.0 %collective-permute-start.5 = (bf16[192,1280]{1,0:T(8,128)(2,1)}, bf16[192,1280]{1,0:T(8,128)(2,1)}, u32[]{:S(2)}, u32[]{:S(2)}) collective-permute-start(bf16[192,1280]{1,0:T(8,128)(2,1)} %pad_maximum_fusion.refs_4_.refs_10_), channel_id=1, source_target_pairs={{0,4},{1,3},{2,6},{3,1},{4,0},{5,7},{6,2},{7,5},{8,12},{9,11},{10,... | collective-permute-start | bytes 1474568 | tf_op jit(solution)/shard_map/ppermute | solution.py:61
  35.1 12.6 %collective-permute-start.8 = (bf16[48,1920]{1,0:T(8,128)(2,1)S(1)}, bf16[48,1920]{1,0:T(8,128)(2,1)S(1)}, u32[]{:S(2)}, u32[]{:S(2)}) collective-permute-start(bf16[48,1920]{1,0:T(8,128)(2,1)S(1)} %maximum_select_fusion.1), channel_id=1, source_target_pairs={{0,16},{1,17},{2,18},{3,19},{4,20},{5,21},{6,22},{7,23},{8,24},{9,... | collective-permute-start | bytes 552968 | tf_op jit(solution)/shard_map/ppermute | solution.py:61
  47.8 284.1 %all-gather.6.cloned.1.call-start = ((), (), s32[]{:S(2)}) async-start(), calls=%async_computation.1 | async-start | bytes 6488064 | tf_op jit(solution)/shard_map/all_gather | solution.py:1440
  47.9 27.2 %collective-permute-start.13 = (bf16[192,1920]{1,0:T(8,128)(2,1)S(1)}, bf16[192,1920]{1,0:T(8,128)(2,1)S(1)}, u32[]{:S(2)}, u32[]{:S(2)}) collective-permute-start(bf16[192,1920]{1,0:T(8,128)(2,1)S(1)} %constant_dynamic-update-slice_fusion.refs_7_.refs_14_), channel_id=1, source_target_pairs={{0,2},{1,5},{2,0},{3,7},{4,6},{5,1},{6,4},{7,3},{8,10},{9,13},{10,... | collective-permute-start | bytes 2211848 | tf_op jit(solution)/shard_map/ppermute | solution.py:61
  48.5 26.6 %collective-permute-start.12 = (bf16[192,1920]{1,0:T(8,128)(2,1)S(1)}, bf16[192,1920]{1,0:T(8,128)(2,1)}, u32[]{:S(2)}, u32[]{:S(2)}) collective-permute-start(bf16[192,1920]{1,0:T(8,128)(2,1)S(1)} %constant_dynamic-update-slice_fusion.refs_7_.refs_14_), channel_id=1, source_target_pairs={{0,4},{1,3},{2,6},{3,1},{4,0},{5,7},{6,2},{7,5},{8,12},{9,11},{10,... | collective-permute-start | bytes 2211848 | tf_op jit(solution)/shard_map/ppermute | solution.py:61
  49.0 26.1 %collective-permute-start.11 = (bf16[192,1280]{1,0:T(8,128)(2,1)}, bf16[192,1280]{1,0:T(8,128)(2,1)}, u32[]{:S(2)}, u32[]{:S(2)}) collective-permute-start(bf16[192,1280]{1,0:T(8,128)(2,1)} %collective-permute-done.5.refs_5_.refs_11_), channel_id=1, source_target_pairs={{0,2},{1,5},{2,0},{3,7},{4,6},{5,1},{6,4},{7,3},{8,10},{9,13},{10,... | collective-permute-start | bytes 1474568 | tf_op jit(solution)/shard_map/ppermute | solution.py:61
  55.0 14.3 %collective-permute-start.15 = (bf16[192,384]{1,0:T(8,128)(2,1)S(1)}, bf16[192,384]{1,0:T(8,128)(2,1)S(1)}, u32[]{:S(2)}, u32[]{:S(2)}) collective-permute-start(bf16[192,384]{1,0:T(8,128)(2,1)S(1)} %maximum_select_fusion.3), channel_id=1, source_target_pairs={{0,16},{1,17},{2,18},{3,19},{4,20},{5,21},{6,22},{7,23},{8,24},{9,... | collective-permute-start | bytes 442376 | tf_op jit(solution)/shard_map/ppermute | solution.py:61
  60.4 14.1 %collective-permute-start.14 = (bf16[192,384]{1,0:T(8,128)(2,1)S(1)}, bf16[192,384]{1,0:T(8,128)(2,1)S(1)}, u32[]{:S(2)}, u32[]{:S(2)}) collective-permute-start(bf16[192,384]{1,0:T(8,128)(2,1)S(1)} %maximum_select_fusion.3), channel_id=1, source_target_pairs={{0,24},{1,25},{2,26},{3,27},{4,28},{5,29},{6,30},{7,31},{8,0},{9,1... | collective-permute-start | bytes 442376 | tf_op jit(solution)/shard_map/ppermute | solution.py:61
  76.5 15.7 %collective-permute-start.21 = (bf16[192,1920]{1,0:T(8,128)(2,1)S(1)}, bf16[192,1920]{1,0:T(8,128)(2,1)S(1)}, u32[]{:S(2)}, u32[]{:S(2)}) collective-permute-start(bf16[192,1920]{1,0:T(8,128)(2,1)S(1)} %constant_dynamic-update-slice_fusion.refs_7_.refs_14_), channel_id=1, source_target_pairs={{0,1},{1,0},{2,3},{3,2},{4,5},{5,4},{6,7},{7,6},{8,9},{9,8},{10,11... | collective-permute-start | bytes 2211848 | tf_op jit(solution)/shard_map/ppermute | solution.py:61
  76.7 36.5 %collective-permute-start.24 = (bf16[192,1920]{1,0:T(8,128)(2,1)}, bf16[192,1920]{1,0:T(8,128)(2,1)}, u32[]{:S(2)}, u32[]{:S(2)}) collective-permute-start(bf16[192,1920]{1,0:T(8,128)(2,1)} %collective-permute-done.12.refs_8_.refs_15_), channel_id=1, source_target_pairs={{0,2},{1,5},{2,0},{3,7},{4,6},{5,1},{6,4},{7,3},{8,10},{9,13},{10,... | collective-permute-start | bytes 2211848 | tf_op jit(solution)/shard_map/ppermute | solution.py:61
  77.4 35.8 %collective-permute-start.22 = (bf16[192,1920]{1,0:T(8,128)(2,1)}, bf16[192,1920]{1,0:T(8,128)(2,1)}, u32[]{:S(2)}, u32[]{:S(2)}) collective-permute-start(bf16[192,1920]{1,0:T(8,128)(2,1)} %collective-permute-done.12.refs_8_.refs_15_), channel_id=1, source_target_pairs={{0,1},{1,0},{2,3},{3,2},{4,5},{5,4},{6,7},{7,6},{8,9},{9,8},{10,11... | collective-permute-start | bytes 2211848 | tf_op jit(solution)/shard_map/ppermute | solution.py:61
  78.3 28.5 %collective-permute-start.26 = (bf16[768,384]{1,0:T(8,128)(2,1)S(1)}, bf16[768,384]{1,0:T(8,128)(2,1)}, u32[]{:S(2)}, u32[]{:S(2)}) collective-permute-start(bf16[768,384]{1,0:T(8,128)(2,1)S(1)} %constant_dynamic-update-slice_fusion.4.refs_15_.refs_22_), channel_id=1, source_target_pairs={{0,2},{1,5},{2,0},{3,7},{4,6},{5,1},{6,4},{7,3},{8,10},{9,13},{10,... | collective-permute-start | bytes 1769480 | tf_op jit(solution)/shard_map/ppermute | solution.py:61
  78.9 34.4 %collective-permute-start.23 = (bf16[192,1920]{1,0:T(8,128)(2,1)S(1)}, bf16[192,1920]{1,0:T(8,128)(2,1)}, u32[]{:S(2)}, u32[]{:S(2)}) collective-permute-start(bf16[192,1920]{1,0:T(8,128)(2,1)S(1)} %collective-permute-done.13.refs_9_.refs_16_), channel_id=1, source_target_pairs={{0,1},{1,0},{2,3},{3,2},{4,5},{5,4},{6,7},{7,6},{8,9},{9,8},{10,11... | collective-permute-start | bytes 2211848 | tf_op jit(solution)/shard_map/ppermute | solution.py:61
  92.2 21.0 %collective-permute-start.25 = (bf16[768,384]{1,0:T(8,128)(2,1)S(1)}, bf16[768,384]{1,0:T(8,128)(2,1)S(1)}, u32[]{:S(2)}, u32[]{:S(2)}) collective-permute-start(bf16[768,384]{1,0:T(8,128)(2,1)S(1)} %constant_dynamic-update-slice_fusion.4.refs_15_.refs_22_), channel_id=1, source_target_pairs={{0,4},{1,3},{2,6},{3,1},{4,0},{5,7},{6,2},{7,5},{8,12},{9,11},{10,... | collective-permute-start | bytes 1769480 | tf_op jit(solution)/shard_map/ppermute | solution.py:61
  192.1 32.3 %collective-permute-start.38 = (bf16[384,1920]{1,0:T(8,128)(2,1)}, bf16[384,1920]{1,0:T(8,128)(2,1)}, u32[]{:S(2)}, u32[]{:S(2)}) collective-permute-start(bf16[384,1920]{1,0:T(8,128)(2,1)} %add_convert_fusion), channel_id=1, source_target_pairs={{0,2},{1,5},{2,0},{3,7},{4,6},{5,1},{6,4},{7,3},{8,10},{9,13},{10,... | collective-permute-start | bytes 4423688 | tf_op jit(solution)/shard_map/ppermute | solution.py:61
  195.7 28.7 %collective-permute-start.37 = (bf16[1536,384]{1,0:T(8,128)(2,1)}, bf16[1536,384]{1,0:T(8,128)(2,1)}, u32[]{:S(2)}, u32[]{:S(2)}) collective-permute-start(bf16[1536,384]{1,0:T(8,128)(2,1)} %add_convert_fusion.1), channel_id=1, source_target_pairs={{0,2},{1,5},{2,0},{3,7},{4,6},{5,1},{6,4},{7,3},{8,10},{9,13},{10,... | collective-permute-start | bytes 3538952 | tf_op jit(solution)/shard_map/ppermute | solution.py:61
  227.0 31.4 %collective-permute-start.40 = (bf16[192,1920]{1,0:T(8,128)(2,1)}, bf16[192,1920]{1,0:T(8,128)(2,1)}, u32[]{:S(2)}, u32[]{:S(2)}) collective-permute-start(bf16[192,1920]{1,0:T(8,128)(2,1)} %add_convert_fusion.3), channel_id=1, source_target_pairs={{0,4},{1,3},{2,6},{3,1},{4,0},{5,7},{6,2},{7,5},{8,12},{9,11},{10,... | collective-permute-start | bytes 2211848 | tf_op jit(solution)/shard_map/ppermute | solution.py:61
  230.5 27.9 %collective-permute-start.39 = (bf16[768,384]{1,0:T(8,128)(2,1)}, bf16[768,384]{1,0:T(8,128)(2,1)}, u32[]{:S(2)}, u32[]{:S(2)}) collective-permute-start(bf16[768,384]{1,0:T(8,128)(2,1)} %add_convert_fusion.4), channel_id=1, source_target_pairs={{0,4},{1,3},{2,6},{3,1},{4,0},{5,7},{6,2},{7,5},{8,12},{9,11},{10,... | collective-permute-start | bytes 1769480 | tf_op jit(solution)/shard_map/ppermute | solution.py:61
  264.8 14.4 %collective-permute-start.42 = (bf16[384,1280]{1,0:T(8,128)(2,1)S(1)}, bf16[384,1280]{1,0:T(8,128)(2,1)S(1)}, u32[]{:S(2)}, u32[]{:S(2)}) collective-permute-start(bf16[384,1280]{1,0:T(8,128)(2,1)S(1)} %add_convert_fusion.2), channel_id=1, source_target_pairs={{0,2},{1,5},{2,0},{3,7},{4,6},{5,1},{6,4},{7,3},{8,10},{9,13},{10,... | collective-permute-start | bytes 2949128 | tf_op jit(solution)/shard_map/ppermute | solution.py:61
  267.6 38.6 %collective-permute-start.46 = (bf16[192,384]{1,0:T(8,128)(2,1)S(1)}, bf16[192,384]{1,0:T(8,128)(2,1)S(1)}, u32[]{:S(2)}, u32[]{:S(2)}) collective-permute-start(bf16[192,384]{1,0:T(8,128)(2,1)S(1)} %get-tuple-element.347), channel_id=1, source_target_pairs={{0,24},{1,25},{2,26},{3,27},{4,28},{5,29},{6,30},{7,31},{8,0},{9,1... | collective-permute-start | bytes 442376 | tf_op jit(solution)/shard_map/ppermute | solution.py:61
  274.8 31.3 %collective-permute-start.45 = (bf16[192,384]{1,0:T(8,128)(2,1)S(1)}, bf16[192,384]{1,0:T(8,128)(2,1)S(1)}, u32[]{:S(2)}, u32[]{:S(2)}) collective-permute-start(bf16[192,384]{1,0:T(8,128)(2,1)S(1)} %get-tuple-element.348), channel_id=1, source_target_pairs={{0,16},{1,17},{2,18},{3,19},{4,20},{5,21},{6,22},{7,23},{8,24},{9,... | collective-permute-start | bytes 442376 | tf_op jit(solution)/shard_map/ppermute | solution.py:61
  280.7 45.0 %collective-permute-start.43 = (bf16[192,1280]{1,0:T(8,128)(2,1)S(1)}, bf16[192,1280]{1,0:T(8,128)(2,1)S(1)}, u32[]{:S(2)}, u32[]{:S(2)}) collective-permute-start(bf16[192,1280]{1,0:T(8,128)(2,1)S(1)} %add_convert_fusion.5), channel_id=1, source_target_pairs={{0,4},{1,3},{2,6},{3,1},{4,0},{5,7},{6,2},{7,5},{8,12},{9,11},{10,... | collective-permute-start | bytes 1474568 | tf_op jit(solution)/shard_map/ppermute | solution.py:61
  283.4 35.4 %collective-permute-start.49 = (bf16[48,1920]{1,0:T(8,128)(2,1)S(1)}, bf16[48,1920]{1,0:T(8,128)(2,1)S(1)}, u32[]{:S(2)}, u32[]{:S(2)}) collective-permute-start(bf16[48,1920]{1,0:T(8,128)(2,1)S(1)} %get-tuple-element.344), channel_id=1, source_target_pairs={{0,24},{1,25},{2,26},{3,27},{4,28},{5,29},{6,30},{7,31},{8,0},{9,1... | collective-permute-start | bytes 552968 | tf_op jit(solution)/shard_map/ppermute | solution.py:61
  299.1 26.7 %collective-permute-start.48 = (bf16[48,1920]{1,0:T(8,128)(2,1)S(1)}, bf16[48,1920]{1,0:T(8,128)(2,1)S(1)}, u32[]{:S(2)}, u32[]{:S(2)}) collective-permute-start(bf16[48,1920]{1,0:T(8,128)(2,1)S(1)} %get-tuple-element.345), channel_id=1, source_target_pairs={{0,16},{1,17},{2,18},{3,19},{4,20},{5,21},{6,22},{7,23},{8,24},{9,... | collective-permute-start | bytes 552968 | tf_op jit(solution)/shard_map/ppermute | solution.py:61
  306.1 19.6 %collective-permute-start.47 = (bf16[48,1920]{1,0:T(8,128)(2,1)S(1)}, bf16[48,1920]{1,0:T(8,128)(2,1)S(1)}, u32[]{:S(2)}, u32[]{:S(2)}) collective-permute-start(bf16[48,1920]{1,0:T(8,128)(2,1)S(1)} %get-tuple-element.346), channel_id=1, source_target_pairs={{0,8},{1,9},{2,10},{3,11},{4,12},{5,13},{6,14},{7,15},{8,16},{9,17... | collective-permute-start | bytes 552968 | tf_op jit(solution)/shard_map/ppermute | solution.py:61
  306.2 12.6 %collective-permute-start.44 = (bf16[192,384]{1,0:T(8,128)(2,1)S(1)}, bf16[192,384]{1,0:T(8,128)(2,1)S(1)}, u32[]{:S(2)}, u32[]{:S(2)}) collective-permute-start(bf16[192,384]{1,0:T(8,128)(2,1)S(1)} %get-tuple-element.349), channel_id=1, source_target_pairs={{0,8},{1,9},{2,10},{3,11},{4,12},{5,13},{6,14},{7,15},{8,16},{9,17... | collective-permute-start | bytes 442376 | tf_op jit(solution)/shard_map/ppermute | solution.py:61
  327.1 14.1 %collective-permute-start.54 = (bf16[24,1920]{1,0:T(8,128)(2,1)S(1)}, bf16[24,1920]{1,0:T(8,128)(2,1)S(1)}, u32[]{:S(2)}, u32[]{:S(2)}) collective-permute-start(bf16[24,1920]{1,0:T(8,128)(2,1)S(1)} %get-tuple-element.362), channel_id=1, source_target_pairs={{0,1},{1,0},{2,3},{3,2},{4,5},{5,4},{6,7},{7,6},{8,9},{9,8},{10,11... | collective-permute-start | bytes 276488 | tf_op jit(solution)/shard_map/ppermute | solution.py:61
  328.4 12.8 %collective-permute-start.52 = (bf16[48,1280]{1,0:T(8,128)(2,1)S(1)}, bf16[48,1280]{1,0:T(8,128)(2,1)S(1)}, u32[]{:S(2)}, u32[]{:S(2)}) collective-permute-start(bf16[48,1280]{1,0:T(8,128)(2,1)S(1)} %get-tuple-element.350), channel_id=1, source_target_pairs={{0,24},{1,25},{2,26},{3,27},{4,28},{5,29},{6,30},{7,31},{8,0},{9,1... | collective-permute-start | bytes 368648 | tf_op jit(solution)/shard_map/ppermute | solution.py:61
  328.5 12.7 %collective-permute-start.51 = (bf16[48,1280]{1,0:T(8,128)(2,1)S(1)}, bf16[48,1280]{1,0:T(8,128)(2,1)S(1)}, u32[]{:S(2)}, u32[]{:S(2)}) collective-permute-start(bf16[48,1280]{1,0:T(8,128)(2,1)S(1)} %get-tuple-element.351), channel_id=1, source_target_pairs={{0,16},{1,17},{2,18},{3,19},{4,20},{5,21},{6,22},{7,23},{8,24},{9,... | collective-permute-start | bytes 368648 | tf_op jit(solution)/shard_map/ppermute | solution.py:61
  328.5 12.7 %collective-permute-start.50 = (bf16[48,1280]{1,0:T(8,128)(2,1)S(1)}, bf16[48,1280]{1,0:T(8,128)(2,1)S(1)}, u32[]{:S(2)}, u32[]{:S(2)}) collective-permute-start(bf16[48,1280]{1,0:T(8,128)(2,1)S(1)} %get-tuple-element.352), channel_id=1, source_target_pairs={{0,8},{1,9},{2,10},{3,11},{4,12},{5,13},{6,14},{7,15},{8,16},{9,17... | collective-permute-start | bytes 368648 | tf_op jit(solution)/shard_map/ppermute | solution.py:61
  (49 other events, 569.6 us)
Sparse Core Ops, SparseCore 0:
  47.9 121.2 all-gather.3
  224.6 84.1 all-gather.5

commit v4 on v3

--- a/solution.py
+++ b/solution.py
@@ -51,6 +51,15 @@
             out.append((i, ((z * self.nx + x) * self.ny + y) * 2 + c))
         return out
 
+    def line_pairs(self, t, step):
+        out = []
+        for i, to in self.pairs("z", step):
+            z = i // (2 * self.ny * self.nx)
+            place = z if step == 1 else self.nz - 1 - z
+            if place < min(t, self.nz - 1):
+                out.append((i, to))
+        return out
+
     def size(self, axis):
         return {"core": 2, "z": self.nz}.get(axis, self.nx)
 
@@ -132,7 +141,7 @@
         unit = lax.all_gather(unit, AXES, axis=0, tiled=True)
         return (Whole(self, unit, rows, widths, near.shape[1], wide.shape),)
 
-    def deliver(self, keep, away):
+    def deliver(self, keep, away, folded=0):
         terms = [keep, (yield self.send(away, "core"))]
 
         def total(start, stop):
@@ -146,17 +155,39 @@
             terms.append((yield self.send(total(half, 2 * half), axis)))
             half = half // 2
         rows = 2 * half // self.nz
-        steps = [total(k * rows, (k + 1) * rows) for k in range(1, self.nz)]
-        terms += list((yield [self.send(step, "z", k + 1) for k, step in enumerate(steps)]))
+        if folded:
+            right = left = None
+            for t in range(1, self.nz):
+                out = []
+                for k, came, step in ((self.nz - t, right, 1), (t, left, -1)):
+                    made = total(k * rows, (k + 1) * rows)
+                    if came is not None:
+                        made = (made.astype(jnp.float32) + came.astype(jnp.float32)).astype(jnp.bfloat16)
+                    out.append(lax.ppermute(made, AXES, self.line_pairs(t, step)))
+                right, left = yield out
+            terms += [right, left]
+        else:
+            steps = [total(k * rows, (k + 1) * rows) for k in range(1, self.nz)]
+            terms += list((yield [self.send(step, "z", k + 1) for k, step in enumerate(steps)]))
         mine = total(0, rows)
-        rows = mine.shape[0] // 2
-        keep = jnp.where(self.even, mine[:rows], mine[rows:])
-        came = yield self.send(jnp.where(self.even, mine[rows:], mine[:rows]), "core")
-        yield jnp.where(
-            self.even,
-            jnp.concatenate([keep, came], axis=1),
-            jnp.concatenate([came, keep], axis=1),
-        ).astype(jnp.float32)
+        rows, width = mine.shape[0] // 2, mine.shape[1] - folded
+        plain, rest = mine[:, :width], mine[:, width:]
+        pairs = [(plain[:rows], plain[rows:])]
+        if folded:
+            pairs.append((rest[:, : folded // 2], rest[:, folded // 2 :]))
+        came = yield [self.send(jnp.where(self.even, two, one), "core") for one, two in pairs]
+        out = []
+        for number, ((one, two), other) in enumerate(zip(pairs, came)):
+            own = jnp.where(self.even, one, two)
+            if number:
+                own, other = self.unfold(own), self.unfold(other)
+            joined = jnp.concatenate([own, other], axis=1), jnp.concatenate([other, own], axis=1)
+            out.append(jnp.where(self.even, *joined).astype(jnp.float32))
+        yield out
+
+    def unfold(self, blocks):
+        half = blocks.shape[1] // 2
+        return jnp.concatenate([blocks[:, :half], blocks[:, half:]])
 
     def settle(self, mine):
         rows = mine.shape[0] // 2
@@ -210,12 +241,13 @@
 
 
 class Delivery:
-    def __init__(self, grid, pair):
+    def __init__(self, grid, pairs, folded=0):
         if grid.pieces:
-            self.steps = grid.deliver(*pair)
+            self.steps = grid.deliver(*pairs, folded)
             self.under_way = next(self.steps)
         else:
-            self.steps, self.under_way = None, grid.scatter(*pair)
+            lots = zip(pairs[::2], pairs[1::2])
+            self.steps, self.under_way = None, [grid.scatter(*lot) for lot in lots]
 
 
 def phase(values, land=(), start=()):
@@ -627,7 +659,7 @@
             traffic.flush(1, rows, slice(None))
             return carry
 
-        lax.fori_loop(0, windows, window_step, 0)
+        lax.fori_loop(0, windows, window_step, 0, unroll=2)
         mixeds_ref[...] = first_of_windows(mixed_ref, count)
 
     return call(
@@ -668,8 +700,9 @@
         self.grid, self.place, self.outs, self.numbers = grid, place, outs, numbers
         self.traffic, self.piece, self.turned = traffic, piece, turned
 
-    def put(self, made, start, half, at):
-        columns = slice(at, at + made.shape[1])
+    def put(self, made, start, half, at, fold=1):
+        width = made.shape[1]
+        columns = slice(at, at + width)
         if not self.grid.pieces:
             number = self.numbers[half]
             rows = pl.ds(start, made.shape[0])
@@ -678,37 +711,46 @@
             return
         z, x, y, core = (self.place[i] for i in range(4))
         nz, piece = self.grid.nz, self.piece
-        first_index = start // piece if isinstance(start, int) else lax.div(start, piece)
-        for step in range(made.shape[0] // piece):
+        large = piece * fold
+        first_index = start // large if isinstance(start, int) else lax.div(start, large)
+        for step in range(made.shape[0] // large):
             index = first_index + step
             y_off = lax.rem(index + y, 2)
             x_off = lax.rem(lax.div(index, 2) + x, 2)
             z_off = lax.rem(lax.div(index, 4) - z + nz, nz)
             first, second = (x_off, y_off) if half == 0 else (y_off, x_off)
             goal = pl.multiple_of(((second * 2 + first) * nz + z_off) * piece, 16)
-            block = made[step * piece : (step + 1) * piece]
+            blocks = []
+            for part in range(fold):
+                begin = step * large + part * piece
+                ends = slice(at + part * width, at + (part + 1) * width)
+                blocks.append((made[begin : begin + piece], ends))
             for slot, own in enumerate((core == half, core != half)):
 
                 @pl.when(own)
-                def _(slot=slot, block=block, goal=goal):
+                def _(slot=slot, blocks=blocks, goal=goal):
                     number = self.numbers[slot]
-                    self.outs[number][pl.ds(goal, piece), columns] = block
-                    self.traffic.flush(number, pl.ds(goal, piece), columns)
-
-    def product(self, left, right, at):
+                    for block, ends in blocks:
+                        self.outs[number][pl.ds(goal, piece), ends] = block
+                    ends = slice(blocks[0][1].start, blocks[-1][1].stop)
+                    self.traffic.flush(number, pl.ds(goal, piece), ends)
+
+    def product(self, left, right, at, fold=1):
         rows, width = left.shape[1], right.shape[1] // 2
         tile = self.turned.shape[0]
-        block = min(width, 768)
+        block = min(2 * width, 768)
 
         def step(index, carry):
             start = pl.multiple_of(index * tile, tile)
             self.turned[...] = left[:, pl.ds(start, tile)].T
-            for half in range(2):
-                for column in range(0, width, block):
-                    begin = half * width + column
-                    end = min(begin + block, (half + 1) * width)
-                    made = nn(self.turned[...], right[:, begin:end])
-                    self.put(made.astype(LOW), start, half, at + column)
+            for begin in range(0, 2 * width, block):
+                end = begin + block
+                made = nn(self.turned[...], right[:, begin:end]).astype(LOW)
+                for half in range(2):
+                    low, high = max(begin, half * width), min(end, (half + 1) * width)
+                    if low < high:
+                        part = made[:, low - begin : high - begin]
+                        self.put(part, start, half, at + low - half * width, fold)
             return carry
 
         lax.fori_loop(0, rows // tile, step, 0)
@@ -728,6 +770,13 @@
     count, features = tokens.shape
     hidden = in_bias.shape[1]
     windows = count // SEG
+    near_width = (features + hidden) // 2
+    lots, fc2_at = (hidden // features, near_width) if grid.pieces else (1, 0)
+    if grid.pieces:
+        gradients = (shape_of(LOW, features, near_width + hidden // 2),) * 2
+    else:
+        gradients = (shape_of(LOW, features, near_width),) * 2
+        gradients += (shape_of(LOW, hidden, features // 2),) * 2
 
     def kernel(place_ref, inputs, weights, outs, scratch, traffic):
         x_ref, mixed_ref, table_ref, bias_ref, teacher_ref, weight_ref = inputs
@@ -738,8 +787,10 @@
         sem_out, sem_in, sem_fc2 = scratch[15:]
         near.start(place_ref, weights[0], (w_out, w_in), (sem_out, sem_in))
         wide.start(place_ref, weights[1], (w_fc2,), (sem_fc2,))
-        fc2_sums = Sums(grid, place_ref, outs, (14, 15), traffic, 2 * hidden // grid.count, turned)
-        near_sums = Sums(grid, place_ref, outs, (16, 17), traffic, 2 * features // grid.count, turned)
+        made = Sums(grid, place_ref, outs, (14, 15), traffic, 2 * features // grid.count, turned)
+        others = made
+        if not grid.pieces:
+            others = Sums(grid, place_ref, outs, (16, 17), traffic, 0, turned)
         traffic.need(0, 1, 2, 3)
         finish(w_out, sem_out)
 
@@ -781,10 +832,10 @@
                 slope_ref[rows, columns] = slope.astype(LOW)
                 return inner_carry
 
-            lax.fori_loop(0, count // 64, gelu, 0)
+            lax.fori_loop(0, count // 64, gelu, 0, unroll=True)
             return carry
 
-        lax.fori_loop(0, hidden // TILE, inner, 0)
+        lax.fori_loop(0, hidden // TILE, inner, 0, unroll=2)
         finish(w_fc2, sem_fc2)
 
         def second(tile, carry):
@@ -804,10 +855,10 @@
             normed, inverse = norm_parts(start + (hold[rows, :] + last_bias))
             n2_ref[rows, :] = normed
             v2_ref[rows, :] = inverse
-            made = normed * gain2 + shift2
-            out_ref[rows, :] = made
+            here = normed * gain2 + shift2
+            out_ref[rows, :] = here
             traffic.flush(0, rows, slice(None))
-            misfit = made - teacher_ref[rows, :]
+            misfit = here - teacher_ref[rows, :]
             grad = weight_ref[rows, :] * misfit
             err = err + fold(grad * misfit)
             total_gain = total_gain + fold(grad * normed)
@@ -838,7 +889,7 @@
         held = (n1_ref, v1_ref, n2_ref, v2_ref, slope_ref, low_ref, act_ref)
         for goal, source in zip(outs[7:14], held):
             goal[...] = first_of_windows(source, count)
-        fc2_sums.product(act_ref, second_ref, 0)
+        others.product(act_ref, second_ref, fc2_at, lots)
 
         def before_inner(tile, carry):
             columns = rows_of(tile, TILE)
@@ -848,8 +899,8 @@
             bias_sums_ref[:, columns] = sums(fold(grad.astype(F32)))
             return carry
 
-        lax.fori_loop(0, hidden // TILE, before_inner, 0)
-        near_sums.product(low_ref, pre_ref, features // 2)
+        lax.fori_loop(0, hidden // TILE, before_inner, 0, unroll=2)
+        made.product(low_ref, pre_ref, features // 2)
 
         def middle(tile, carry):
             columns = rows_of(tile, TILE)
@@ -886,7 +937,7 @@
             return carry
 
         lax.fori_loop(0, features // TILE, before, 0)
-        near_sums.product(mixed_ref, branch_ref, 0)
+        made.product(mixed_ref, branch_ref, 0)
 
     return call(
         kernel,
@@ -906,8 +957,7 @@
             shape_of(F32, 8, features),
             shape_of(F32, 8, hidden),
         )
-        + (shape_of(LOW, hidden, features // 2),) * 2
-        + (shape_of(LOW, features, (features + hidden) // 2),) * 2,
+        + gradients,
         [
             pltpu.VMEM((features, features), LOW),
             pltpu.VMEM((features, hidden), LOW),
@@ -1185,7 +1235,7 @@
                 sums_ref[1, :, ends] += fold(grad_values.astype(F32))
             return carry
 
-        lax.fori_loop(0, windows, window_step, 0)
+        lax.fori_loop(0, windows, window_step, 0, unroll=2)
         traffic.need(5)
         low_ref[...] = x_ref[...].astype(LOW)
         made = Sums(grid, place_ref, outs, (1, 2), traffic, 2 * features // grid.count, turned)
@@ -1419,10 +1469,10 @@
     )
     first_out, cls_rows, grad_mixed, resid, sums, bias_sums, err = made[:7]
     n1s, v1s, n2s, v2s, slopes, lows, actives = made[7:14]
-    fc2_way, near_way = Delivery(grid, made[14:16]), Delivery(grid, made[16:])
+    ffn_way = Delivery(grid, made[14:], hidden // 2)
     gathered = [cls_rows[:windows], cls_only(teacher), jnp.broadcast_to(cls_only(weight), (windows, SMALL))]
     gathered = lax.all_gather(jnp.concatenate(gathered, axis=1), "fsdp", axis=0, tiled=True)
-    gathered = phase(gathered, (fc2_way, near_way), (fc2_way, near_way))
+    gathered = phase(gathered, (ffn_way,), (ffn_way,))
     output, grad_mixed, resid, factors, more_sums, more_bias = cls_block(
         place,
         gathered,
@@ -1436,7 +1486,7 @@
         group_near,
         group_fc2,
     )
-    grad_mixed, factors = phase((grad_mixed, factors), (fc2_way, near_way), (fc2_way, near_way))
+    grad_mixed, factors = phase((grad_mixed, factors), (ffn_way,), (ffn_way,))
     factors = lax.all_gather(factors, AXES, axis=0, tiled=True)
     grad_tokens, *pair = seg_attention_back(
         grid,
@@ -1450,18 +1500,16 @@
         (sums, more_sums, (bias_sums + more_bias).reshape(features, -1).T),
         group_qkv,
     )
-    pair = phase(pair, (fc2_way, near_way), (fc2_way, near_way))
-    ways = (Delivery(grid, pair), fc2_way, near_way)
-    qkv_way = ways[0]
+    pair = phase(pair, (ffn_way,), (ffn_way,))
+    qkv_way = Delivery(grid, pair)
     if grid.pieces:
-        phase((), (qkv_way,), (qkv_way,))
-        phase((), (qkv_way,), (qkv_way,))
-        phase((), ways, ways)
+        for _ in range(3):
+            phase((), (qkv_way, ffn_way), (qkv_way, ffn_way))
     cls_grads = cls_weight_grads(place, factors, grid, features, hidden, slot_count, everything)
     if grid.pieces:
-        cls_grads = phase(cls_grads, ways, ways)
+        cls_grads = phase(cls_grads, (qkv_way, ffn_way), (qkv_way, ffn_way))
         phase((), (qkv_way,), (qkv_way,))
-    grad_qkv, grad_near, grad_fc2 = qkv_way.under_way, near_way.under_way, fc2_way.under_way
+    (grad_qkv,), (grad_near, grad_fc2) = qkv_way.under_way, ffn_way.under_way
     extra_out, extra_in, extra_fc2, loss = cls_grads[8:]
     ends = grad_near.shape[1] // 2
     seg_grad_out, seg_grad_in = cut((grad_near[:, :ends], grad_near[:, ends:]), features, hidden)

time: 360 us -> 347 us (0.964)
  waiting for transfers between devices: 87.1 us -> 105 us
  starting transfers between devices: 78.3 us -> 62.1 us
  other arithmetic: 33.4 us -> 24.2 us
  Pallas kernels: 121 us -> 112 us
    ppermute x0 -> x6, waiting for transfers between devices: none -> 32.3 us  [deliver(): out.append(lax.ppermute(made, AXES, self.line_pairs(t, step)))]
    ppermute x56 -> x47, starting transfers between devices: 78.2 us -> 49.3 us  [send(): return lax.ppermute(value, AXES, self.pairs(axis, step))]
    ppermute x56 -> x47, waiting for transfers between devices: 87 us -> 73.1 us  [send(): return lax.ppermute(value, AXES, self.pairs(axis, step))]
    ppermute x0 -> x6, starting transfers between devices: none -> 12.7 us  [deliver(): out.append(lax.ppermute(made, AXES, self.line_pairs(t, step)))]
    convert_element_type x12 -> x8, other arithmetic: 23.7 us -> 13.2 us  [total(): return made.astype(jnp.bfloat16)]
    pallas_call x6, Pallas kernels: 121 us -> 112 us  [call(): pl.pallas_call(body, out_shape=tuple((jax.ShapeDtypeStruct(c.shape, c.dty...]
  transfers between devices with their start and end apart: 58 -> 55, of which waited for: 19 -> 19; matrix products, arithmetic and copies ran while one was open for 11% -> 10% of each run, Pallas kernels for 33% -> 32%
where the time goes in v4:
time: 347 us; the launch traced here: 342 us
  Pallas kernels  112 us (32%)
  waiting for transfers between devices  105 us (30%)
  starting transfers between devices  62.1 us (18%)
  other arithmetic  24.2 us (7%)
  between operations  15.6 us (4%)
  local copies, waits for them, and re-layouts  14.9 us (4%)
  blocking collectives  7.64 us (2%)
    pallas_call x6, Pallas kernels, call(): pl.pallas_call(body, out_shape=tuple((jax.ShapeDtypeStruct(c.shape, c.dty...  112 us
    ppermute x47, waiting for transfers between devices, send(): return lax.ppermute(value, AXES, self.pairs(axis, step))  73.1 us
    ppermute x47, starting transfers between devices, send(): return lax.ppermute(value, AXES, self.pairs(axis, step))  49.3 us
    ppermute x6, waiting for transfers between devices, deliver(): out.append(lax.ppermute(made, AXES, self.line_pairs(t, step)))  32.3 us
    convert_element_type x8, other arithmetic, total(): return made.astype(jnp.bfloat16)  13.2 us
    ppermute x6, starting transfers between devices, deliver(): out.append(lax.ppermute(made, AXES, self.line_pairs(t, step)))  12.7 us
    all_gather x1, blocking collectives, per_device(): lax.all_gather(jnp.concatenate(gathered, axis=1), 'fsdp', axis=0, tiled=T...  7.64 us
  transfers between devices with their start and end apart: 55, of which 19 were waited for; matrix products, arithmetic and copies ran while one was open for 10% of the time, Pallas kernels for 32%

profile of v4, /device:TPU:0, one launch (start us, length us, event | category | flops | bytes accessed | tf_op | source)
XLA Modules:
  0.0 342.2 jit_solution(12268484836120014637)
XLA Ops:
  7.9 3.6 %pack.1 = (bf16[24,1280]{1,0:T(8,128)(2,1)}, bf16[24,1280]{1,0:T(8,128)(2,1)}, bf16[24,1920]{1,0:T(8,128)(2,1)}, bf16[24,1920]{1,0:T(8,128)(2,1)}, bf16[24,3072]...) custom-call(s32[6]{0:T(128)} %stack.27.refs_0_, ...), custom_call_target="tpu_custom_call" | custom-call | bytes 2672384 | tf_op jit(solution)/shard_map/pack/pallas_call | solution.py:490
  14.2 5.0 %collective-permute-start.1 = (bf16[48,1280]{1,0:T(8,128)(2,1)S(1)}, bf16[48,1280]{1,0:T(8,128)(2,1)S(1)}, u32[]{:S(2)}, u32[]{:S(2)}) collective-permute-start(bf16[48,1280]{1,0:T(8,128)(2,1)S(1)} %maximum_select_fusion.6), channel_id=1, source_target_pairs={{0,24},{1,25},{2,26},{3,27},{4,28},{5,29},{6,30},{7,31},{8,0},{9,1... | collective-permute-start | bytes 368648 | tf_op jit(solution)/shard_map/ppermute | solution.py:70
  24.3 5.9 %collective-permute-done.2 = bf16[48,1280]{1,0:T(8,128)(2,1)S(1)} collective-permute-done((bf16[48,1280]{1,0:T(8,128)(2,1)S(1)}, bf16[48,1280]{1,0:T(8,128)(2,1)S(1)}, u32[]{:S(2)}, u32[]{:S(2)}) %collective-permute-start.2) | collective-permute-done | bytes 122912 | tf_op jit(solution)/shard_map/ppermute | solution.py:70
  35.9 1.9 collective-permute-start.9
  37.8 2.2 collective-permute-done.7
  40.0 11.1 %collective-permute-done.8 = bf16[48,1920]{1,0:T(8,128)(2,1)S(1)} collective-permute-done((bf16[48,1920]{1,0:T(8,128)(2,1)S(1)}, bf16[48,1920]{1,0:T(8,128)(2,1)S(1)}, u32[]{:S(2)}, u32[]{:S(2)}) %collective-permute-start.8) | collective-permute-done | bytes 184352 | tf_op jit(solution)/shard_map/ppermute | solution.py:70
  54.9 4.7 %collective-permute-done.14 = bf16[192,384]{1,0:T(8,128)(2,1)S(1)} collective-permute-done((bf16[192,384]{1,0:T(8,128)(2,1)S(1)}, bf16[192,384]{1,0:T(8,128)(2,1)S(1)}, u32[]{:S(2)}, u32[]{:S(2)}) %collective-permute-start.14) | collective-permute-done | bytes 147488 | tf_op jit(solution)/shard_map/ppermute | solution.py:70
  59.6 6.8 %collective-permute-start.16 = (bf16[192,384]{1,0:T(8,128)(2,1)S(1)}, bf16[192,384]{1,0:T(8,128)(2,1)S(1)}, u32[]{:S(2)}, u32[]{:S(2)}) collective-permute-start(bf16[192,384]{1,0:T(8,128)(2,1)S(1)} %maximum_select_fusion.3), channel_id=1, source_target_pairs={{0,8},{1,9},{2,10},{3,11},{4,12},{5,13},{6,14},{7,15},{8,16},{9,17... | collective-permute-start | bytes 442376 | tf_op jit(solution)/shard_map/ppermute | solution.py:70
  66.4 9.6 %collective-permute-done.15 = bf16[192,384]{1,0:T(8,128)(2,1)S(1)} collective-permute-done((bf16[192,384]{1,0:T(8,128)(2,1)S(1)}, bf16[192,384]{1,0:T(8,128)(2,1)S(1)}, u32[]{:S(2)}, u32[]{:S(2)}) %collective-permute-start.15) | collective-permute-done | bytes 147488 | tf_op jit(solution)/shard_map/ppermute | solution.py:70
  83.3 11.0 %seg_attention.1 = (bf16[512,2304]{1,0:T(8,128)(2,1)}, bf16[512,768]{1,0:T(8,128)(2,1)}, bf16[2,768,128]{2,1,0:T(8,128)(2,1)}, f32[2,48,768]{2,1,0:T(8,128)}, f32[8,768]{1,0:T(8,128)}) custom-call(s32[6]{0:T(128)} %stack.27.refs_0_, f32[512,768]{1,0:T(8,128)} %refs_6_.3, s32[512,1]{1,0:T(8,128)} %copy.55.refs_2_.refs_4_, s32[4,128]{1,0:T(4,128)} %bitcast.32, ...), custom_call_target="tpu_custom_call" | custom-call | flops 1811939328 | bytes 9367552 | tf_op jit(solution)/shard_map/seg_attention/pallas_call | solution.py:490
  100.3 10.7 %collective-permute-done.25.refs_16_.refs_23_ = bf16[768,384]{1,0:T(8,128)(2,1)} collective-permute-done((bf16[768,384]{1,0:T(8,128)(2,1)S(1)}, bf16[768,384]{1,0:T(8,128)(2,1)}, u32[]{:S(2)}, u32[]{:S(2)}) %collective-permute-start.25) | collective-permute-done | bytes 589856 | tf_op jit(solution)/shard_map/ppermute | solution.py:70
  112.0 5.6 %collective-permute-start.27 = (bf16[192,1920]{1,0:T(8,128)(2,1)}, bf16[192,1920]{1,0:T(8,128)(2,1)S(1)}, u32[]{:S(2)}, u32[]{:S(2)}) collective-permute-start(bf16[192,1920]{1,0:T(8,128)(2,1)} %collective-permute-done.24.refs_10_.refs_17_), channel_id=1, source_target_pairs={{0,1},{1,0},{2,3},{3,2},{4,5},{5,4},{6,7},{7,6},{8,9},{9,8},{10,11... | collective-permute-start | bytes 2211848 | tf_op jit(solution)/shard_map/ppermute | solution.py:70
  122.2 9.6 %collective-permute-done.31.refs_18_.refs_25_ = bf16[768,384]{1,0:T(8,128)(2,1)} collective-permute-done((bf16[768,384]{1,0:T(8,128)(2,1)}, bf16[768,384]{1,0:T(8,128)(2,1)}, u32[]{:S(2)}, u32[]{:S(2)}) %collective-permute-start.31) | collective-permute-done | bytes 589856 | tf_op jit(solution)/shard_map/ppermute | solution.py:70
  134.8 43.1 %seg_block.1 = (f32[512,768]{1,0:T(8,128)}, f32[8,768]{1,0:T(8,128)}, bf16[512,768]{1,0:T(8,128)(2,1)}, f32[512,768]{1,0:T(8,128)}, f32[8,768]{1,0:T(8,128)}, /*...) custom-call(s32[6]{0:T(128)} %stack.27.refs_0_, ...), custom_call_target="tpu_custom_call" | custom-call | flops 16307453952 | bytes 29739076 | tf_op jit(solution)/shard_map/seg_block/pallas_call | solution.py:490
  180.1 7.6 %all-gather = f32[4,4,1664]{2,1,0:T(4,128)S(1)} all-gather(f32[1,4,1664]{2,1,0:T(4,128)S(1)} %maximum_bitcast_fusion), channel_id=1, replica_groups=mesh['dp'=8,'fsdp'=4] {'fsdp'}, dimensions={0}, use_global_device_ids=true | all-gather | bytes 133120 | tf_op jit(solution)/shard_map/all_gather | solution.py:1474
  188.4 4.6 %add_convert_fusion = bf16[384,3456]{1,0:T(8,128)(2,1)} fusion(bf16[768,3456]{1,0:T(8,128)(2,1)} %collective-permute-done.33, bf16[768,3456]{1,0:T(8,128)(2,1)} %get-tuple-element.209), kind=kLoop, calls=%fused_computation | loop fusion | flops 5308416 | bytes 7962624 | tf_op jit(solution)/shard_map/convert_element_type | solution.py:151
  193.0 2.5 collective-permute-start.36
  195.5 20.8 %cls_block.1 = (f32[512,768]{1,0:T(8,128)}, bf16[512,768]{1,0:T(8,128)(2,1)}, f32[512,768]{1,0:T(8,128)}, bf16[8,12288]{1,0:T(8,128)(2,1)}, f32[8,768]{1,0:T(8,128)}, /*index=5*/f32[1,3072]{1,0:T(1,128)}) custom-call(s32[6]{0:T(128)} %stack.27.refs_0_, f32[16,1664]{1,0:T(8,128)} %reshape.91.refs_1_, ...), custom_call_target="tpu_custom_call", output_to_operand_aliasing={{0}: (30, {}), {1}: (31, {}), {2}: (32, {})} | custom-call | flops 452984832 | bytes 25714756 | tf_op jit(solution)/shard_map/cls_block/pallas_call | solution.py:490
  216.3 9.4 %collective-permute-done.36 = bf16[384,3456]{1,0:T(8,128)(2,1)S(1)} collective-permute-done((bf16[384,3456]{1,0:T(8,128)(2,1)}, bf16[384,3456]{1,0:T(8,128)(2,1)S(1)}, u32[]{:S(2)}, u32[]{:S(2)}) %collective-permute-start.36) | collective-permute-done | bytes 2654240 | tf_op jit(solution)/shard_map/ppermute | solution.py:70
  225.7 3.4 add_convert_fusion.1
  230.3 24.5 %seg_attention_back.1 = (f32[512,768]{1,0:T(8,128)}, bf16[768,1280]{1,0:T(8,128)(2,1)}, bf16[768,1280]{1,0:T(8,128)(2,1)}) custom-call(s32[6]{0:T(128)} %stack.27.refs_0_, bf16[512,2304]{1,0:T(8,128)(2,1)} %get-tuple-element.224.refs_1_, bf16[512,768]{1,0:T(8,128)(2,1)} %get-tuple-element.225.refs_2_, f32[512,768]{1,0:T(8,128)} %get-tuple-element.226.refs_3_, ...), custom_call_target="tpu_custom_call" | custom-call | flops 3623878656 | bytes 15794176 | tf_op jit(solution)/shard_map/seg_attention_back/pallas_call | solution.py:490
  256.1 1.8 add_convert_fusion.8
  260.0 9.8 %collective-permute-done.39 = bf16[48,3456]{1,0:T(8,128)(2,1)S(1)} collective-permute-done((bf16[48,3456]{1,0:T(8,128)(2,1)S(1)}, bf16[48,3456]{1,0:T(8,128)(2,1)S(1)}, u32[]{:S(2)}, u32[]{:S(2)}) %collective-permute-start.39) | collective-permute-done | bytes 331808 | tf_op jit(solution)/shard_map/ppermute | solution.py:166
  273.3 4.3 %collective-permute-start.42 = (bf16[48,3456]{1,0:T(8,128)(2,1)S(1)}, bf16[48,3456]{1,0:T(8,128)(2,1)S(1)}, u32[]{:S(2)}, u32[]{:S(2)}) collective-permute-start(bf16[48,3456]{1,0:T(8,128)(2,1)S(1)} %fusion), channel_id=1, source_target_pairs={{0,8},{1,9},{2,10},{3,11},{4,12},{5,13},{6,14},{7,15},{8,16},{9,17... | collective-permute-start | bytes 995336 | tf_op jit(solution)/shard_map/ppermute | solution.py:166
  278.3 12.2 %collective-permute-done.42 = bf16[48,3456]{1,0:T(8,128)(2,1)S(1)} collective-permute-done((bf16[48,3456]{1,0:T(8,128)(2,1)S(1)}, bf16[48,3456]{1,0:T(8,128)(2,1)S(1)}, u32[]{:S(2)}, u32[]{:S(2)}) %collective-permute-start.42) | collective-permute-done | bytes 331808 | tf_op jit(solution)/shard_map/ppermute | solution.py:166
  290.5 4.9 %collective-permute-done.41 = bf16[384,1280]{1,0:T(8,128)(2,1)S(1)} collective-permute-done((bf16[384,1280]{1,0:T(8,128)(2,1)S(1)}, bf16[384,1280]{1,0:T(8,128)(2,1)S(1)}, u32[]{:S(2)}, u32[]{:S(2)}) %collective-permute-start.41) | collective-permute-done | bytes 983072 | tf_op jit(solution)/shard_map/ppermute | solution.py:70
  296.4 4.4 %collective-permute-start.45 = (bf16[48,3456]{1,0:T(8,128)(2,1)S(1)}, bf16[48,3456]{1,0:T(8,128)(2,1)S(1)}, u32[]{:S(2)}, u32[]{:S(2)}) collective-permute-start(bf16[48,3456]{1,0:T(8,128)(2,1)S(1)} %add_convert_fusion.6), channel_id=1, source_target_pairs={{0,8},{1,9},{2,10},{3,11},{4,12},{5,13},{6,14},{7,15},{8,16},{9,17... | collective-permute-start | bytes 995336 | tf_op jit(solution)/shard_map/ppermute | solution.py:166
  302.2 5.4 %collective-permute-done.45 = bf16[48,3456]{1,0:T(8,128)(2,1)S(1)} collective-permute-done((bf16[48,3456]{1,0:T(8,128)(2,1)S(1)}, bf16[48,3456]{1,0:T(8,128)(2,1)S(1)}, u32[]{:S(2)}, u32[]{:S(2)}) %collective-permute-start.45) | collective-permute-done | bytes 331808 | tf_op jit(solution)/shard_map/ppermute | solution.py:166
  307.5 4.9 %collective-permute-done.46 = bf16[48,3456]{1,0:T(8,128)(2,1)S(1)} collective-permute-done((bf16[48,3456]{1,0:T(8,128)(2,1)S(1)}, bf16[48,3456]{1,0:T(8,128)(2,1)S(1)}, u32[]{:S(2)}, u32[]{:S(2)}) %collective-permute-start.46) | collective-permute-done | bytes 331808 | tf_op jit(solution)/shard_map/ppermute | solution.py:166
  312.6 1.8 collective-permute-start.47
  314.4 2.7 collective-permute-start.49
  319.3 9.2 %cls_weight_grads.1 = (f32[24,2304]{1,0:T(8,128)}, f32[24,768]{1,0:T(8,128)}, f32[24,3072]{1,0:T(8,128)}, f32[96,768]{1,0:T(8,128)}, f32[2,24]{1,0:T(2,128)}, /*...) custom-call(s32[6]{0:T(128)} %stack.27.refs_0_, ...), custom_call_target="tpu_custom_call" | custom-call | flops 327680000 | bytes 7842436 | tf_op jit(solution)/shard_map/cls_weight_grads/pallas_call | solution.py:490
  (204 shorter events, 61.4 us)
Async XLA Ops:
  7.2 188.3 %all-gather.4.cloned.1.call-start = ((), (), s32[]{:S(2)}) async-start(), calls=%async_computation | async-start | bytes 14598144 | tf_op jit(solution)/shard_map/all_gather | solution.py:141
  30.3 20.9 %collective-permute-start.5 = (bf16[192,1280]{1,0:T(8,128)(2,1)S(1)}, bf16[192,1280]{1,0:T(8,128)(2,1)}, u32[]{:S(2)}, u32[]{:S(2)}) collective-permute-start(bf16[192,1280]{1,0:T(8,128)(2,1)S(1)} %pad_maximum_fusion.refs_4_.refs_10_), channel_id=1, source_target_pairs={{0,4},{1,3},{2,6},{3,1},{4,0},{5,7},{6,2},{7,5},{8,12},{9,11},{10,... | collective-permute-start | bytes 1474568 | tf_op jit(solution)/shard_map/ppermute | solution.py:70
  31.9 19.3 %collective-permute-start.6 = (bf16[192,1280]{1,0:T(8,128)(2,1)S(1)}, bf16[192,1280]{1,0:T(8,128)(2,1)}, u32[]{:S(2)}, u32[]{:S(2)}) collective-permute-start(bf16[192,1280]{1,0:T(8,128)(2,1)S(1)} %pad_maximum_fusion.refs_4_.refs_10_), channel_id=1, source_target_pairs={{0,2},{1,5},{2,0},{3,7},{4,6},{5,1},{6,4},{7,3},{8,10},{9,13},{10,... | collective-permute-start | bytes 1474568 | tf_op jit(solution)/shard_map/ppermute | solution.py:70
  34.9 16.3 %collective-permute-start.8 = (bf16[48,1920]{1,0:T(8,128)(2,1)S(1)}, bf16[48,1920]{1,0:T(8,128)(2,1)S(1)}, u32[]{:S(2)}, u32[]{:S(2)}) collective-permute-start(bf16[48,1920]{1,0:T(8,128)(2,1)S(1)} %maximum_select_fusion.1), channel_id=1, source_target_pairs={{0,16},{1,17},{2,18},{3,19},{4,20},{5,21},{6,22},{7,23},{8,24},{9,... | collective-permute-start | bytes 552968 | tf_op jit(solution)/shard_map/ppermute | solution.py:70
  35.9 15.3 %collective-permute-start.9 = (bf16[48,1920]{1,0:T(8,128)(2,1)S(1)}, bf16[48,1920]{1,0:T(8,128)(2,1)S(1)}, u32[]{:S(2)}, u32[]{:S(2)}) collective-permute-start(bf16[48,1920]{1,0:T(8,128)(2,1)S(1)} %maximum_select_fusion.1), channel_id=1, source_target_pairs={{0,8},{1,9},{2,10},{3,11},{4,12},{5,13},{6,14},{7,15},{8,16},{9,17... | collective-permute-start | bytes 552968 | tf_op jit(solution)/shard_map/ppermute | solution.py:70
  51.2 268.0 %all-gather.6.cloned.1.call-start = ((), (), s32[]{:S(2)}) async-start(), calls=%async_computation.1 | async-start | bytes 6488064 | tf_op jit(solution)/shard_map/all_gather | solution.py:1490
  51.4 25.2 %collective-permute-start.12 = (bf16[192,1920]{1,0:T(8,128)(2,1)S(1)}, bf16[192,1920]{1,0:T(8,128)(2,1)S(1)}, u32[]{:S(2)}, u32[]{:S(2)}) collective-permute-start(bf16[192,1920]{1,0:T(8,128)(2,1)S(1)} %constant_dynamic-update-slice_fusion.refs_7_.refs_14_), channel_id=1, source_target_pairs={{0,4},{1,3},{2,6},{3,1},{4,0},{5,7},{6,2},{7,5},{8,12},{9,11},{10,... | collective-permute-start | bytes 2211848 | tf_op jit(solution)/shard_map/ppermute | solution.py:70
  52.0 24.6 %collective-permute-start.13 = (bf16[192,1920]{1,0:T(8,128)(2,1)S(1)}, bf16[192,1920]{1,0:T(8,128)(2,1)}, u32[]{:S(2)}, u32[]{:S(2)}) collective-permute-start(bf16[192,1920]{1,0:T(8,128)(2,1)S(1)} %constant_dynamic-update-slice_fusion.refs_7_.refs_14_), channel_id=1, source_target_pairs={{0,2},{1,5},{2,0},{3,7},{4,6},{5,1},{6,4},{7,3},{8,10},{9,13},{10,... | collective-permute-start | bytes 2211848 | tf_op jit(solution)/shard_map/ppermute | solution.py:70
  52.5 24.0 %collective-permute-start.11 = (bf16[192,1280]{1,0:T(8,128)(2,1)}, bf16[192,1280]{1,0:T(8,128)(2,1)}, u32[]{:S(2)}, u32[]{:S(2)}) collective-permute-start(bf16[192,1280]{1,0:T(8,128)(2,1)} %collective-permute-done.5.refs_5_.refs_11_), channel_id=1, source_target_pairs={{0,2},{1,5},{2,0},{3,7},{4,6},{5,1},{6,4},{7,3},{8,10},{9,13},{10,... | collective-permute-start | bytes 1474568 | tf_op jit(solution)/shard_map/ppermute | solution.py:70
  54.0 22.0 %collective-permute-start.15 = (bf16[192,384]{1,0:T(8,128)(2,1)S(1)}, bf16[192,384]{1,0:T(8,128)(2,1)S(1)}, u32[]{:S(2)}, u32[]{:S(2)}) collective-permute-start(bf16[192,384]{1,0:T(8,128)(2,1)S(1)} %maximum_select_fusion.3), channel_id=1, source_target_pairs={{0,16},{1,17},{2,18},{3,19},{4,20},{5,21},{6,22},{7,23},{8,24},{9,... | collective-permute-start | bytes 442376 | tf_op jit(solution)/shard_map/ppermute | solution.py:70
  59.6 16.4 %collective-permute-start.16 = (bf16[192,384]{1,0:T(8,128)(2,1)S(1)}, bf16[192,384]{1,0:T(8,128)(2,1)S(1)}, u32[]{:S(2)}, u32[]{:S(2)}) collective-permute-start(bf16[192,384]{1,0:T(8,128)(2,1)S(1)} %maximum_select_fusion.3), channel_id=1, source_target_pairs={{0,8},{1,9},{2,10},{3,11},{4,12},{5,13},{6,14},{7,15},{8,16},{9,17... | collective-permute-start | bytes 442376 | tf_op jit(solution)/shard_map/ppermute | solution.py:70
  78.0 17.4 %collective-permute-start.21 = (bf16[192,1920]{1,0:T(8,128)(2,1)S(1)}, bf16[192,1920]{1,0:T(8,128)(2,1)S(1)}, u32[]{:S(2)}, u32[]{:S(2)}) collective-permute-start(bf16[192,1920]{1,0:T(8,128)(2,1)S(1)} %constant_dynamic-update-slice_fusion.refs_7_.refs_14_), channel_id=1, source_target_pairs={{0,1},{1,0},{2,3},{3,2},{4,5},{5,4},{6,7},{7,6},{8,9},{9,8},{10,11... | collective-permute-start | bytes 2211848 | tf_op jit(solution)/shard_map/ppermute | solution.py:70
  81.0 31.0 %collective-permute-start.22 = (bf16[192,1920]{1,0:T(8,128)(2,1)S(1)}, bf16[192,1920]{1,0:T(8,128)(2,1)}, u32[]{:S(2)}, u32[]{:S(2)}) collective-permute-start(bf16[192,1920]{1,0:T(8,128)(2,1)S(1)} %collective-permute-done.12.refs_8_.refs_15_), channel_id=1, source_target_pairs={{0,1},{1,0},{2,3},{3,2},{4,5},{5,4},{6,7},{7,6},{8,9},{9,8},{10,11... | collective-permute-start | bytes 2211848 | tf_op jit(solution)/shard_map/ppermute | solution.py:70
  81.5 30.5 %collective-permute-start.24 = (bf16[192,1920]{1,0:T(8,128)(2,1)S(1)}, bf16[192,1920]{1,0:T(8,128)(2,1)}, u32[]{:S(2)}, u32[]{:S(2)}) collective-permute-start(bf16[192,1920]{1,0:T(8,128)(2,1)S(1)} %collective-permute-done.12.refs_8_.refs_15_), channel_id=1, source_target_pairs={{0,2},{1,5},{2,0},{3,7},{4,6},{5,1},{6,4},{7,3},{8,10},{9,13},{10,... | collective-permute-start | bytes 2211848 | tf_op jit(solution)/shard_map/ppermute | solution.py:70
  82.6 29.5 %collective-permute-start.23 = (bf16[192,1920]{1,0:T(8,128)(2,1)}, bf16[192,1920]{1,0:T(8,128)(2,1)}, u32[]{:S(2)}, u32[]{:S(2)}) collective-permute-start(bf16[192,1920]{1,0:T(8,128)(2,1)} %collective-permute-done.13.refs_9_.refs_16_), channel_id=1, source_target_pairs={{0,1},{1,0},{2,3},{3,2},{4,5},{5,4},{6,7},{7,6},{8,9},{9,8},{10,11... | collective-permute-start | bytes 2211848 | tf_op jit(solution)/shard_map/ppermute | solution.py:70
  82.6 28.4 %collective-permute-start.25 = (bf16[768,384]{1,0:T(8,128)(2,1)S(1)}, bf16[768,384]{1,0:T(8,128)(2,1)}, u32[]{:S(2)}, u32[]{:S(2)}) collective-permute-start(bf16[768,384]{1,0:T(8,128)(2,1)S(1)} %constant_dynamic-update-slice_fusion.4.refs_15_.refs_22_), channel_id=1, source_target_pairs={{0,4},{1,3},{2,6},{3,1},{4,0},{5,7},{6,2},{7,5},{8,12},{9,11},{10,... | collective-permute-start | bytes 1769480 | tf_op jit(solution)/shard_map/ppermute | solution.py:70
  95.4 16.6 %collective-permute-start.26 = (bf16[768,384]{1,0:T(8,128)(2,1)S(1)}, bf16[768,384]{1,0:T(8,128)(2,1)}, u32[]{:S(2)}, u32[]{:S(2)}) collective-permute-start(bf16[768,384]{1,0:T(8,128)(2,1)S(1)} %constant_dynamic-update-slice_fusion.4.refs_15_.refs_22_), channel_id=1, source_target_pairs={{0,2},{1,5},{2,0},{3,7},{4,6},{5,1},{6,4},{7,3},{8,10},{9,13},{10,... | collective-permute-start | bytes 1769480 | tf_op jit(solution)/shard_map/ppermute | solution.py:70
  112.0 19.8 %collective-permute-start.27 = (bf16[192,1920]{1,0:T(8,128)(2,1)}, bf16[192,1920]{1,0:T(8,128)(2,1)S(1)}, u32[]{:S(2)}, u32[]{:S(2)}) collective-permute-start(bf16[192,1920]{1,0:T(8,128)(2,1)} %collective-permute-done.24.refs_10_.refs_17_), channel_id=1, source_target_pairs={{0,1},{1,0},{2,3},{3,2},{4,5},{5,4},{6,7},{7,6},{8,9},{9,8},{10,11... | collective-permute-start | bytes 2211848 | tf_op jit(solution)/shard_map/ppermute | solution.py:70
  118.2 13.6 %collective-permute-start.31 = (bf16[768,384]{1,0:T(8,128)(2,1)}, bf16[768,384]{1,0:T(8,128)(2,1)}, u32[]{:S(2)}, u32[]{:S(2)}) collective-permute-start(bf16[768,384]{1,0:T(8,128)(2,1)} %collective-permute-done.25.refs_16_.refs_23_), channel_id=1, source_target_pairs={{0,2},{1,5},{2,0},{3,7},{4,6},{5,1},{6,4},{7,3},{8,10},{9,13},{10,... | collective-permute-start | bytes 1769480 | tf_op jit(solution)/shard_map/ppermute | solution.py:70
  193.0 32.7 %collective-permute-start.36 = (bf16[384,3456]{1,0:T(8,128)(2,1)}, bf16[384,3456]{1,0:T(8,128)(2,1)S(1)}, u32[]{:S(2)}, u32[]{:S(2)}) collective-permute-start(bf16[384,3456]{1,0:T(8,128)(2,1)} %add_convert_fusion), channel_id=1, source_target_pairs={{0,2},{1,5},{2,0},{3,7},{4,6},{5,1},{6,4},{7,3},{8,10},{9,13},{10,... | collective-permute-start | bytes 7962632 | tf_op jit(solution)/shard_map/ppermute | solution.py:70
  229.1 25.7 %collective-permute-start.37 = (bf16[192,3456]{1,0:T(8,128)(2,1)}, bf16[192,3456]{1,0:T(8,128)(2,1)}, u32[]{:S(2)}, u32[]{:S(2)}) collective-permute-start(bf16[192,3456]{1,0:T(8,128)(2,1)} %add_convert_fusion.1), channel_id=1, source_target_pairs={{0,4},{1,3},{2,6},{3,1},{4,0},{5,7},{6,2},{7,5},{8,12},{9,11},{10,... | collective-permute-start | bytes 3981320 | tf_op jit(solution)/shard_map/ppermute | solution.py:70
  254.8 15.0 %collective-permute-start.38 = (bf16[768,1280]{1,0:T(8,128)(2,1)}, bf16[768,1280]{1,0:T(8,128)(2,1)S(1)}, u32[]{:S(2)}, u32[]{:S(2)}) collective-permute-start(bf16[768,1280]{1,0:T(8,128)(2,1)} %get-tuple-element.235), channel_id=1, source_target_pairs={{0,1},{1,0},{2,3},{3,2},{4,5},{5,4},{6,7},{7,6},{8,9},{9,8},{10,11... | collective-permute-start | bytes 5898248 | tf_op jit(solution)/shard_map/ppermute | solution.py:70
  258.0 11.9 %collective-permute-start.39 = (bf16[48,3456]{1,0:T(8,128)(2,1)S(1)}, bf16[48,3456]{1,0:T(8,128)(2,1)S(1)}, u32[]{:S(2)}, u32[]{:S(2)}) collective-permute-start(bf16[48,3456]{1,0:T(8,128)(2,1)S(1)} %get-tuple-element.341), channel_id=1, source_target_pairs={{0,8},{1,9},{2,10},{3,11},{4,12},{5,13},{6,14},{7,15}} | collective-permute-start | bytes 995336 | tf_op jit(solution)/shard_map/ppermute | solution.py:166
  270.1 25.4 %collective-permute-start.41 = (bf16[384,1280]{1,0:T(8,128)(2,1)S(1)}, bf16[384,1280]{1,0:T(8,128)(2,1)S(1)}, u32[]{:S(2)}, u32[]{:S(2)}) collective-permute-start(bf16[384,1280]{1,0:T(8,128)(2,1)S(1)} %add_convert_fusion.2), channel_id=1, source_target_pairs={{0,2},{1,5},{2,0},{3,7},{4,6},{5,1},{6,4},{7,3},{8,10},{9,13},{10,... | collective-permute-start | bytes 2949128 | tf_op jit(solution)/shard_map/ppermute | solution.py:70
  273.3 17.2 %collective-permute-start.42 = (bf16[48,3456]{1,0:T(8,128)(2,1)S(1)}, bf16[48,3456]{1,0:T(8,128)(2,1)S(1)}, u32[]{:S(2)}, u32[]{:S(2)}) collective-permute-start(bf16[48,3456]{1,0:T(8,128)(2,1)S(1)} %fusion), channel_id=1, source_target_pairs={{0,8},{1,9},{2,10},{3,11},{4,12},{5,13},{6,14},{7,15},{8,16},{9,17... | collective-permute-start | bytes 995336 | tf_op jit(solution)/shard_map/ppermute | solution.py:166
  277.6 12.9 %collective-permute-start.43 = (bf16[48,3456]{1,0:T(8,128)(2,1)S(1)}, bf16[48,3456]{1,0:T(8,128)(2,1)S(1)}, u32[]{:S(2)}, u32[]{:S(2)}) collective-permute-start(bf16[48,3456]{1,0:T(8,128)(2,1)S(1)} %get-tuple-element.336), channel_id=1, source_target_pairs={{16,8},{17,9},{18,10},{19,11},{20,12},{21,13},{22,14},{23,15},{24,... | collective-permute-start | bytes 995336 | tf_op jit(solution)/shard_map/ppermute | solution.py:166
  295.7 16.8 %collective-permute-start.44 = (bf16[192,1280]{1,0:T(8,128)(2,1)S(1)}, bf16[192,1280]{1,0:T(8,128)(2,1)S(1)}, u32[]{:S(2)}, u32[]{:S(2)}) collective-permute-start(bf16[192,1280]{1,0:T(8,128)(2,1)S(1)} %add_convert_fusion.3), channel_id=1, source_target_pairs={{0,4},{1,3},{2,6},{3,1},{4,0},{5,7},{6,2},{7,5},{8,12},{9,11},{10,... | collective-permute-start | bytes 1474568 | tf_op jit(solution)/shard_map/ppermute | solution.py:70
  296.4 11.2 %collective-permute-start.45 = (bf16[48,3456]{1,0:T(8,128)(2,1)S(1)}, bf16[48,3456]{1,0:T(8,128)(2,1)S(1)}, u32[]{:S(2)}, u32[]{:S(2)}) collective-permute-start(bf16[48,3456]{1,0:T(8,128)(2,1)S(1)} %add_convert_fusion.6), channel_id=1, source_target_pairs={{0,8},{1,9},{2,10},{3,11},{4,12},{5,13},{6,14},{7,15},{8,16},{9,17... | collective-permute-start | bytes 995336 | tf_op jit(solution)/shard_map/ppermute | solution.py:166
  300.9 11.6 %collective-permute-start.46 = (bf16[48,3456]{1,0:T(8,128)(2,1)S(1)}, bf16[48,3456]{1,0:T(8,128)(2,1)S(1)}, u32[]{:S(2)}, u32[]{:S(2)}) collective-permute-start(bf16[48,3456]{1,0:T(8,128)(2,1)S(1)} %add_convert_fusion.5), channel_id=1, source_target_pairs={{8,0},{9,1},{10,2},{11,3},{12,4},{13,5},{14,6},{15,7},{16,8},{17,9... | collective-permute-start | bytes 995336 | tf_op jit(solution)/shard_map/ppermute | solution.py:166
  312.6 15.9 %collective-permute-start.47 = (bf16[48,1280]{1,0:T(8,128)(2,1)S(1)}, bf16[48,1280]{1,0:T(8,128)(2,1)}, u32[]{:S(2)}, u32[]{:S(2)}) collective-permute-start(bf16[48,1280]{1,0:T(8,128)(2,1)S(1)} %get-tuple-element.344), channel_id=1, source_target_pairs={{0,8},{1,9},{2,10},{3,11},{4,12},{5,13},{6,14},{7,15},{8,16},{9,17... | collective-permute-start | bytes 368648 | tf_op jit(solution)/shard_map/ppermute | solution.py:70
  314.4 14.1 %collective-permute-start.48 = (bf16[48,1280]{1,0:T(8,128)(2,1)S(1)}, bf16[48,1280]{1,0:T(8,128)(2,1)}, u32[]{:S(2)}, u32[]{:S(2)}) collective-permute-start(bf16[48,1280]{1,0:T(8,128)(2,1)S(1)} %get-tuple-element.343), channel_id=1, source_target_pairs={{0,16},{1,17},{2,18},{3,19},{4,20},{5,21},{6,22},{7,23},{8,24},{9,... | collective-permute-start | bytes 368648 | tf_op jit(solution)/shard_map/ppermute | solution.py:70
  314.4 14.1 %collective-permute-start.49 = (bf16[48,1280]{1,0:T(8,128)(2,1)S(1)}, bf16[48,1280]{1,0:T(8,128)(2,1)}, u32[]{:S(2)}, u32[]{:S(2)}) collective-permute-start(bf16[48,1280]{1,0:T(8,128)(2,1)S(1)} %get-tuple-element.342), channel_id=1, source_target_pairs={{0,24},{1,25},{2,26},{3,27},{4,28},{5,29},{6,30},{7,31},{8,0},{9,1... | collective-permute-start | bytes 368648 | tf_op jit(solution)/shard_map/ppermute | solution.py:70
  (47 other events, 547.6 us)
Sparse Core Ops, SparseCore 0:
  51.3 120.6 all-gather.3
  225.8 76.2 all-gather.5

commit v5 on v4

--- a/solution.py
+++ b/solution.py
@@ -1263,7 +1263,7 @@
             pltpu.VMEM((count, 3 * features), LOW),
             pltpu.VMEM((count, features), LOW),
             pltpu.VMEM((2, 8, features), F32),
-            pltpu.VMEM((TILE_ROWS, count), LOW),
+            pltpu.VMEM((features, count), LOW),
             pltpu.SemaphoreType.DMA,
         ],
         place,
@@ -1455,12 +1455,11 @@
     if grid.pieces:
         mixed, (others, last, threes) = sync((mixed, under_way))
         two, three = two + (last,), (three,) + tuple(threes)
-        mixed, (more, others_fc2, last) = sync(
-            (mixed, (grid.send(last, "core"), grid.swap(three), grid.send(threes[0], "second")))
-        )
+        mixed, (more, last) = sync((mixed, (grid.send(last, "core"), grid.send(threes[0], "second"))))
         group_near = grid.grouped(two, tuple(others) + (more,), half, wide_half)
-        mixed, more = sync((mixed, grid.send(last, "core")))
-        group_fc2 = grid.grouped(three + (last,), tuple(others_fc2) + (more,), half)
+        three = three + (last,)
+        mixed, others_fc2 = sync((mixed, grid.swap(three)))
+        group_fc2 = grid.grouped(three, others_fc2, half)
     def cls_only(rows):
         return rows.reshape(windows, SEG, -1)[:, 0]
 

time: 347 us -> 344 us (level)
  transfers between devices with their start and end apart: 55 -> 55, of which waited for: 19 -> 16; matrix products, arithmetic and copies ran while one was open for 10% -> 10% of each run, Pallas kernels for 32% -> 32%
where the time goes in v5:
time: 344 us; the launch traced here: 340 us
  Pallas kernels  112 us (33%)
  waiting for transfers between devices  105 us (31%)
  starting transfers between devices  62.5 us (18%)
  other arithmetic  23.8 us (7%)
  between operations  15.7 us (5%)
  local copies, waits for them, and re-layouts  14.1 us (4%)
  blocking collectives  7.63 us (2%)
    pallas_call x6, Pallas kernels, call(): pl.pallas_call(body, out_shape=tuple((jax.ShapeDtypeStruct(c.shape, c.dty...  112 us
    ppermute x47, waiting for transfers between devices, send(): return lax.ppermute(value, AXES, self.pairs(axis, step))  70.8 us
    ppermute x47, starting transfers between devices, send(): return lax.ppermute(value, AXES, self.pairs(axis, step))  49.5 us
    ppermute x6, waiting for transfers between devices, deliver(): out.append(lax.ppermute(made, AXES, self.line_pairs(t, step)))  33.7 us
    convert_element_type x8, other arithmetic, total(): return made.astype(jnp.bfloat16)  13.2 us
    ppermute x6, starting transfers between devices, deliver(): out.append(lax.ppermute(made, AXES, self.line_pairs(t, step)))  12.9 us
    all_gather x1, blocking collectives, per_device(): lax.all_gather(jnp.concatenate(gathered, axis=1), 'fsdp', axis=0, tiled=T...  7.63 us
  transfers between devices with their start and end apart: 55, of which 16 were waited for; matrix products, arithmetic and copies ran while one was open for 10% of the time, Pallas kernels for 32%

profile of v5, /device:TPU:0, one launch (start us, length us, event | category | flops | bytes accessed | tf_op | source)
XLA Modules:
  0.0 340.0 jit_solution(8591227510224150322)
XLA Ops:
  7.9 3.6 %pack.1 = (bf16[24,1280]{1,0:T(8,128)(2,1)}, bf16[24,1280]{1,0:T(8,128)(2,1)}, bf16[24,1920]{1,0:T(8,128)(2,1)}, bf16[24,1920]{1,0:T(8,128)(2,1)}, bf16[24,3072]...) custom-call(s32[6]{0:T(128)} %stack.27.refs_0_, ...), custom_call_target="tpu_custom_call" | custom-call | bytes 2672384 | tf_op jit(solution)/shard_map/pack/pallas_call | solution.py:490
  14.1 5.0 %collective-permute-start.1 = (bf16[48,1280]{1,0:T(8,128)(2,1)S(1)}, bf16[48,1280]{1,0:T(8,128)(2,1)S(1)}, u32[]{:S(2)}, u32[]{:S(2)}) collective-permute-start(bf16[48,1280]{1,0:T(8,128)(2,1)S(1)} %maximum_select_fusion.6), channel_id=1, source_target_pairs={{0,24},{1,25},{2,26},{3,27},{4,28},{5,29},{6,30},{7,31},{8,0},{9,1... | collective-permute-start | bytes 368648 | tf_op jit(solution)/shard_map/ppermute | solution.py:70
  24.3 5.9 %collective-permute-done.2 = bf16[48,1280]{1,0:T(8,128)(2,1)S(1)} collective-permute-done((bf16[48,1280]{1,0:T(8,128)(2,1)S(1)}, bf16[48,1280]{1,0:T(8,128)(2,1)S(1)}, u32[]{:S(2)}, u32[]{:S(2)}) %collective-permute-start.2) | collective-permute-done | bytes 122912 | tf_op jit(solution)/shard_map/ppermute | solution.py:70
  35.8 1.9 collective-permute-start.9
  37.8 2.2 collective-permute-done.7
  40.0 11.1 %collective-permute-done.8 = bf16[48,1920]{1,0:T(8,128)(2,1)S(1)} collective-permute-done((bf16[48,1920]{1,0:T(8,128)(2,1)S(1)}, bf16[48,1920]{1,0:T(8,128)(2,1)S(1)}, u32[]{:S(2)}, u32[]{:S(2)}) %collective-permute-start.8) | collective-permute-done | bytes 184352 | tf_op jit(solution)/shard_map/ppermute | solution.py:70
  54.9 4.7 %collective-permute-done.14 = bf16[192,384]{1,0:T(8,128)(2,1)S(1)} collective-permute-done((bf16[192,384]{1,0:T(8,128)(2,1)S(1)}, bf16[192,384]{1,0:T(8,128)(2,1)S(1)}, u32[]{:S(2)}, u32[]{:S(2)}) %collective-permute-start.14) | collective-permute-done | bytes 147488 | tf_op jit(solution)/shard_map/ppermute | solution.py:70
  59.5 6.8 %collective-permute-start.16 = (bf16[192,384]{1,0:T(8,128)(2,1)S(1)}, bf16[192,384]{1,0:T(8,128)(2,1)S(1)}, u32[]{:S(2)}, u32[]{:S(2)}) collective-permute-start(bf16[192,384]{1,0:T(8,128)(2,1)S(1)} %maximum_select_fusion.3), channel_id=1, source_target_pairs={{0,8},{1,9},{2,10},{3,11},{4,12},{5,13},{6,14},{7,15},{8,16},{9,17... | collective-permute-start | bytes 442376 | tf_op jit(solution)/shard_map/ppermute | solution.py:70
  66.3 9.6 %collective-permute-done.15 = bf16[192,384]{1,0:T(8,128)(2,1)S(1)} collective-permute-done((bf16[192,384]{1,0:T(8,128)(2,1)S(1)}, bf16[192,384]{1,0:T(8,128)(2,1)S(1)}, u32[]{:S(2)}, u32[]{:S(2)}) %collective-permute-start.15) | collective-permute-done | bytes 147488 | tf_op jit(solution)/shard_map/ppermute | solution.py:70
  83.3 11.0 %seg_attention.1 = (bf16[512,2304]{1,0:T(8,128)(2,1)}, bf16[512,768]{1,0:T(8,128)(2,1)}, bf16[2,768,128]{2,1,0:T(8,128)(2,1)}, f32[2,48,768]{2,1,0:T(8,128)}, f32[8,768]{1,0:T(8,128)}) custom-call(s32[6]{0:T(128)} %stack.27.refs_0_, f32[512,768]{1,0:T(8,128)} %refs_6_.3, s32[512,1]{1,0:T(8,128)} %copy.55.refs_2_.refs_4_, s32[4,128]{1,0:T(4,128)} %bitcast.32, ...), custom_call_target="tpu_custom_call" | custom-call | flops 1811939328 | bytes 9367552 | tf_op jit(solution)/shard_map/seg_attention/pallas_call | solution.py:490
  100.3 10.7 %collective-permute-done.25.refs_16_.refs_23_ = bf16[768,384]{1,0:T(8,128)(2,1)} collective-permute-done((bf16[768,384]{1,0:T(8,128)(2,1)S(1)}, bf16[768,384]{1,0:T(8,128)(2,1)}, u32[]{:S(2)}, u32[]{:S(2)}) %collective-permute-start.25) | collective-permute-done | bytes 589856 | tf_op jit(solution)/shard_map/ppermute | solution.py:70
  111.9 5.6 %collective-permute-start.27 = (bf16[192,1920]{1,0:T(8,128)(2,1)}, bf16[192,1920]{1,0:T(8,128)(2,1)S(1)}, u32[]{:S(2)}, u32[]{:S(2)}) collective-permute-start(bf16[192,1920]{1,0:T(8,128)(2,1)} %collective-permute-done.24.refs_10_.refs_17_), channel_id=1, source_target_pairs={{0,1},{1,0},{2,3},{3,2},{4,5},{5,4},{6,7},{7,6},{8,9},{9,8},{10,11... | collective-permute-start | bytes 2211848 | tf_op jit(solution)/shard_map/ppermute | solution.py:70
  119.5 10.4 %collective-permute-done.28.refs_18_.refs_25_ = bf16[768,384]{1,0:T(8,128)(2,1)S(1)} collective-permute-done((bf16[768,384]{1,0:T(8,128)(2,1)}, bf16[768,384]{1,0:T(8,128)(2,1)S(1)}, u32[]{:S(2)}, u32[]{:S(2)}) %collective-permute-start.28) | collective-permute-done | bytes 589856 | tf_op jit(solution)/shard_map/ppermute | solution.py:70
  132.1 43.3 %seg_block.1 = (f32[512,768]{1,0:T(8,128)}, f32[8,768]{1,0:T(8,128)}, bf16[512,768]{1,0:T(8,128)(2,1)}, f32[512,768]{1,0:T(8,128)}, f32[8,768]{1,0:T(8,128)}, /*...) custom-call(s32[6]{0:T(128)} %stack.27.refs_0_, ...), custom_call_target="tpu_custom_call" | custom-call | flops 16307453952 | bytes 29739076 | tf_op jit(solution)/shard_map/seg_block/pallas_call | solution.py:490
  177.4 7.6 %all-gather = f32[4,4,1664]{2,1,0:T(4,128)S(1)} all-gather(f32[1,4,1664]{2,1,0:T(4,128)S(1)} %maximum_bitcast_fusion), channel_id=1, replica_groups=mesh['dp'=8,'fsdp'=4] {'fsdp'}, dimensions={0}, use_global_device_ids=true | all-gather | bytes 133120 | tf_op jit(solution)/shard_map/all_gather | solution.py:1473
  185.7 4.6 %add_convert_fusion = bf16[384,3456]{1,0:T(8,128)(2,1)} fusion(bf16[768,3456]{1,0:T(8,128)(2,1)} %collective-permute-done.33, bf16[768,3456]{1,0:T(8,128)(2,1)} %get-tuple-element.209), kind=kLoop, calls=%fused_computation | loop fusion | flops 5308416 | bytes 7962624 | tf_op jit(solution)/shard_map/convert_element_type | solution.py:151
  190.4 2.6 collective-permute-start.36
  192.9 20.6 %cls_block.1 = (f32[512,768]{1,0:T(8,128)}, bf16[512,768]{1,0:T(8,128)(2,1)}, f32[512,768]{1,0:T(8,128)}, bf16[8,12288]{1,0:T(8,128)(2,1)}, f32[8,768]{1,0:T(8,128)}, /*index=5*/f32[1,3072]{1,0:T(1,128)}) custom-call(s32[6]{0:T(128)} %stack.27.refs_0_, f32[16,1664]{1,0:T(8,128)} %reshape.91.refs_1_, ...), custom_call_target="tpu_custom_call", output_to_operand_aliasing={{0}: (30, {}), {1}: (31, {}), {2}: (32, {})} | custom-call | flops 452984832 | bytes 25714756 | tf_op jit(solution)/shard_map/cls_block/pallas_call | solution.py:490
  213.5 9.6 %collective-permute-done.36 = bf16[384,3456]{1,0:T(8,128)(2,1)S(1)} collective-permute-done((bf16[384,3456]{1,0:T(8,128)(2,1)}, bf16[384,3456]{1,0:T(8,128)(2,1)S(1)}, u32[]{:S(2)}, u32[]{:S(2)}) %collective-permute-start.36) | collective-permute-done | bytes 2654240 | tf_op jit(solution)/shard_map/ppermute | solution.py:70
  223.2 3.4 add_convert_fusion.1
  227.7 23.9 %seg_attention_back.1 = (f32[512,768]{1,0:T(8,128)}, bf16[768,1280]{1,0:T(8,128)(2,1)}, bf16[768,1280]{1,0:T(8,128)(2,1)}) custom-call(s32[6]{0:T(128)} %stack.27.refs_0_, bf16[512,2304]{1,0:T(8,128)(2,1)} %get-tuple-element.224.refs_1_, bf16[512,768]{1,0:T(8,128)(2,1)} %get-tuple-element.225.refs_2_, f32[512,768]{1,0:T(8,128)} %get-tuple-element.226.refs_3_, ...), custom_call_target="tpu_custom_call" | custom-call | flops 3623878656 | bytes 15794176 | tf_op jit(solution)/shard_map/seg_attention_back/pallas_call | solution.py:490
  253.0 1.8 add_convert_fusion.8
  256.8 10.1 %collective-permute-done.39 = bf16[48,3456]{1,0:T(8,128)(2,1)S(1)} collective-permute-done((bf16[48,3456]{1,0:T(8,128)(2,1)S(1)}, bf16[48,3456]{1,0:T(8,128)(2,1)S(1)}, u32[]{:S(2)}, u32[]{:S(2)}) %collective-permute-start.39) | collective-permute-done | bytes 331808 | tf_op jit(solution)/shard_map/ppermute | solution.py:166
  269.9 4.6 %collective-permute-start.42 = (bf16[48,3456]{1,0:T(8,128)(2,1)S(1)}, bf16[48,3456]{1,0:T(8,128)(2,1)S(1)}, u32[]{:S(2)}, u32[]{:S(2)}) collective-permute-start(bf16[48,3456]{1,0:T(8,128)(2,1)S(1)} %fusion), channel_id=1, source_target_pairs={{0,8},{1,9},{2,10},{3,11},{4,12},{5,13},{6,14},{7,15},{8,16},{9,17... | collective-permute-start | bytes 995336 | tf_op jit(solution)/shard_map/ppermute | solution.py:166
  275.1 13.1 %collective-permute-done.42 = bf16[48,3456]{1,0:T(8,128)(2,1)S(1)} collective-permute-done((bf16[48,3456]{1,0:T(8,128)(2,1)S(1)}, bf16[48,3456]{1,0:T(8,128)(2,1)S(1)}, u32[]{:S(2)}, u32[]{:S(2)}) %collective-permute-start.42) | collective-permute-done | bytes 331808 | tf_op jit(solution)/shard_map/ppermute | solution.py:166
  288.2 4.4 %collective-permute-done.41 = bf16[384,1280]{1,0:T(8,128)(2,1)S(1)} collective-permute-done((bf16[384,1280]{1,0:T(8,128)(2,1)S(1)}, bf16[384,1280]{1,0:T(8,128)(2,1)S(1)}, u32[]{:S(2)}, u32[]{:S(2)}) %collective-permute-start.41) | collective-permute-done | bytes 983072 | tf_op jit(solution)/shard_map/ppermute | solution.py:70
  293.7 4.4 %collective-permute-start.45 = (bf16[48,3456]{1,0:T(8,128)(2,1)S(1)}, bf16[48,3456]{1,0:T(8,128)(2,1)S(1)}, u32[]{:S(2)}, u32[]{:S(2)}) collective-permute-start(bf16[48,3456]{1,0:T(8,128)(2,1)S(1)} %add_convert_fusion.6), channel_id=1, source_target_pairs={{0,8},{1,9},{2,10},{3,11},{4,12},{5,13},{6,14},{7,15},{8,16},{9,17... | collective-permute-start | bytes 995336 | tf_op jit(solution)/shard_map/ppermute | solution.py:166
  299.5 4.8 %collective-permute-done.45 = bf16[48,3456]{1,0:T(8,128)(2,1)S(1)} collective-permute-done((bf16[48,3456]{1,0:T(8,128)(2,1)S(1)}, bf16[48,3456]{1,0:T(8,128)(2,1)S(1)}, u32[]{:S(2)}, u32[]{:S(2)}) %collective-permute-start.45) | collective-permute-done | bytes 331808 | tf_op jit(solution)/shard_map/ppermute | solution.py:166
  304.3 5.8 %collective-permute-done.46 = bf16[48,3456]{1,0:T(8,128)(2,1)S(1)} collective-permute-done((bf16[48,3456]{1,0:T(8,128)(2,1)S(1)}, bf16[48,3456]{1,0:T(8,128)(2,1)S(1)}, u32[]{:S(2)}, u32[]{:S(2)}) %collective-permute-start.46) | collective-permute-done | bytes 331808 | tf_op jit(solution)/shard_map/ppermute | solution.py:166
  310.3 1.8 collective-permute-start.47
  312.1 2.8 collective-permute-start.49
  317.0 9.2 %cls_weight_grads.1 = (f32[24,2304]{1,0:T(8,128)}, f32[24,768]{1,0:T(8,128)}, f32[24,3072]{1,0:T(8,128)}, f32[96,768]{1,0:T(8,128)}, f32[2,24]{1,0:T(2,128)}, /*...) custom-call(s32[6]{0:T(128)} %stack.27.refs_0_, ...), custom_call_target="tpu_custom_call" | custom-call | flops 327680000 | bytes 7842436 | tf_op jit(solution)/shard_map/cls_weight_grads/pallas_call | solution.py:490
  (202 shorter events, 57.5 us)
Async XLA Ops:
  7.2 185.7 %all-gather.4.cloned.1.call-start = ((), (), s32[]{:S(2)}) async-start(), calls=%async_computation | async-start | bytes 14598144 | tf_op jit(solution)/shard_map/all_gather | solution.py:141
  30.2 20.9 %collective-permute-start.5 = (bf16[192,1280]{1,0:T(8,128)(2,1)S(1)}, bf16[192,1280]{1,0:T(8,128)(2,1)}, u32[]{:S(2)}, u32[]{:S(2)}) collective-permute-start(bf16[192,1280]{1,0:T(8,128)(2,1)S(1)} %pad_maximum_fusion.refs_4_.refs_10_), channel_id=1, source_target_pairs={{0,4},{1,3},{2,6},{3,1},{4,0},{5,7},{6,2},{7,5},{8,12},{9,11},{10,... | collective-permute-start | bytes 1474568 | tf_op jit(solution)/shard_map/ppermute | solution.py:70
  31.8 19.3 %collective-permute-start.6 = (bf16[192,1280]{1,0:T(8,128)(2,1)S(1)}, bf16[192,1280]{1,0:T(8,128)(2,1)}, u32[]{:S(2)}, u32[]{:S(2)}) collective-permute-start(bf16[192,1280]{1,0:T(8,128)(2,1)S(1)} %pad_maximum_fusion.refs_4_.refs_10_), channel_id=1, source_target_pairs={{0,2},{1,5},{2,0},{3,7},{4,6},{5,1},{6,4},{7,3},{8,10},{9,13},{10,... | collective-permute-start | bytes 1474568 | tf_op jit(solution)/shard_map/ppermute | solution.py:70
  34.8 16.3 %collective-permute-start.8 = (bf16[48,1920]{1,0:T(8,128)(2,1)S(1)}, bf16[48,1920]{1,0:T(8,128)(2,1)S(1)}, u32[]{:S(2)}, u32[]{:S(2)}) collective-permute-start(bf16[48,1920]{1,0:T(8,128)(2,1)S(1)} %maximum_select_fusion.1), channel_id=1, source_target_pairs={{0,16},{1,17},{2,18},{3,19},{4,20},{5,21},{6,22},{7,23},{8,24},{9,... | collective-permute-start | bytes 552968 | tf_op jit(solution)/shard_map/ppermute | solution.py:70
  35.8 15.3 %collective-permute-start.9 = (bf16[48,1920]{1,0:T(8,128)(2,1)S(1)}, bf16[48,1920]{1,0:T(8,128)(2,1)S(1)}, u32[]{:S(2)}, u32[]{:S(2)}) collective-permute-start(bf16[48,1920]{1,0:T(8,128)(2,1)S(1)} %maximum_select_fusion.1), channel_id=1, source_target_pairs={{0,8},{1,9},{2,10},{3,11},{4,12},{5,13},{6,14},{7,15},{8,16},{9,17... | collective-permute-start | bytes 552968 | tf_op jit(solution)/shard_map/ppermute | solution.py:70
  51.2 265.9 %all-gather.6.cloned.1.call-start = ((), (), s32[]{:S(2)}) async-start(), calls=%async_computation.1 | async-start | bytes 6488064 | tf_op jit(solution)/shard_map/all_gather | solution.py:1489
  51.3 25.2 %collective-permute-start.12 = (bf16[192,1920]{1,0:T(8,128)(2,1)S(1)}, bf16[192,1920]{1,0:T(8,128)(2,1)S(1)}, u32[]{:S(2)}, u32[]{:S(2)}) collective-permute-start(bf16[192,1920]{1,0:T(8,128)(2,1)S(1)} %constant_dynamic-update-slice_fusion.refs_7_.refs_14_), channel_id=1, source_target_pairs={{0,4},{1,3},{2,6},{3,1},{4,0},{5,7},{6,2},{7,5},{8,12},{9,11},{10,... | collective-permute-start | bytes 2211848 | tf_op jit(solution)/shard_map/ppermute | solution.py:70
  51.9 24.6 %collective-permute-start.13 = (bf16[192,1920]{1,0:T(8,128)(2,1)S(1)}, bf16[192,1920]{1,0:T(8,128)(2,1)}, u32[]{:S(2)}, u32[]{:S(2)}) collective-permute-start(bf16[192,1920]{1,0:T(8,128)(2,1)S(1)} %constant_dynamic-update-slice_fusion.refs_7_.refs_14_), channel_id=1, source_target_pairs={{0,2},{1,5},{2,0},{3,7},{4,6},{5,1},{6,4},{7,3},{8,10},{9,13},{10,... | collective-permute-start | bytes 2211848 | tf_op jit(solution)/shard_map/ppermute | solution.py:70
  52.4 24.0 %collective-permute-start.11 = (bf16[192,1280]{1,0:T(8,128)(2,1)}, bf16[192,1280]{1,0:T(8,128)(2,1)}, u32[]{:S(2)}, u32[]{:S(2)}) collective-permute-start(bf16[192,1280]{1,0:T(8,128)(2,1)} %collective-permute-done.5.refs_5_.refs_11_), channel_id=1, source_target_pairs={{0,2},{1,5},{2,0},{3,7},{4,6},{5,1},{6,4},{7,3},{8,10},{9,13},{10,... | collective-permute-start | bytes 1474568 | tf_op jit(solution)/shard_map/ppermute | solution.py:70
  54.0 22.0 %collective-permute-start.15 = (bf16[192,384]{1,0:T(8,128)(2,1)S(1)}, bf16[192,384]{1,0:T(8,128)(2,1)S(1)}, u32[]{:S(2)}, u32[]{:S(2)}) collective-permute-start(bf16[192,384]{1,0:T(8,128)(2,1)S(1)} %maximum_select_fusion.3), channel_id=1, source_target_pairs={{0,16},{1,17},{2,18},{3,19},{4,20},{5,21},{6,22},{7,23},{8,24},{9,... | collective-permute-start | bytes 442376 | tf_op jit(solution)/shard_map/ppermute | solution.py:70
  59.5 16.4 %collective-permute-start.16 = (bf16[192,384]{1,0:T(8,128)(2,1)S(1)}, bf16[192,384]{1,0:T(8,128)(2,1)S(1)}, u32[]{:S(2)}, u32[]{:S(2)}) collective-permute-start(bf16[192,384]{1,0:T(8,128)(2,1)S(1)} %maximum_select_fusion.3), channel_id=1, source_target_pairs={{0,8},{1,9},{2,10},{3,11},{4,12},{5,13},{6,14},{7,15},{8,16},{9,17... | collective-permute-start | bytes 442376 | tf_op jit(solution)/shard_map/ppermute | solution.py:70
  77.9 17.4 %collective-permute-start.21 = (bf16[192,1920]{1,0:T(8,128)(2,1)S(1)}, bf16[192,1920]{1,0:T(8,128)(2,1)S(1)}, u32[]{:S(2)}, u32[]{:S(2)}) collective-permute-start(bf16[192,1920]{1,0:T(8,128)(2,1)S(1)} %constant_dynamic-update-slice_fusion.refs_7_.refs_14_), channel_id=1, source_target_pairs={{0,1},{1,0},{2,3},{3,2},{4,5},{5,4},{6,7},{7,6},{8,9},{9,8},{10,11... | collective-permute-start | bytes 2211848 | tf_op jit(solution)/shard_map/ppermute | solution.py:70
  80.9 31.0 %collective-permute-start.22 = (bf16[192,1920]{1,0:T(8,128)(2,1)S(1)}, bf16[192,1920]{1,0:T(8,128)(2,1)}, u32[]{:S(2)}, u32[]{:S(2)}) collective-permute-start(bf16[192,1920]{1,0:T(8,128)(2,1)S(1)} %collective-permute-done.12.refs_8_.refs_15_), channel_id=1, source_target_pairs={{0,1},{1,0},{2,3},{3,2},{4,5},{5,4},{6,7},{7,6},{8,9},{9,8},{10,11... | collective-permute-start | bytes 2211848 | tf_op jit(solution)/shard_map/ppermute | solution.py:70
  81.4 30.5 %collective-permute-start.24 = (bf16[192,1920]{1,0:T(8,128)(2,1)S(1)}, bf16[192,1920]{1,0:T(8,128)(2,1)}, u32[]{:S(2)}, u32[]{:S(2)}) collective-permute-start(bf16[192,1920]{1,0:T(8,128)(2,1)S(1)} %collective-permute-done.12.refs_8_.refs_15_), channel_id=1, source_target_pairs={{0,2},{1,5},{2,0},{3,7},{4,6},{5,1},{6,4},{7,3},{8,10},{9,13},{10,... | collective-permute-start | bytes 2211848 | tf_op jit(solution)/shard_map/ppermute | solution.py:70
  82.5 29.5 %collective-permute-start.23 = (bf16[192,1920]{1,0:T(8,128)(2,1)}, bf16[192,1920]{1,0:T(8,128)(2,1)}, u32[]{:S(2)}, u32[]{:S(2)}) collective-permute-start(bf16[192,1920]{1,0:T(8,128)(2,1)} %collective-permute-done.13.refs_9_.refs_16_), channel_id=1, source_target_pairs={{0,1},{1,0},{2,3},{3,2},{4,5},{5,4},{6,7},{7,6},{8,9},{9,8},{10,11... | collective-permute-start | bytes 2211848 | tf_op jit(solution)/shard_map/ppermute | solution.py:70
  82.5 28.4 %collective-permute-start.25 = (bf16[768,384]{1,0:T(8,128)(2,1)S(1)}, bf16[768,384]{1,0:T(8,128)(2,1)}, u32[]{:S(2)}, u32[]{:S(2)}) collective-permute-start(bf16[768,384]{1,0:T(8,128)(2,1)S(1)} %constant_dynamic-update-slice_fusion.4.refs_15_.refs_22_), channel_id=1, source_target_pairs={{0,4},{1,3},{2,6},{3,1},{4,0},{5,7},{6,2},{7,5},{8,12},{9,11},{10,... | collective-permute-start | bytes 1769480 | tf_op jit(solution)/shard_map/ppermute | solution.py:70
  95.4 16.6 %collective-permute-start.26 = (bf16[768,384]{1,0:T(8,128)(2,1)S(1)}, bf16[768,384]{1,0:T(8,128)(2,1)}, u32[]{:S(2)}, u32[]{:S(2)}) collective-permute-start(bf16[768,384]{1,0:T(8,128)(2,1)S(1)} %constant_dynamic-update-slice_fusion.4.refs_15_.refs_22_), channel_id=1, source_target_pairs={{0,2},{1,5},{2,0},{3,7},{4,6},{5,1},{6,4},{7,3},{8,10},{9,13},{10,... | collective-permute-start | bytes 1769480 | tf_op jit(solution)/shard_map/ppermute | solution.py:70
  111.9 18.0 %collective-permute-start.27 = (bf16[192,1920]{1,0:T(8,128)(2,1)}, bf16[192,1920]{1,0:T(8,128)(2,1)S(1)}, u32[]{:S(2)}, u32[]{:S(2)}) collective-permute-start(bf16[192,1920]{1,0:T(8,128)(2,1)} %collective-permute-done.24.refs_10_.refs_17_), channel_id=1, source_target_pairs={{0,1},{1,0},{2,3},{3,2},{4,5},{5,4},{6,7},{7,6},{8,9},{9,8},{10,11... | collective-permute-start | bytes 2211848 | tf_op jit(solution)/shard_map/ppermute | solution.py:70
  117.6 12.4 %collective-permute-start.28 = (bf16[768,384]{1,0:T(8,128)(2,1)}, bf16[768,384]{1,0:T(8,128)(2,1)S(1)}, u32[]{:S(2)}, u32[]{:S(2)}) collective-permute-start(bf16[768,384]{1,0:T(8,128)(2,1)} %collective-permute-done.25.refs_16_.refs_23_), channel_id=1, source_target_pairs={{0,2},{1,5},{2,0},{3,7},{4,6},{5,1},{6,4},{7,3},{8,10},{9,13},{10,... | collective-permute-start | bytes 1769480 | tf_op jit(solution)/shard_map/ppermute | solution.py:70
  119.0 12.0 %collective-permute-start.29 = (bf16[768,384]{1,0:T(8,128)(2,1)S(1)}, bf16[768,384]{1,0:T(8,128)(2,1)S(1)}, u32[]{:S(2)}, u32[]{:S(2)}) collective-permute-start(bf16[768,384]{1,0:T(8,128)(2,1)S(1)} %constant_dynamic-update-slice_fusion.4.refs_15_.refs_22_), channel_id=1, source_target_pairs={{0,1},{1,0},{2,3},{3,2},{4,5},{5,4},{6,7},{7,6},{8,9},{9,8},{10,11... | collective-permute-start | bytes 1769480 | tf_op jit(solution)/shard_map/ppermute | solution.py:70
  119.0 12.0 %collective-permute-start.30 = (bf16[768,384]{1,0:T(8,128)(2,1)}, bf16[768,384]{1,0:T(8,128)(2,1)S(1)}, u32[]{:S(2)}, u32[]{:S(2)}) collective-permute-start(bf16[768,384]{1,0:T(8,128)(2,1)} %collective-permute-done.25.refs_16_.refs_23_), channel_id=1, source_target_pairs={{0,1},{1,0},{2,3},{3,2},{4,5},{5,4},{6,7},{7,6},{8,9},{9,8},{10,11... | collective-permute-start | bytes 1769480 | tf_op jit(solution)/shard_map/ppermute | solution.py:70
  190.4 32.7 %collective-permute-start.36 = (bf16[384,3456]{1,0:T(8,128)(2,1)}, bf16[384,3456]{1,0:T(8,128)(2,1)S(1)}, u32[]{:S(2)}, u32[]{:S(2)}) collective-permute-start(bf16[384,3456]{1,0:T(8,128)(2,1)} %add_convert_fusion), channel_id=1, source_target_pairs={{0,2},{1,5},{2,0},{3,7},{4,6},{5,1},{6,4},{7,3},{8,10},{9,13},{10,... | collective-permute-start | bytes 7962632 | tf_op jit(solution)/shard_map/ppermute | solution.py:70
  226.5 25.1 %collective-permute-start.37 = (bf16[192,3456]{1,0:T(8,128)(2,1)}, bf16[192,3456]{1,0:T(8,128)(2,1)}, u32[]{:S(2)}, u32[]{:S(2)}) collective-permute-start(bf16[192,3456]{1,0:T(8,128)(2,1)} %add_convert_fusion.1), channel_id=1, source_target_pairs={{0,4},{1,3},{2,6},{3,1},{4,0},{5,7},{6,2},{7,5},{8,12},{9,11},{10,... | collective-permute-start | bytes 3981320 | tf_op jit(solution)/shard_map/ppermute | solution.py:70
  251.7 15.2 %collective-permute-start.38 = (bf16[768,1280]{1,0:T(8,128)(2,1)}, bf16[768,1280]{1,0:T(8,128)(2,1)S(1)}, u32[]{:S(2)}, u32[]{:S(2)}) collective-permute-start(bf16[768,1280]{1,0:T(8,128)(2,1)} %get-tuple-element.235), channel_id=1, source_target_pairs={{0,1},{1,0},{2,3},{3,2},{4,5},{5,4},{6,7},{7,6},{8,9},{9,8},{10,11... | collective-permute-start | bytes 5898248 | tf_op jit(solution)/shard_map/ppermute | solution.py:70
  254.8 12.1 %collective-permute-start.39 = (bf16[48,3456]{1,0:T(8,128)(2,1)S(1)}, bf16[48,3456]{1,0:T(8,128)(2,1)S(1)}, u32[]{:S(2)}, u32[]{:S(2)}) collective-permute-start(bf16[48,3456]{1,0:T(8,128)(2,1)S(1)} %get-tuple-element.341), channel_id=1, source_target_pairs={{0,8},{1,9},{2,10},{3,11},{4,12},{5,13},{6,14},{7,15}} | collective-permute-start | bytes 995336 | tf_op jit(solution)/shard_map/ppermute | solution.py:166
  267.2 25.4 %collective-permute-start.41 = (bf16[384,1280]{1,0:T(8,128)(2,1)S(1)}, bf16[384,1280]{1,0:T(8,128)(2,1)S(1)}, u32[]{:S(2)}, u32[]{:S(2)}) collective-permute-start(bf16[384,1280]{1,0:T(8,128)(2,1)S(1)} %add_convert_fusion.2), channel_id=1, source_target_pairs={{0,2},{1,5},{2,0},{3,7},{4,6},{5,1},{6,4},{7,3},{8,10},{9,13},{10,... | collective-permute-start | bytes 2949128 | tf_op jit(solution)/shard_map/ppermute | solution.py:70
  269.9 18.3 %collective-permute-start.42 = (bf16[48,3456]{1,0:T(8,128)(2,1)S(1)}, bf16[48,3456]{1,0:T(8,128)(2,1)S(1)}, u32[]{:S(2)}, u32[]{:S(2)}) collective-permute-start(bf16[48,3456]{1,0:T(8,128)(2,1)S(1)} %fusion), channel_id=1, source_target_pairs={{0,8},{1,9},{2,10},{3,11},{4,12},{5,13},{6,14},{7,15},{8,16},{9,17... | collective-permute-start | bytes 995336 | tf_op jit(solution)/shard_map/ppermute | solution.py:166
  274.4 13.8 %collective-permute-start.43 = (bf16[48,3456]{1,0:T(8,128)(2,1)S(1)}, bf16[48,3456]{1,0:T(8,128)(2,1)S(1)}, u32[]{:S(2)}, u32[]{:S(2)}) collective-permute-start(bf16[48,3456]{1,0:T(8,128)(2,1)S(1)} %get-tuple-element.336), channel_id=1, source_target_pairs={{16,8},{17,9},{18,10},{19,11},{20,12},{21,13},{22,14},{23,15},{24,... | collective-permute-start | bytes 995336 | tf_op jit(solution)/shard_map/ppermute | solution.py:166
  292.8 17.3 %collective-permute-start.44 = (bf16[192,1280]{1,0:T(8,128)(2,1)S(1)}, bf16[192,1280]{1,0:T(8,128)(2,1)S(1)}, u32[]{:S(2)}, u32[]{:S(2)}) collective-permute-start(bf16[192,1280]{1,0:T(8,128)(2,1)S(1)} %add_convert_fusion.3), channel_id=1, source_target_pairs={{0,4},{1,3},{2,6},{3,1},{4,0},{5,7},{6,2},{7,5},{8,12},{9,11},{10,... | collective-permute-start | bytes 1474568 | tf_op jit(solution)/shard_map/ppermute | solution.py:70
  310.3 16.1 %collective-permute-start.47 = (bf16[48,1280]{1,0:T(8,128)(2,1)S(1)}, bf16[48,1280]{1,0:T(8,128)(2,1)}, u32[]{:S(2)}, u32[]{:S(2)}) collective-permute-start(bf16[48,1280]{1,0:T(8,128)(2,1)S(1)} %get-tuple-element.344), channel_id=1, source_target_pairs={{0,8},{1,9},{2,10},{3,11},{4,12},{5,13},{6,14},{7,15},{8,16},{9,17... | collective-permute-start | bytes 368648 | tf_op jit(solution)/shard_map/ppermute | solution.py:70
  312.1 14.3 %collective-permute-start.48 = (bf16[48,1280]{1,0:T(8,128)(2,1)S(1)}, bf16[48,1280]{1,0:T(8,128)(2,1)}, u32[]{:S(2)}, u32[]{:S(2)}) collective-permute-start(bf16[48,1280]{1,0:T(8,128)(2,1)S(1)} %get-tuple-element.343), channel_id=1, source_target_pairs={{0,16},{1,17},{2,18},{3,19},{4,20},{5,21},{6,22},{7,23},{8,24},{9,... | collective-permute-start | bytes 368648 | tf_op jit(solution)/shard_map/ppermute | solution.py:70
  312.1 14.3 %collective-permute-start.49 = (bf16[48,1280]{1,0:T(8,128)(2,1)S(1)}, bf16[48,1280]{1,0:T(8,128)(2,1)}, u32[]{:S(2)}, u32[]{:S(2)}) collective-permute-start(bf16[48,1280]{1,0:T(8,128)(2,1)S(1)} %get-tuple-element.342), channel_id=1, source_target_pairs={{0,24},{1,25},{2,26},{3,27},{4,28},{5,29},{6,30},{7,31},{8,0},{9,1... | collective-permute-start | bytes 368648 | tf_op jit(solution)/shard_map/ppermute | solution.py:70
  (46 other events, 539.4 us)
Sparse Core Ops, SparseCore 0:
  51.3 120.6 all-gather.3
  223.3 76.4 all-gather.5
